TPU v7x, 128 devices: a whole 4x4x4 slice. The times are simulated.
128 devices in a mesh: gz: 64 (over z, y_lo, x, core), col: 2 (over y_hi).
Axes of the slice: x: 4, y: 4 (y_hi: 2, y_lo: 2; y = y_hi * 2 + y_lo), z: 4, core: 2. Of those that a mesh axis runs over, the one named last changes fastest.
Arguments:
- volume: float32 [256, 24, 4096], P('gz', None, 'col'), may hold values from -6 to 6
- images: bfloat16 [256, 264, 2048], P('gz', None, 'col'), may hold values from -96 to 96
- owners: int32 [256], replicated, may hold values from 0 to 255, each once
- subsets: int32 [2, 6], replicated, may hold values from 0 to 255, as said below
- offsets: int32 [64], replicated, may hold values from 0 to 254, as said below
Outputs:
- reconstruction: float32 [256, 24, 4096], P('gz', None, 'col')
Inputs may be any that keep to these rules, and one draw needn't show every extreme that they name: `owners`: A permutation: every view number is stored at exactly one position. All view numbers in subsets are distinct; view 0 and view 256 - 1 always appear. offsets[g] - g * 4 lies in 0 .. 2; it is 0 for the first slab and 2 for the last.
All inputs are finite; a program needn't handle non-finite values.
Results may differ from a plain program's by a relative error of at most 0.0003.
Values may be sent and summed in bfloat16 or wider, within the bound.
No kernel may reach another device: no remote copies, remote signals or barrier semaphores. Data moves between devices by JAX's collectives and lax.ppermute only.
A program may use at most 128 MiB of HBM per device.

v0:
```python
import jax
import jax.numpy as jnp
from jax import lax
from jax.sharding import PartitionSpec as P

SUBSET = 6
SUBSETS = 2
PASSES = 4
MARGIN = 64


relaxation = 0.8
smooth_step = 0.05
smooth_floor = 0.1


def passed_along(value, axis, steps):
    count = lax.axis_size(axis)
    initial, last = (max(0, -steps), min(count, count - steps))
    return lax.ppermute(value, axis, [(source, source + steps) for source in range(initial, last)])


def from_root(block, axis, owner):
    block = jnp.where(lax.axis_index(axis) == owner, block, jnp.zeros_like(block))
    return lax.psum(block, axis)


def extended_2(cells, sides, width):
    for axis, dim in sides:
        count = lax.axis_size(axis)
        ends = count - 1
        head = lax.slice_in_dim(cells, 0, width, axis=dim)
        tail = lax.slice_in_dim(cells, cells.shape[dim] - width, cells.shape[dim], axis=dim)
        cells = jnp.concatenate(
            [
                lax.ppermute(tail, axis, [(i, (i + 1) % count) for i in range(ends)]),
                cells,
                lax.ppermute(head, axis, [((i + 1) % count, i) for i in range(ends)]),
            ],
            axis=dim,
        )
    return cells


def view_geometry(view, xcount, margin, nviews):
    angles = jnp.pi * view.astype(jnp.float32) / nviews
    across = (2.0 * jnp.arange(xcount, dtype=jnp.float32) - (xcount - 1)) / xcount
    shifted = margin * (0.375 * jnp.cos(angles) + 0.25 * jnp.sin(angles) * across) + margin
    integral = jnp.floor(shifted)
    return (integral.astype(jnp.int32), shifted - integral)


def kernel(fraction):
    half_steps = 0.5 * jnp.arange(128, dtype=jnp.float32)
    columns = jnp.arange(128, dtype=jnp.float32)
    distance = half_steps[None, :, None] + fraction[:, None, None] - columns[None, None, :]
    return jnp.maximum(0.0, 1.0 - jnp.abs(distance))


def project(slices, column_step, weights, margin):
    slab_depth, xcount, length = slices.shape
    block_count = length // 128
    blocks = slices.reshape(slab_depth, xcount, block_count, 128)
    pieces = jnp.einsum("kxby,xyj->xkbj", blocks, weights, precision=lax.Precision.HIGHEST)
    front_half = pieces[..., :64].reshape(xcount, slab_depth, block_count * 64)
    second = pieces[..., 64:].reshape(xcount, slab_depth, block_count * 64)
    joined = jnp.pad(front_half, ((0, 0), (0, 0), (0, 64))) + jnp.pad(
        second, ((0, 0), (0, 0), (64, 0))
    )
    padded = jnp.pad(joined, ((0, 0), (0, 0), (2 * margin, 2 * margin)))
    extent = block_count * 64 + 2 * margin

    def moved_row(single, offset_cols):
        return lax.dynamic_slice_in_dim(single, 2 * margin - offset_cols, extent, axis=1)

    return jnp.sum(jax.vmap(moved_row)(padded, column_step), axis=0)


def spread(rows_ext, column_step, weights, length):
    slab_depth = rows_ext.shape[0]
    block_count = length // 128
    padded = jnp.pad(rows_ext, ((0, 0), (0, block_count * 64 + 64)))

    def one_row(offset_cols, weight):
        window = lax.dynamic_slice_in_dim(padded, offset_cols, block_count * 64 + 64, axis=1)
        lower = window[:, : block_count * 64].reshape(slab_depth, block_count, 64)
        upper = window[:, 64:].reshape(slab_depth, block_count, 64)
        stacked = jnp.concatenate([lower, upper], axis=2)
        result = jnp.einsum("kbj,yj->kby", stacked, weight, precision=lax.Precision.HIGHEST)
        return result.reshape(slab_depth, length)

    return jax.vmap(one_row, out_axes=1)(column_step, weights)


def forward_diff(values, direction):
    count = values.shape[direction]
    following = jnp.concatenate(
        [
            lax.slice_in_dim(values, 1, count, axis=direction),
            jnp.zeros_like(lax.slice_in_dim(values, 0, 1, axis=direction)),
        ],
        axis=direction,
    )
    return following - values


def behind(values, direction):
    count = values.shape[direction]
    return jnp.concatenate(
        [
            jnp.zeros_like(lax.slice_in_dim(values, 0, 1, axis=direction)),
            lax.slice_in_dim(values, 0, count - 1, axis=direction),
        ],
        axis=direction,
    )


def smooth_pass(padded, inside):
    differences = [forward_diff(padded, direction) for direction in range(3)]
    magnitude = jnp.sqrt(
        differences[0] * differences[0]
        + differences[1] * differences[1]
        + differences[2] * differences[2]
        + smooth_floor
    )
    fluxes = [item_diff / magnitude * inside for item_diff in differences]
    gradient = (
        behind(fluxes[0], 0)
        - fluxes[0]
        + (behind(fluxes[1], 1) - fluxes[1])
        + (behind(fluxes[2], 2) - fluxes[2])
    )
    return (padded - smooth_step * gradient) * inside


def inside_mask(slab_index, column, shape_info, border):
    slab_depth, xcount, length, slab_count, col_count = shape_info
    depth_cells = (
        slab_index * slab_depth - border + jnp.arange(slab_depth + 2 * border, dtype=jnp.int32)
    )
    depth_ok = (depth_cells >= 0) & (depth_cells < slab_depth * slab_count)
    row_cells = jnp.arange(xcount + 2 * border, dtype=jnp.int32)
    row_ok = (row_cells >= border) & (row_cells < border + xcount)
    line_cells = column * length - border + jnp.arange(length + 2 * border, dtype=jnp.int32)
    line_ok = (line_cells >= 0) & (line_cells < length * col_count)
    return (
        depth_ok[:, None, None].astype(jnp.float32)
        * row_ok[None, :, None].astype(jnp.float32)
        * line_ok[None, None, :].astype(jnp.float32)
    )


def spill(portion, offset_by):
    return passed_along(portion, "col", offset_by)


def body(volume, images, owners, subsets, offsets):
    slab_count = lax.axis_size("gz")
    col_count = lax.axis_size("col")
    slab_index = lax.axis_index("gz")
    column = lax.axis_index("col")
    slab_depth, xcount, length = volume.shape
    detector = length // 2
    stored = images.shape[0]
    nviews = owners.shape[0]
    window = 2 * slab_depth
    shape_info = (slab_depth, xcount, length, slab_count, col_count)
    own_start = lax.dynamic_index_in_dim(offsets, slab_index, 0, keepdims=False)
    prev_start = lax.dynamic_index_in_dim(
        offsets, jnp.maximum(slab_index - 1, 0), 0, keepdims=False
    )
    next_start = lax.dynamic_index_in_dim(
        offsets, jnp.minimum(slab_index + 1, slab_count - 1), 0, keepdims=False
    )
    has_prev = (slab_index > 0).astype(jnp.float32)
    has_next = (slab_index < slab_count - 1).astype(jnp.float32)
    local_rows = jnp.arange(window, dtype=jnp.int32)
    centers = 1.5 * jnp.arange(slab_depth, dtype=jnp.float32) + 0.25
    row_weight = jnp.maximum(
        0.0, 1.0 - jnp.abs(centers[:, None] - local_rows[None, :].astype(jnp.float32))
    )
    row_total = jnp.sum(row_weight, axis=0)
    from_prev = (local_rows[None, :] == local_rows[:, None] + own_start - prev_start).astype(
        jnp.float32
    ) * has_prev
    from_next = (local_rows[None, :] == local_rows[:, None] + own_start - next_start).astype(
        jnp.float32
    ) * has_next
    gathered_total = (
        row_total
        + jnp.dot(
            from_prev,
            row_total,
            precision=lax.Precision.HIGHEST,
            preferred_element_type=jnp.float32,
        )
        + jnp.dot(
            from_next,
            row_total,
            precision=lax.Precision.HIGHEST,
            preferred_element_type=jnp.float32,
        )
    )
    unit_slice = jnp.ones((1, xcount, length), jnp.float32)
    current = volume
    for subset_index in range(SUBSETS):
        chosen = subsets[subset_index]
        positions = jnp.sum(
            jnp.where(
                owners[None, :] == chosen[:, None], jnp.arange(nviews, dtype=jnp.int32)[None, :], 0
            ),
            axis=1,
        )
        gathered_rows = []
        for view_slot in range(SUBSET):
            owner = positions[view_slot] // stored
            slot_index = positions[view_slot] % stored
            own_image = lax.dynamic_index_in_dim(images, slot_index, 0, keepdims=False)
            full_image = from_root(own_image, "gz", owner)
            gathered_rows.append(lax.dynamic_slice_in_dim(full_image, own_start, window, 0))
        measured = jnp.stack(gathered_rows)
        stacked = jnp.concatenate([current, unit_slice], axis=0)

        def forward_view(view):
            column_step, fraction = view_geometry(view, xcount, MARGIN, nviews)
            return project(stacked, column_step, kernel(fraction), MARGIN)

        extended = lax.map(forward_view, chosen)
        middle = extended[:, :, MARGIN : MARGIN + detector]
        left_part = spill(extended[:, :, MARGIN + detector :], 1)
        right_part = spill(extended[:, :, :MARGIN], -1)
        middle = (
            middle
            + jnp.pad(left_part, ((0, 0), (0, 0), (0, detector - MARGIN)))
            + jnp.pad(right_part, ((0, 0), (0, 0), (detector - MARGIN, 0)))
        )
        predicted = jnp.einsum(
            "kr,vku->vru", row_weight, middle[:, :slab_depth], precision=lax.Precision.HIGHEST
        )
        beside_all = extended_2(predicted[None].astype(jnp.bfloat16), (("gz", 0),), 1).astype(
            jnp.float32
        )
        combined = (
            predicted
            + jnp.einsum("rs,vsu->vru", from_prev, beside_all[0], precision=lax.Precision.HIGHEST)
            + jnp.einsum("rs,vsu->vru", from_next, beside_all[2], precision=lax.Precision.HIGHEST)
        )
        raysum = gathered_total[None, :, None] * middle[:, slab_depth][:, None, :]
        residual = (measured.astype(jnp.float32) - combined) / jnp.maximum(raysum, 1.0)
        widened = extended_2(residual, (("col", 2),), MARGIN)
        row_mixed = jnp.einsum("kr,vru->vku", row_weight, widened, precision=lax.Precision.HIGHEST)

        def back_view(sum_so_far, element):
            view, rows_ext = element
            column_step, fraction = view_geometry(view, xcount, MARGIN, nviews)
            return (sum_so_far + spread(rows_ext, column_step, kernel(fraction), length), None)

        update, _ = lax.scan(back_view, jnp.zeros_like(current), (chosen, row_mixed))
        current = current + relaxation / SUBSET * update
        inside = inside_mask(slab_index, column, shape_info, 1)
        for pass_index in range(PASSES):
            padded = extended_2(current, (("gz", 0), ("col", 2)), 1)
            padded = jnp.pad(padded, ((0, 0), (1, 1), (0, 0)))
            current = smooth_pass(padded, inside)[1:-1, 1:-1, 1:-1]
    return current


def solution(mesh):
    in_specs = (P("gz", None, "col"), P("gz", None, "col"), P(), P(), P())
    out_specs = P("gz", None, "col")
    return jax.shard_map(body, mesh=mesh, in_specs=in_specs, out_specs=out_specs, check_vma=False)
```

profile of v0, /device:TPU:15, one launch (start us, length us, event | category | flops | bytes accessed | tf_op | source)
XLA Modules:
  0.0 1744.7 jit_solution(1282124142669183649)
XLA Ops:
  44.9 418.9 %while.61 = (s32[]{:T(128)}, f32[6,5,1152]{2,1,0:T(8,128)S(1)}, s32[6]{0:T(128)S(1)}, f32[5,24,2048]{2,1,0:T(8,128)S(1)}, s32[]{:T(128)}, /*index=5*/s32[]{:T(12...) while((s32[]{:T(128)}, f32[6,5,1152]{2,1,0:T(8,128)S(1)}, s32[6]{0:T(128)S(1)}, ...), condition=%wide.region_9.10_spmd, body=%wide.region_7.9_spmd.sunk | while | flops 379327008 | bytes 21149980 | solution.py:228
  50.4 63.0 %while.68 = (s32[]{:T(128)}, f32[24,5,1344]{2,0,1:T(8,128)S(1)}, s32[24,3]{0,1:T(4,128)S(1)}, f32[24,5,1152]{2,1,0:T(8,128)}, s32[]{:T(128)}) while((s32[]{:T(128)}, f32[24,5,1344]{2,0,1:T(8,128)S(1)}, s32[24,3]{0,1:T(4,128)S(1)}, f32[24,5,1152]{2,1,0:T(8,128)}, s32[]{:T(128)}) %tuple.259), condition=%wide.while_cond, body=%wide.while_body.sunk | while | flops 2 | bytes 106109 | solution.py:74
  120.2 63.0 %while.68 = (s32[]{:T(128)}, f32[24,5,1344]{2,0,1:T(8,128)S(1)}, s32[24,3]{0,1:T(4,128)S(1)}, f32[24,5,1152]{2,1,0:T(8,128)}, s32[]{:T(128)}) while((s32[]{:T(128)}, f32[24,5,1344]{2,0,1:T(8,128)S(1)}, s32[24,3]{0,1:T(4,128)S(1)}, f32[24,5,1152]{2,1,0:T(8,128)}, s32[]{:T(128)}) %tuple.259), condition=%wide.while_cond, body=%wide.while_body.sunk | while | flops 2 | bytes 106109 | solution.py:74
  190.0 63.0 %while.68 = (s32[]{:T(128)}, f32[24,5,1344]{2,0,1:T(8,128)S(1)}, s32[24,3]{0,1:T(4,128)S(1)}, f32[24,5,1152]{2,1,0:T(8,128)}, s32[]{:T(128)}) while((s32[]{:T(128)}, f32[24,5,1344]{2,0,1:T(8,128)S(1)}, s32[24,3]{0,1:T(4,128)S(1)}, f32[24,5,1152]{2,1,0:T(8,128)}, s32[]{:T(128)}) %tuple.259), condition=%wide.while_cond, body=%wide.while_body.sunk | while | flops 2 | bytes 106109 | solution.py:74
  259.8 63.0 %while.68 = (s32[]{:T(128)}, f32[24,5,1344]{2,0,1:T(8,128)S(1)}, s32[24,3]{0,1:T(4,128)S(1)}, f32[24,5,1152]{2,1,0:T(8,128)}, s32[]{:T(128)}) while((s32[]{:T(128)}, f32[24,5,1344]{2,0,1:T(8,128)S(1)}, s32[24,3]{0,1:T(4,128)S(1)}, f32[24,5,1152]{2,1,0:T(8,128)}, s32[]{:T(128)}) %tuple.259), condition=%wide.while_cond, body=%wide.while_body.sunk | while | flops 2 | bytes 106109 | solution.py:74
  329.7 63.0 %while.68 = (s32[]{:T(128)}, f32[24,5,1344]{2,0,1:T(8,128)S(1)}, s32[24,3]{0,1:T(4,128)S(1)}, f32[24,5,1152]{2,1,0:T(8,128)}, s32[]{:T(128)}) while((s32[]{:T(128)}, f32[24,5,1344]{2,0,1:T(8,128)S(1)}, s32[24,3]{0,1:T(4,128)S(1)}, f32[24,5,1152]{2,1,0:T(8,128)}, s32[]{:T(128)}) %tuple.259), condition=%wide.while_cond, body=%wide.while_body.sunk | while | flops 2 | bytes 106109 | solution.py:74
  399.5 63.0 %while.68 = (s32[]{:T(128)}, f32[24,5,1344]{2,0,1:T(8,128)S(1)}, s32[24,3]{0,1:T(4,128)S(1)}, f32[24,5,1152]{2,1,0:T(8,128)}, s32[]{:T(128)}) while((s32[]{:T(128)}, f32[24,5,1344]{2,0,1:T(8,128)S(1)}, s32[24,3]{0,1:T(4,128)S(1)}, f32[24,5,1152]{2,1,0:T(8,128)}, s32[]{:T(128)}) %tuple.259), condition=%wide.while_cond, body=%wide.while_body.sunk | while | flops 2 | bytes 106109 | solution.py:74
  463.9 3.9 collective-permute-start
  474.6 3.9 collective-permute-start.3
  478.6 4.6 collective-permute-start.2
  484.1 97.1 %all-reduce.77.cloned.1.call-done = (bf16[264,1024]{1,0:T(8,128)(2,1)}, bf16[264,1024]{1,0:T(8,128)(2,1)}, bf16[264,1024]{1,0:T(8,128)(2,1)}, bf16[264,1024]{1,0...) async-done(((bf16[264,1024]{1,0:T(8,128)(2,1)}, ...) | async-done | bytes 6488080 | tf_op jit(solution)/shard_map/psum | solution.py:25
  587.5 5.7 collective-permute-start.4
  594.5 227.8 %while.65 = (s32[]{:T(128)}, f32[4,24,2048]{2,0,1:T(4,128)S(1)}, f32[6,4,1152]{2,1,0:T(4,128)S(1)}, s32[6]{0:T(128)S(1)}, s32[]{:T(128)}, /*index=5*/s32[]{:T(12...) while((s32[]{:T(128)}, f32[4,24,2048]{2,0,1:T(4,128)S(1)}, ...), condition=%wide.region_12.13_spmd.clone, body=%wide.region_11.12_spmd.clone.sunk | while | flops 304156224 | bytes 8805308 | solution.py:258
  596.0 31.2 %while.70 = (s32[]{:T(128)}, f32[4,2240]{1,0:T(4,128)S(1)}, s32[24,2]{0,1:T(2,128)S(1)}, f32[24,4,1088]{2,1,0:T(4,128)S(1)}, s32[]{:T(128)}) while((s32[]{:T(128)}, f32[4,2240]{1,0:T(4,128)S(1)}, s32[24,2]{0,1:T(2,128)S(1)}, f32[24,4,1088]{2,1,0:T(4,128)S(1)}, s32[]{:T(128)}) %tuple.253), condition=%wide.while_cond.1, body=%wide.while_body.1.sunk | while | flops 2 | bytes 36969 | solution.py:85
  628.2 3.3 fusion.219
  634.0 31.2 %while.70 = (s32[]{:T(128)}, f32[4,2240]{1,0:T(4,128)S(1)}, s32[24,2]{0,1:T(2,128)S(1)}, f32[24,4,1088]{2,1,0:T(4,128)S(1)}, s32[]{:T(128)}) while((s32[]{:T(128)}, f32[4,2240]{1,0:T(4,128)S(1)}, s32[24,2]{0,1:T(2,128)S(1)}, f32[24,4,1088]{2,1,0:T(4,128)S(1)}, s32[]{:T(128)}) %tuple.253), condition=%wide.while_cond.1, body=%wide.while_body.1.sunk | while | flops 2 | bytes 36969 | solution.py:85
  666.2 3.3 fusion.219
  672.0 31.2 %while.70 = (s32[]{:T(128)}, f32[4,2240]{1,0:T(4,128)S(1)}, s32[24,2]{0,1:T(2,128)S(1)}, f32[24,4,1088]{2,1,0:T(4,128)S(1)}, s32[]{:T(128)}) while((s32[]{:T(128)}, f32[4,2240]{1,0:T(4,128)S(1)}, s32[24,2]{0,1:T(2,128)S(1)}, f32[24,4,1088]{2,1,0:T(4,128)S(1)}, s32[]{:T(128)}) %tuple.253), condition=%wide.while_cond.1, body=%wide.while_body.1.sunk | while | flops 2 | bytes 36969 | solution.py:85
  704.2 3.3 fusion.219
  709.9 31.2 %while.70 = (s32[]{:T(128)}, f32[4,2240]{1,0:T(4,128)S(1)}, s32[24,2]{0,1:T(2,128)S(1)}, f32[24,4,1088]{2,1,0:T(4,128)S(1)}, s32[]{:T(128)}) while((s32[]{:T(128)}, f32[4,2240]{1,0:T(4,128)S(1)}, s32[24,2]{0,1:T(2,128)S(1)}, f32[24,4,1088]{2,1,0:T(4,128)S(1)}, s32[]{:T(128)}) %tuple.253), condition=%wide.while_cond.1, body=%wide.while_body.1.sunk | while | flops 2 | bytes 36969 | solution.py:85
  742.1 3.3 fusion.219
  747.9 31.2 %while.70 = (s32[]{:T(128)}, f32[4,2240]{1,0:T(4,128)S(1)}, s32[24,2]{0,1:T(2,128)S(1)}, f32[24,4,1088]{2,1,0:T(4,128)S(1)}, s32[]{:T(128)}) while((s32[]{:T(128)}, f32[4,2240]{1,0:T(4,128)S(1)}, s32[24,2]{0,1:T(2,128)S(1)}, f32[24,4,1088]{2,1,0:T(4,128)S(1)}, s32[]{:T(128)}) %tuple.253), condition=%wide.while_cond.1, body=%wide.while_body.1.sunk | while | flops 2 | bytes 36969 | solution.py:85
  780.1 3.3 fusion.219
  785.9 31.2 %while.70 = (s32[]{:T(128)}, f32[4,2240]{1,0:T(4,128)S(1)}, s32[24,2]{0,1:T(2,128)S(1)}, f32[24,4,1088]{2,1,0:T(4,128)S(1)}, s32[]{:T(128)}) while((s32[]{:T(128)}, f32[4,2240]{1,0:T(4,128)S(1)}, s32[24,2]{0,1:T(2,128)S(1)}, f32[24,4,1088]{2,1,0:T(4,128)S(1)}, s32[]{:T(128)}) %tuple.253), condition=%wide.while_cond.1, body=%wide.while_body.1.sunk | while | flops 2 | bytes 36969 | solution.py:85
  818.1 3.3 fusion.219
  824.0 4.0 collective-permute-start.6
  830.9 7.1 collective-permute-done.7
  839.4 5.5 collective-permute-start.8
  851.0 3.9 collective-permute-start.10
  857.6 7.4 collective-permute-done.11
  866.4 5.9 collective-permute-start.12
  883.9 7.4 collective-permute-done.15
  892.8 5.5 collective-permute-start.16
  911.1 6.2 collective-permute-done.19
  918.8 5.7 collective-permute-start.20
  932.9 431.7 %while.63 = (s32[]{:T(128)}, f32[6,5,1152]{2,1,0:T(8,128)S(1)}, s32[6]{0:T(128)S(1)}, f32[5,24,2048]{2,1,0:T(8,128)S(1)}, s32[]{:T(128)}, /*index=5*/s32[]{:T(12...) while((s32[]{:T(128)}, f32[6,5,1152]{2,1,0:T(8,128)S(1)}, s32[6]{0:T(128)S(1)}, ...), condition=%wide.region_22.23_spmd, body=%wide.region_20.22_spmd.sunk | while | flops 379327008 | bytes 21149980 | solution.py:228
  938.5 65.0 %while.69 = (s32[]{:T(128)}, f32[24,5,1344]{2,0,1:T(8,128)S(1)}, s32[24,3]{0,1:T(4,128)S(1)}, f32[24,5,1152]{2,1,0:T(8,128)}, s32[]{:T(128)}) while((s32[]{:T(128)}, f32[24,5,1344]{2,0,1:T(8,128)S(1)}, s32[24,3]{0,1:T(4,128)S(1)}, f32[24,5,1152]{2,1,0:T(8,128)}, s32[]{:T(128)}) %tuple.256), condition=%wide.while_cond.2, body=%wide.while_body.2.sunk | while | flops 2 | bytes 106109 | solution.py:74
  1010.5 65.0 %while.69 = (s32[]{:T(128)}, f32[24,5,1344]{2,0,1:T(8,128)S(1)}, s32[24,3]{0,1:T(4,128)S(1)}, f32[24,5,1152]{2,1,0:T(8,128)}, s32[]{:T(128)}) while((s32[]{:T(128)}, f32[24,5,1344]{2,0,1:T(8,128)S(1)}, s32[24,3]{0,1:T(4,128)S(1)}, f32[24,5,1152]{2,1,0:T(8,128)}, s32[]{:T(128)}) %tuple.256), condition=%wide.while_cond.2, body=%wide.while_body.2.sunk | while | flops 2 | bytes 106109 | solution.py:74
  1082.4 65.0 %while.69 = (s32[]{:T(128)}, f32[24,5,1344]{2,0,1:T(8,128)S(1)}, s32[24,3]{0,1:T(4,128)S(1)}, f32[24,5,1152]{2,1,0:T(8,128)}, s32[]{:T(128)}) while((s32[]{:T(128)}, f32[24,5,1344]{2,0,1:T(8,128)S(1)}, s32[24,3]{0,1:T(4,128)S(1)}, f32[24,5,1152]{2,1,0:T(8,128)}, s32[]{:T(128)}) %tuple.256), condition=%wide.while_cond.2, body=%wide.while_body.2.sunk | while | flops 2 | bytes 106109 | solution.py:74
  1154.4 65.0 %while.69 = (s32[]{:T(128)}, f32[24,5,1344]{2,0,1:T(8,128)S(1)}, s32[24,3]{0,1:T(4,128)S(1)}, f32[24,5,1152]{2,1,0:T(8,128)}, s32[]{:T(128)}) while((s32[]{:T(128)}, f32[24,5,1344]{2,0,1:T(8,128)S(1)}, s32[24,3]{0,1:T(4,128)S(1)}, f32[24,5,1152]{2,1,0:T(8,128)}, s32[]{:T(128)}) %tuple.256), condition=%wide.while_cond.2, body=%wide.while_body.2.sunk | while | flops 2 | bytes 106109 | solution.py:74
  1226.4 65.0 %while.69 = (s32[]{:T(128)}, f32[24,5,1344]{2,0,1:T(8,128)S(1)}, s32[24,3]{0,1:T(4,128)S(1)}, f32[24,5,1152]{2,1,0:T(8,128)}, s32[]{:T(128)}) while((s32[]{:T(128)}, f32[24,5,1344]{2,0,1:T(8,128)S(1)}, s32[24,3]{0,1:T(4,128)S(1)}, f32[24,5,1152]{2,1,0:T(8,128)}, s32[]{:T(128)}) %tuple.256), condition=%wide.while_cond.2, body=%wide.while_body.2.sunk | while | flops 2 | bytes 106109 | solution.py:74
  1298.3 65.0 %while.69 = (s32[]{:T(128)}, f32[24,5,1344]{2,0,1:T(8,128)S(1)}, s32[24,3]{0,1:T(4,128)S(1)}, f32[24,5,1152]{2,1,0:T(8,128)}, s32[]{:T(128)}) while((s32[]{:T(128)}, f32[24,5,1344]{2,0,1:T(8,128)S(1)}, s32[24,3]{0,1:T(4,128)S(1)}, f32[24,5,1152]{2,1,0:T(8,128)}, s32[]{:T(128)}) %tuple.256), condition=%wide.while_cond.2, body=%wide.while_body.2.sunk | while | flops 2 | bytes 106109 | solution.py:74
  1364.7 5.2 collective-permute-start.22
  1372.6 3.4 collective-permute-done.23
  1379.9 6.7 collective-permute-start.24
  1390.8 5.7 collective-permute-start.26
  1399.0 223.5 %while.67 = (s32[]{:T(128)}, f32[4,24,2048]{2,0,1:T(4,128)S(1)}, f32[6,4,1152]{2,1,0:T(4,128)}, s32[6]{0:T(128)S(1)}, s32[]{:T(128)}, /*index=5*/s32[]{:T(128)},...) while((s32[]{:T(128)}, f32[4,24,2048]{2,0,1:T(4,128)S(1)}, ...), condition=%wide.region_24.25_spmd.clone, body=%wide.region_23.24_spmd.clone.sunk | while | flops 304156224 | bytes 8805308 | solution.py:258
  1401.2 29.9 %while.71 = (s32[]{:T(128)}, f32[4,2240]{1,0:T(4,128)S(1)}, s32[24,2]{0,1:T(2,128)S(1)}, f32[24,4,1088]{2,1,0:T(4,128)S(1)}, s32[]{:T(128)}) while((s32[]{:T(128)}, f32[4,2240]{1,0:T(4,128)S(1)}, s32[24,2]{0,1:T(2,128)S(1)}, f32[24,4,1088]{2,1,0:T(4,128)S(1)}, s32[]{:T(128)}) %tuple.250), condition=%wide.while_cond.3, body=%wide.while_body.3.sunk | while | flops 2 | bytes 36969 | solution.py:85
  1438.4 29.9 %while.71 = (s32[]{:T(128)}, f32[4,2240]{1,0:T(4,128)S(1)}, s32[24,2]{0,1:T(2,128)S(1)}, f32[24,4,1088]{2,1,0:T(4,128)S(1)}, s32[]{:T(128)}) while((s32[]{:T(128)}, f32[4,2240]{1,0:T(4,128)S(1)}, s32[24,2]{0,1:T(2,128)S(1)}, f32[24,4,1088]{2,1,0:T(4,128)S(1)}, s32[]{:T(128)}) %tuple.250), condition=%wide.while_cond.3, body=%wide.while_body.3.sunk | while | flops 2 | bytes 36969 | solution.py:85
  1469.2 3.3 fusion.223
  1475.7 29.9 %while.71 = (s32[]{:T(128)}, f32[4,2240]{1,0:T(4,128)S(1)}, s32[24,2]{0,1:T(2,128)S(1)}, f32[24,4,1088]{2,1,0:T(4,128)S(1)}, s32[]{:T(128)}) while((s32[]{:T(128)}, f32[4,2240]{1,0:T(4,128)S(1)}, s32[24,2]{0,1:T(2,128)S(1)}, f32[24,4,1088]{2,1,0:T(4,128)S(1)}, s32[]{:T(128)}) %tuple.250), condition=%wide.while_cond.3, body=%wide.while_body.3.sunk | while | flops 2 | bytes 36969 | solution.py:85
  1512.9 29.9 %while.71 = (s32[]{:T(128)}, f32[4,2240]{1,0:T(4,128)S(1)}, s32[24,2]{0,1:T(2,128)S(1)}, f32[24,4,1088]{2,1,0:T(4,128)S(1)}, s32[]{:T(128)}) while((s32[]{:T(128)}, f32[4,2240]{1,0:T(4,128)S(1)}, s32[24,2]{0,1:T(2,128)S(1)}, f32[24,4,1088]{2,1,0:T(4,128)S(1)}, s32[]{:T(128)}) %tuple.250), condition=%wide.while_cond.3, body=%wide.while_body.3.sunk | while | flops 2 | bytes 36969 | solution.py:85
  1550.2 29.9 %while.71 = (s32[]{:T(128)}, f32[4,2240]{1,0:T(4,128)S(1)}, s32[24,2]{0,1:T(2,128)S(1)}, f32[24,4,1088]{2,1,0:T(4,128)S(1)}, s32[]{:T(128)}) while((s32[]{:T(128)}, f32[4,2240]{1,0:T(4,128)S(1)}, s32[24,2]{0,1:T(2,128)S(1)}, f32[24,4,1088]{2,1,0:T(4,128)S(1)}, s32[]{:T(128)}) %tuple.250), condition=%wide.while_cond.3, body=%wide.while_body.3.sunk | while | flops 2 | bytes 36969 | solution.py:85
  1587.4 29.9 %while.71 = (s32[]{:T(128)}, f32[4,2240]{1,0:T(4,128)S(1)}, s32[24,2]{0,1:T(2,128)S(1)}, f32[24,4,1088]{2,1,0:T(4,128)S(1)}, s32[]{:T(128)}) while((s32[]{:T(128)}, f32[4,2240]{1,0:T(4,128)S(1)}, s32[24,2]{0,1:T(2,128)S(1)}, f32[24,4,1088]{2,1,0:T(4,128)S(1)}, s32[]{:T(128)}) %tuple.250), condition=%wide.while_cond.3, body=%wide.while_body.3.sunk | while | flops 2 | bytes 36969 | solution.py:85
  1624.2 7.9 collective-permute-start.28
  1634.6 7.4 collective-permute-done.29
  1643.5 5.5 collective-permute-start.30
  1660.6 7.4 collective-permute-done.33
  1669.5 6.6 collective-permute-start.34
  1687.8 7.4 collective-permute-done.37
  1696.6 6.0 collective-permute-start.38
  1714.6 7.4 collective-permute-done.41
  1723.4 5.8 collective-permute-start.42
  1733.7 3.7 fusion.74
  (2681 shorter events, 1390.8 us)
Async XLA Ops:
  6.5 574.7 %all-reduce.77.cloned.1.call-start = ((), (), s32[]{:S(2)}) async-start(), calls=%async_computation | async-start | bytes 12976128 | tf_op jit(solution)/shard_map/psum | solution.py:25
  38.4 2.9 copy-start.4
  44.8 424.3 %copy-start.7 = (s32[64]{0:T(128)S(1)}, s32[64]{0:T(128)}, u32[]{:S(2)}) copy-start(s32[64]{0:T(128)} %param.17) | copy-start | bytes 772
  50.3 64.4 %copy-start.3 = (f32[5,24,2048]{2,1,0:T(8,128)S(1)}, f32[5,24,2048]{2,1,0:T(8,128)}, u32[]{:S(2)}) copy-start(f32[5,24,2048]{2,1,0:T(8,128)} %copy-done.2) | copy-start | bytes 2949124 | tf_op jit(solution)/shard_map/while
  120.1 64.4 %copy-start.3 = (f32[5,24,2048]{2,1,0:T(8,128)S(1)}, f32[5,24,2048]{2,1,0:T(8,128)}, u32[]{:S(2)}) copy-start(f32[5,24,2048]{2,1,0:T(8,128)} %copy-done.2) | copy-start | bytes 2949124 | tf_op jit(solution)/shard_map/while
  190.0 64.4 %copy-start.3 = (f32[5,24,2048]{2,1,0:T(8,128)S(1)}, f32[5,24,2048]{2,1,0:T(8,128)}, u32[]{:S(2)}) copy-start(f32[5,24,2048]{2,1,0:T(8,128)} %copy-done.2) | copy-start | bytes 2949124 | tf_op jit(solution)/shard_map/while
  259.8 64.4 %copy-start.3 = (f32[5,24,2048]{2,1,0:T(8,128)S(1)}, f32[5,24,2048]{2,1,0:T(8,128)}, u32[]{:S(2)}) copy-start(f32[5,24,2048]{2,1,0:T(8,128)} %copy-done.2) | copy-start | bytes 2949124 | tf_op jit(solution)/shard_map/while
  329.6 64.4 %copy-start.3 = (f32[5,24,2048]{2,1,0:T(8,128)S(1)}, f32[5,24,2048]{2,1,0:T(8,128)}, u32[]{:S(2)}) copy-start(f32[5,24,2048]{2,1,0:T(8,128)} %copy-done.2) | copy-start | bytes 2949124 | tf_op jit(solution)/shard_map/while
  399.4 64.4 %copy-start.3 = (f32[5,24,2048]{2,1,0:T(8,128)S(1)}, f32[5,24,2048]{2,1,0:T(8,128)}, u32[]{:S(2)}) copy-start(f32[5,24,2048]{2,1,0:T(8,128)} %copy-done.2) | copy-start | bytes 2949124 | tf_op jit(solution)/shard_map/while
  463.9 10.2 collective-permute-start
  467.8 6.3 collective-permute-start.1
  474.6 9.1 collective-permute-start.3
  478.6 107.2 %collective-permute-start.2 = (bf16[1,6,8,1024]{3,2,1,0:T(8,128)(2,1)S(1)}, bf16[1,6,8,1024]{3,2,1,0:T(8,128)(2,1)S(1)}, u32[]{:S(2)}, u32[]{:S(2)}) collective-permute-start(bf16[1,6,8,1024]{3,2,1,0:T(8,128)(2,1)S(1)} %convert_bitcast_fusion.1), channel_id=1, source_target_pairs={{0,2},{2,4},{4,6},{6,8},{8,10},{10,12},{12,14},{14,16},{16,18},{18... | collective-permute-start | bytes 294920 | tf_op jit(solution)/shard_map/ppermute | solution.py:36
  586.2 7.0 collective-permute-start.5
  587.5 6.4 collective-permute-start.4
  824.0 6.9 collective-permute-start.6
  828.0 10.0 collective-permute-start.7
  838.1 6.8 collective-permute-start.9
  839.4 6.9 collective-permute-start.8
  851.0 6.5 collective-permute-start.10
  855.0 10.0 collective-permute-start.11
  865.1 7.2 collective-permute-start.13
  866.4 6.9 collective-permute-start.12
  878.1 5.8 collective-permute-start.14
  881.3 10.0 collective-permute-start.15
  891.5 7.6 collective-permute-start.17
  892.8 6.9 collective-permute-start.16
  904.4 6.7 collective-permute-start.18
  907.3 10.0 collective-permute-start.19
  917.5 7.8 collective-permute-start.21
  918.8 6.9 collective-permute-start.20
  929.0 2.7 copy-start.5
  932.9 1.9 copy-start
  938.5 66.4 %copy-start.1 = (f32[5,24,2048]{2,1,0:T(8,128)S(1)}, f32[5,24,2048]{2,1,0:T(8,128)}, u32[]{:S(2)}) copy-start(f32[5,24,2048]{2,1,0:T(8,128)} %copy-done) | copy-start | bytes 2949124 | tf_op jit(solution)/shard_map/while
  1004.9 1.9 copy-start
  1010.4 66.4 %copy-start.1 = (f32[5,24,2048]{2,1,0:T(8,128)S(1)}, f32[5,24,2048]{2,1,0:T(8,128)}, u32[]{:S(2)}) copy-start(f32[5,24,2048]{2,1,0:T(8,128)} %copy-done) | copy-start | bytes 2949124 | tf_op jit(solution)/shard_map/while
  1076.8 1.9 copy-start
  1082.4 66.4 %copy-start.1 = (f32[5,24,2048]{2,1,0:T(8,128)S(1)}, f32[5,24,2048]{2,1,0:T(8,128)}, u32[]{:S(2)}) copy-start(f32[5,24,2048]{2,1,0:T(8,128)} %copy-done) | copy-start | bytes 2949124 | tf_op jit(solution)/shard_map/while
  1154.3 66.4 %copy-start.1 = (f32[5,24,2048]{2,1,0:T(8,128)S(1)}, f32[5,24,2048]{2,1,0:T(8,128)}, u32[]{:S(2)}) copy-start(f32[5,24,2048]{2,1,0:T(8,128)} %copy-done) | copy-start | bytes 2949124 | tf_op jit(solution)/shard_map/while
  1226.3 66.4 %copy-start.1 = (f32[5,24,2048]{2,1,0:T(8,128)S(1)}, f32[5,24,2048]{2,1,0:T(8,128)}, u32[]{:S(2)}) copy-start(f32[5,24,2048]{2,1,0:T(8,128)} %copy-done) | copy-start | bytes 2949124 | tf_op jit(solution)/shard_map/while
  1292.7 1.9 copy-start
  1298.2 66.4 %copy-start.1 = (f32[5,24,2048]{2,1,0:T(8,128)S(1)}, f32[5,24,2048]{2,1,0:T(8,128)}, u32[]{:S(2)}) copy-start(f32[5,24,2048]{2,1,0:T(8,128)} %copy-done) | copy-start | bytes 2949124 | tf_op jit(solution)/shard_map/while
  1364.7 7.9 collective-permute-start.22
  1369.9 6.1 collective-permute-start.23
  1376.6 10.0 collective-permute-start.25
  1379.9 8.3 collective-permute-start.24
  1389.5 7.0 collective-permute-start.27
  1390.8 7.0 collective-permute-start.26
  1624.2 10.5 collective-permute-start.28
  1632.0 10.0 collective-permute-start.29
  1642.2 6.8 collective-permute-start.31
  1643.5 6.9 collective-permute-start.30
  1655.1 5.5 collective-permute-start.32
  1658.0 10.0 collective-permute-start.33
  1668.2 7.9 collective-permute-start.35
  1669.5 7.8 collective-permute-start.34
  1681.9 5.8 collective-permute-start.36
  1685.2 10.0 collective-permute-start.37
  1695.3 7.3 collective-permute-start.39
  1696.6 7.4 collective-permute-start.38
  1708.8 5.8 collective-permute-start.40
  1712.0 10.0 collective-permute-start.41
  1722.2 7.1 collective-permute-start.43
  1723.4 6.9 collective-permute-start.42
  (10 other events, 17.2 us)
Sparse Core Ops, SparseCore 0:
  43.7 537.3 all-reduce.76
where the time goes:
time: 1780 us; the launch traced here: 1740 us
  local copies, waits for them, and re-layouts  1220 us (69%)
  waiting for transfers between devices  173 us (10%)
  starting transfers between devices  147 us (8%)
  matrix products  66.9 us (4%)
  other arithmetic  66.7 us (4%)
  between operations  46.7 us (3%)
  loops' own time  24.2 us (1%)
    gather x2016, local copies, waits for them, and re-layouts  1130 us
    ppermute x20, starting transfers between devices, extended_2(): lax.ppermute(tail, axis, [(i, (i + 1) % count) for i in range(ends)])  100 us
    psum x1, waiting for transfers between devices, from_root(): return lax.psum(block, axis)  97.1 us
    ppermute x20, waiting for transfers between devices, extended_2(): lax.ppermute(head, axis, [((i + 1) % count, i) for i in range(ends)])  58.3 us
    dot_general x12, matrix products, one_row(): jnp.einsum('kbj,yj->kby', stacked, weight, precision=lax.Precision.HIGHEST)  39.7 us
  transfers between devices with their start and end apart: 45, of which 28 were waited for; matrix products, arithmetic and copies ran while one was open for 25% of the time, Pallas kernels for 0%

commit v1 on v0

v1 whole, which is shorter than its diff:
```python
import functools

import jax
import jax.numpy as jnp
from jax import lax
from jax.experimental import pallas as pl
from jax.experimental.pallas import tpu as pltpu
from jax.sharding import PartitionSpec as P

SUBSET = 6
SUBSETS = 2
PASSES = 4
MARGIN = 64

relaxation = 0.8
smooth_step = 0.05
smooth_floor = 0.1

ZS = 4
XW = 24
TILES = 9
WIDE = TILES * 128
WINDOW = 8
HIGHEST = lax.Precision.HIGHEST
PARAMS = pltpu.CompilerParams(vmem_limit_bytes=48 * 1024 * 1024)
F32 = jnp.float32


def view_geometry(view, xcount, margin, nviews):
    angles = jnp.pi * view.astype(jnp.float32) / nviews
    across = (2.0 * jnp.arange(xcount, dtype=jnp.float32) - (xcount - 1)) / xcount
    shifted = margin * (
        0.375 * jnp.cos(angles)[:, None] + 0.25 * jnp.sin(angles)[:, None] * across[None, :]
    ) + margin
    integral = jnp.floor(shifted)
    return (integral.astype(jnp.int32), shifted - integral)


def iota2(dim, rows=8):
    return lax.broadcasted_iota(jnp.int32, (rows, 128), dim)


def taps(fraction):
    reach = jnp.where(iota2(0) >= ZS, 0.5, 0.0) + fraction
    return (
        jnp.maximum(0.0, 1.0 - reach),
        1.0 - jnp.abs(reach - 1.0),
        jnp.maximum(0.0, reach - 1.0),
    )


def row_weights(shift, transposed):
    i = iota2(0)
    z = i if transposed else i - shift
    centers = 1.5 * z.astype(F32) + 0.25
    rows = (z + shift).astype(F32)
    weight = jnp.maximum(0.0, 1.0 - jnp.abs(centers - rows))
    return jnp.where((z >= 0) & (z < ZS), weight, 0.0)


def split_matrix(joined):
    r = lax.broadcasted_iota(jnp.int32, (256, 256), 0)
    c = lax.broadcasted_iota(jnp.int32, (256, 256), 1)
    if joined:
        r, c = c, r
    return (r == jnp.where(c < 128, 2 * c, 2 * (c - 128) + 1)).astype(F32)


def project(state, steps, fractions, base, rows_ref, rows16_ref):
    lane = iota2(1)
    weights = [row_weights(shift, False) for shift in range(3)]
    zero = jnp.zeros((8, 128), F32)
    pair = []
    for v in range(SUBSET):

        def one_x(x, sums):
            at = (base + v) * XW + x
            step = steps[at]
            coef = taps(fractions[at])
            here = pl.ds(pl.multiple_of(8 * x, 8), 8)
            turned = [pltpu.roll(state[j, here, :], step, 1) for j in range(TILES)]
            mask = lane >= step
            before = [zero] + turned
            after = turned + [zero]
            moved = [jnp.where(mask, after[j], before[j]) for j in range(TILES + 1)]
            return tuple(
                sums[k * (TILES + 1) + j] + coef[k] * moved[j]
                for k in range(3)
                for j in range(TILES + 1)
            )

        sums = lax.fori_loop(0, XW, one_x, (zero,) * (3 * (TILES + 1)), unroll=2)
        frame = []
        once = [zero] + [pltpu.roll(sums[TILES + 1 + j], 1, 1) for j in range(TILES + 1)]
        twice = [zero] + [pltpu.roll(sums[2 * TILES + 2 + j], 2, 1) for j in range(TILES + 1)]
        for j in range(TILES + 1):
            total = (
                sums[j]
                + jnp.where(lane >= 1, once[j + 1], once[j])
                + jnp.where(lane >= 2, twice[j + 1], twice[j])
            )
            total = total + pltpu.roll(total, 4, 0)
            rows = (
                weights[0] * total
                + weights[1] * pltpu.roll(total, 1, 0)
                + weights[2] * pltpu.roll(total, 2, 0)
            )
            frame.append(pltpu.roll(rows, 64, 1))
        out = [jnp.where(lane < 64, frame[j], frame[j + 1]) for j in range(TILES)]
        for j in range(TILES):
            rows_ref[8 * v : 8 * v + 8, 128 * j : 128 * j + 128] = out[j]
        pair.append(out)
        if v % 2:
            for j in range(TILES):
                both = jnp.concatenate([pair[v - 1][j], pair[v][j]], axis=0)
                rows16_ref[8 * v - 8 : 8 * v + 8, 128 * j : 128 * j + 128] = both.astype(
                    jnp.bfloat16
                )


def pack_kernel(place, first, second, edge_first, edge_second, out, held):
    column = place[0]
    for slot, (image, edge) in enumerate(((first, edge_first), (second, edge_second))):

        @pl.when(column == 0)
        def _():
            held[slot, :, :1024] = image[0].astype(F32)
            held[slot, :, 1024:] = edge[0].astype(F32)

        @pl.when(column == 1)
        def _():
            held[slot, :, 128:] = image[0].astype(F32)
            held[slot, :, :128] = edge[0].astype(F32)

    row = lax.broadcasted_iota(jnp.int32, (8, WIDE), 0)

    def two_slabs(i, carry):
        low, high = [], []
        for slot in range(2):
            a = held[slot, pl.ds(pl.multiple_of(8 * i, 8), 8), :]
            b = held[slot, pl.ds(pl.multiple_of(8 * i + 8, 8), 8), :]
            low.append(a)
            high.append(jnp.where(row < 4, pltpu.roll(a, 4, 0), pltpu.roll(b, 4, 0)))
        out[2 * i] = jnp.concatenate(low, axis=0).astype(jnp.bfloat16)
        out[2 * i + 1] = jnp.concatenate(high, axis=0).astype(jnp.bfloat16)
        return carry

    lax.fori_loop(0, out.shape[0] // 2, two_slabs, 0)


def pack(place, slots, images, edges, slab_count):
    rows = images.shape[1]
    spec = pltpu.PrefetchScalarGridSpec(
        num_scalar_prefetch=2,
        grid=(1,),
        in_specs=[
            pl.BlockSpec((1, rows, 1024), lambda i, p, s: (s[0], 0, 0)),
            pl.BlockSpec((1, rows, 1024), lambda i, p, s: (s[1], 0, 0)),
            pl.BlockSpec((1, rows, 128), lambda i, p, s: (s[0], 0, 0)),
            pl.BlockSpec((1, rows, 128), lambda i, p, s: (s[1], 0, 0)),
        ],
        out_specs=pl.BlockSpec((slab_count, 16, WIDE), lambda i, p, s: (0, 0, 0)),
        scratch_shapes=[pltpu.VMEM((2, rows, WIDE), F32)],
    )

    def kernel(p, s, *refs):
        pack_kernel(p, *refs)

    return pl.pallas_call(
        kernel,
        grid_spec=spec,
        out_shape=jax.ShapeDtypeStruct((slab_count, 16, WIDE), jnp.bfloat16),
        compiler_params=PARAMS,
        name="pack_images",
    )(place, slots, images, images, edges, edges)


def start_kernel(place, steps, fractions, volume, edge, state, rows_ref, rows16_ref):
    column = place[0]
    matrix = split_matrix(False)

    def put(pixels, tile):
        halves = jnp.dot(
            pixels.reshape(ZS * XW, 256), matrix, precision=HIGHEST, preferred_element_type=F32
        )
        for z in range(ZS):
            for p in range(2):
                state[tile, pl.ds(4 * p + z, XW, stride=8), :] = halves[
                    XW * z : XW * z + XW, 128 * p : 128 * p + 128
                ]

    for j in range(TILES - 1):
        put(volume[:, :, 256 * j : 256 * j + 256], j + column)
    put(edge[...], (TILES - 1) * (1 - column))
    project(state, steps, fractions, 0, rows_ref, rows16_ref)


def scalar_call(kernel, scalars, arrays, out_shape, scratch, name):
    vmem = pl.BlockSpec(memory_space=pltpu.VMEM)
    smem = pl.BlockSpec(memory_space=pltpu.SMEM)
    single = not isinstance(out_shape, (list, tuple))
    return pl.pallas_call(
        kernel,
        in_specs=[smem] * len(scalars) + [vmem] * len(arrays),
        out_specs=vmem if single else [vmem] * len(out_shape),
        out_shape=out_shape,
        scratch_shapes=scratch,
        compiler_params=PARAMS,
        name=name,
    )(*scalars, *arrays)


ROWS_OUT = (
    jax.ShapeDtypeStruct((TILES, 8 * XW, 128), F32),
    jax.ShapeDtypeStruct((8 * SUBSET, WIDE), F32),
    jax.ShapeDtypeStruct((8 * SUBSET, WIDE), jnp.bfloat16),
)
SLAB = (ZS, TILES, 2, XW, 128)


def update_kernel(base, place, owner, rank, steps, fractions, *refs):
    images, extra = refs[:SUBSET], refs[SUBSET : 2 * SUBSET]
    state, own, before, after, out, held, moved_state = refs[2 * SUBSET :]
    column, to_before, to_after = place[0], place[1], place[2]
    has_before, has_after, lift = place[3], place[4], place[5]
    lane, sub = iota2(1), iota2(0)
    zero = jnp.zeros((8, 128), F32)
    totals = row_weights(0, False) + row_weights(1, False) + row_weights(2, False)

    def shifted_rows(value, by):
        row = sub + by
        turned = pltpu.roll(value, lax.rem(16 - by, 8), 0)
        return jnp.where((row >= 0) & (row < 8), turned, 0.0)

    row_total = (
        totals
        + shifted_rows(totals, to_before) * has_before.astype(F32)
        + shifted_rows(totals, to_after) * has_after.astype(F32)
    )
    inner = jnp.maximum(row_total * float(2 * XW), 1.0)
    back_weights = [row_weights(shift, True) for shift in range(3)]
    edge_tile = column * (TILES - 1)
    edge_column = lane + column * (2048 - 128)

    for v in range(SUBSET):

        def one_x(x, total):
            at = (base + v) * XW + x
            fraction = fractions[at]
            pixel = edge_column - (steps[at] - MARGIN)
            weights = (
                jnp.maximum(0.0, 1.0 - fraction) + jnp.maximum(0.0, 0.5 - fraction),
                1.0 - jnp.abs(fraction - 1.0) + (1.0 - jnp.abs(fraction - 0.5)),
                jnp.maximum(0.0, fraction - 0.5),
            )
            for k in range(3):
                inside = (pixel - k >= 0) & (pixel - k < 2048)
                total = total + jnp.where(inside, weights[k], 0.0)
            return total

        edge_sum = lax.fori_loop(0, XW, one_x, zero, unroll=4)
        outer = jnp.maximum(row_total * edge_sum, 1.0)
        slot = rank[base + v]
        take = 8 * lax.rem(slot, 2) + lift
        later = (slot >= 2)
        turned = []
        if v % 2 == 0:
            pair_before = before[8 * v : 8 * v + 16, :].astype(F32)
            pair_after = after[8 * v : 8 * v + 16, :].astype(F32)
        low = 8 * (v % 2)
        image = jnp.where(later, extra[v][0].astype(F32), images[v][0].astype(F32))
        image = pltpu.roll(image, lax.rem(16 - take, 16), 0)[:8]
        for j in range(TILES):
            cols = slice(128 * j, 128 * j + 128)
            predicted = (
                own[8 * v : 8 * v + 8, cols]
                + shifted_rows(pair_before[low : low + 8, cols], to_before)
                + shifted_rows(pair_after[low : low + 8, cols], to_after)
            )
            raysum = inner
            if j == 0 or j == TILES - 1:
                raysum = jnp.where(edge_tile == j, outer, inner)
            residual = (image[:, cols] - predicted) / raysum
            mixed = back_weights[0] * residual
            for shift in (1, 2):
                mixed = mixed + back_weights[shift] * pltpu.roll(residual, 8 - shift, 0)
            mixed = mixed + pltpu.roll(mixed, 4, 0)
            turned.append(pltpu.roll(mixed, 64, 1))
        frame = [
            jnp.where(lane < 64, a, b) for a, b in zip([zero] + turned, turned + [zero])
        ]
        for shift in range(3):
            if shift == 0:
                rows = frame
            else:
                back = [pltpu.roll(tile, 128 - shift, 1) for tile in frame] + [zero]
                rows = [
                    jnp.where(lane < 128 - shift, back[j], back[j + 1])
                    for j in range(TILES + 1)
                ]
            for j in range(TILES + 1):
                held[v, shift, j] = rows[j]

    def back_x(x, carry):
        here = pl.ds(pl.multiple_of(8 * x, 8), 8)
        totals_x = [zero] * TILES
        for v in range(SUBSET):
            at = (base + v) * XW + x
            step = steps[at]
            coef = taps(fractions[at])
            turned = []
            for j in range(TILES + 1):
                mix = (
                    coef[0] * held[v, 0, j] + coef[1] * held[v, 1, j] + coef[2] * held[v, 2, j]
                )
                turned.append(pltpu.roll(mix, 128 - step, 1))
            mask = lane < 128 - step
            totals_x = [
                totals_x[j] + jnp.where(mask, turned[j], turned[j + 1]) for j in range(TILES)
            ]
        for j in range(TILES):
            moved_state[j, here, :] = state[j, here, :] + (relaxation / SUBSET) * totals_x[j]
        return carry

    lax.fori_loop(0, XW, back_x, 0)
    for j in range(TILES):
        for z in range(ZS):
            for p in range(2):
                out[z, j, p] = moved_state[j, pl.ds(4 * p + z, XW, stride=8), :]


def update(subset, place, owner, rank, steps, fractions, recv, extra, state, own, before, after):
    base = subset * SUBSET

    def of_view(v):
        return pl.BlockSpec(
            (1, 16, WIDE), lambda i, place, owner, rank, steps, fr: (owner[base + v], 0, 0)
        )

    def whole(array):
        rank_of = array.ndim
        return pl.BlockSpec(array.shape, lambda i, *scalars: (0,) * rank_of)

    spec = pltpu.PrefetchScalarGridSpec(
        num_scalar_prefetch=5,
        grid=(1,),
        in_specs=[of_view(v) for v in range(SUBSET)] * 2
        + [whole(a) for a in (state, own, before, after)],
        out_specs=pl.BlockSpec(SLAB, lambda i, *scalars: (0,) * 5),
        scratch_shapes=[
            pltpu.VMEM((SUBSET, 3, TILES + 1, 8, 128), F32),
            pltpu.VMEM((TILES, 8 * XW, 128), F32),
        ],
    )
    return pl.pallas_call(
        functools.partial(update_kernel, base),
        grid_spec=spec,
        out_shape=jax.ShapeDtypeStruct(SLAB, F32),
        compiler_params=PARAMS,
        name="residual_back",
    )(
        place, owner, rank, steps, fractions,
        *([recv] * SUBSET), *([extra] * SUBSET), state, own, before, after,
    )


def smooth(own, before, after, buffers, along, in_before, in_after, store):
    sources = (before, own, after)
    row24 = lax.broadcasted_iota(jnp.int32, (XW, 128), 0)
    lane24 = lax.broadcasted_iota(jnp.int32, (XW, 128), 1)
    zero = jnp.zeros((XW, 128), F32)
    for index in range(PASSES):
        low, high = 1 + index, 10 - index
        last = index == PASSES - 1
        target = buffers[index % 2]
        source = buffers[(index + 1) % 2]

        def load(z, j, parity, index=index, source=source):
            if index == 0:
                return sources[z // ZS][z % ZS, j, parity]
            return source[z, j, parity]

        for z in range(low, high + 1):
            along[z] = zero

        def one_tile(j, carry, low=low, high=high, last=last, target=target, load=load):
            following = jnp.minimum(j + 1, TILES - 1)
            has_following = j < TILES - 1
            current = [load(low - 1, j, p) for p in range(2)]
            flux_before = None
            for z in range(low - 1, high + 1):
                above = [load(z + 1, j, p) for p in range(2)]
                beside = jnp.where(has_following, load(z, following, 0), 0.0)
                next_even = pltpu.roll(
                    jnp.where(lane24 == 0, beside, current[0]), 127, 1
                )
                ahead = [current[1], next_even]
                fluxes = []
                for p in range(2):
                    c = current[p]
                    dz = above[p] - c
                    dx = jnp.where(row24 < XW - 1, pltpu.roll(c, XW - 1, 0), 0.0) - c
                    dy = ahead[p] - c
                    scale = lax.rsqrt(dz * dz + dx * dx + dy * dy + smooth_floor)
                    fluxes.append((dz * scale, dx * scale, dy * scale))
                flux_z = [fluxes[p][0] for p in range(2)]
                if z < ZS:
                    flux_z = [f * in_before for f in flux_z]
                if z >= low:
                    turned = pltpu.roll(fluxes[1][2], 1, 1)
                    behind_even = jnp.where(lane24 == 0, along[z], turned)
                    along[z] = turned
                    behind = [behind_even, fluxes[0][2]]
                    for p in range(2):
                        flux_x = fluxes[p][1]
                        back_x = jnp.where(row24 > 0, pltpu.roll(flux_x, 1, 0), 0.0)
                        gradient = (
                            (flux_before[p] - fluxes[p][0])
                            + (back_x - flux_x)
                            + (behind[p] - fluxes[p][2])
                        )
                        fresh = current[p] - smooth_step * gradient
                        if z < ZS:
                            fresh = fresh * in_before
                        if z >= 2 * ZS:
                            fresh = fresh * in_after
                        if last:
                            store(z - ZS, j, p, fresh)
                        else:
                            target[z, j, p] = fresh
                flux_before = flux_z
                current = above
            return carry

        lax.fori_loop(0, TILES, one_tile, 0)


SMOOTH_SCRATCH = [
    pltpu.VMEM((3 * ZS, TILES, 2, XW, 128), F32),
    pltpu.VMEM((3 * ZS, TILES, 2, XW, 128), F32),
    pltpu.VMEM((3 * ZS, XW, 128), F32),
]


def smooth_project_kernel(
    place, steps, fractions, own, before, after, state, rows_ref, rows16_ref, one, two, along
):
    def store(z, j, p, value):
        state[j, pl.ds(4 * p + z, XW, stride=8), :] = value

    smooth(
        own, before, after, (one, two), along,
        place[3].astype(F32), place[4].astype(F32), store,
    )
    project(state, steps, fractions, SUBSET, rows_ref, rows16_ref)


def smooth_end_kernel(place, own, before, after, out, one, two, along):
    def store(z, j, p, value):
        two[z, j, p] = value

    smooth(
        own, before, after, (one, two), along,
        place[3].astype(F32), place[4].astype(F32), store,
    )
    matrix = split_matrix(True)
    column = place[0]
    for j in range(TILES - 1):
        pixels = jnp.concatenate(
            [
                jnp.concatenate([two[z, j + column, 0], two[z, j + column, 1]], axis=1)
                for z in range(ZS)
            ],
            axis=0,
        )
        joined = jnp.dot(pixels, matrix, precision=HIGHEST, preferred_element_type=F32)
        out[:, :, 256 * j : 256 * j + 256] = joined.reshape(ZS, XW, 256)


def to_next(value):
    count = lax.axis_size("gz")
    return lax.ppermute(value, "gz", [(i, i + 1) for i in range(count - 1)])


def to_before(value):
    count = lax.axis_size("gz")
    return lax.ppermute(value, "gz", [(i + 1, i) for i in range(count - 1)])


def swap_halves(value):
    return lax.ppermute(value, "col", [(0, 1), (1, 0)])


def body(volume, images, owners, subsets, offsets):
    slab_count = lax.axis_size("gz")
    slab = lax.axis_index("gz")
    column = lax.axis_index("col")
    stored = images.shape[0]
    nviews = owners.shape[0]

    edge = swap_halves(jnp.where(column == 0, volume[:, :, -256:], volume[:, :, :256]))
    image_edge = swap_halves(jnp.where(column == 0, images[:, :, -128:], images[:, :, :128]))

    views = subsets.reshape(-1)
    positions = jnp.sum(
        jnp.where(
            owners[None, :] == views[:, None], jnp.arange(nviews, dtype=jnp.int32)[None, :], 0
        ),
        axis=1,
    )
    owner = positions // stored
    count = SUBSETS * SUBSET
    order = jnp.arange(count)
    rank = jnp.sum(
        ((owner[None, :] == owner[:, None]) & (order[None, :] < order[:, None])).astype(jnp.int32),
        axis=1,
    )
    slots = jnp.sum(
        jnp.where(
            (owner[None, :] == slab) & (rank[None, :] == jnp.arange(4)[:, None]),
            (positions % stored)[None, :],
            0,
        ),
        axis=1,
    )
    steps, fractions = view_geometry(views, XW, MARGIN, nviews)
    steps, fractions = steps.reshape(-1), fractions.reshape(-1)

    own_start = offsets[slab]
    before_start = offsets[jnp.maximum(slab - 1, 0)]
    next_start = offsets[jnp.minimum(slab + 1, slab_count - 1)]
    place = jnp.stack(
        [
            column,
            own_start - before_start,
            own_start - next_start,
            (slab > 0).astype(jnp.int32),
            (slab < slab_count - 1).astype(jnp.int32),
            own_start - slab * ZS,
        ]
    ).astype(jnp.int32)

    def fetched(two_slots):
        packed = pack(place, two_slots, images, image_edge, slab_count)
        return lax.all_to_all(packed, "gz", 0, 0)

    recv = fetched(slots[:2])
    extra = lax.cond(
        jnp.max(rank) >= 2,
        lambda: fetched(slots[2:]),
        lambda: jnp.zeros((slab_count, 16, WIDE), jnp.bfloat16),
    )

    state, rows, rows16 = scalar_call(
        start_kernel, (place, steps, fractions), (volume, edge), ROWS_OUT, [], "split_project"
    )
    for subset in range(SUBSETS):
        fresh = update(
            subset, place, owner, rank, steps, fractions, recv, extra,
            state, rows, to_next(rows16), to_before(rows16),
        )
        around = (fresh, to_next(fresh), to_before(fresh))
        if subset < SUBSETS - 1:
            state, rows, rows16 = scalar_call(
                smooth_project_kernel, (place, steps, fractions), around, ROWS_OUT,
                SMOOTH_SCRATCH, "smooth_project",
            )
    return scalar_call(
        smooth_end_kernel, (place,), around,
        jax.ShapeDtypeStruct(volume.shape, F32), SMOOTH_SCRATCH, "smooth_join",
    )


def solution(mesh):
    in_specs = (P("gz", None, "col"), P("gz", None, "col"), P(), P(), P())
    out_specs = P("gz", None, "col")
    return jax.shard_map(body, mesh=mesh, in_specs=in_specs, out_specs=out_specs, check_vma=False)
```

time: 1780 us -> 174 us (0.10)
  the two profiles are of different devices: /device:TPU:15 before, /device:TPU:32 now
where the time goes in v1:
time: 174 us; the launch traced here: 173 us
  waiting for transfers between devices  72.2 us (41%)
  Pallas kernels  52 us (30%)
  starting transfers between devices  35.5 us (20%)
  local copies, waits for them, and re-layouts  6.07 us (3%)
  between operations  3.97 us (2%)
  other arithmetic  3.12 us (2%)
    pallas_call x3, Pallas kernels, scalar_call(): pl.pallas_call(kernel, in_specs=[smem] * len(scalars) + [vmem] * len(arra...  35.9 us
    ppermute x2, waiting for transfers between devices, swap_halves(): return lax.ppermute(value, 'col', [(0, 1), (1, 0)])  28.5 us
    ppermute x4, waiting for transfers between devices, to_next(): return lax.ppermute(value, 'gz', [(i, i + 1) for i in range(count - 1)])  27.1 us
    ppermute x4, waiting for transfers between devices, to_before(): return lax.ppermute(value, 'gz', [(i + 1, i) for i in range(count - 1)])  16.6 us
    pallas_call x2, Pallas kernels, update(): pl.pallas_call(functools.partial(update_kernel, base), grid_spec=spec, ou...  13.4 us
    ppermute x4, starting transfers between devices, to_before(): return lax.ppermute(value, 'gz', [(i + 1, i) for i in range(count - 1)])  12 us
    ppermute x4, starting transfers between devices, to_next(): return lax.ppermute(value, 'gz', [(i, i + 1) for i in range(count - 1)])  9.14 us
    all_to_all x1, starting transfers between devices, fetched(): return lax.all_to_all(packed, 'gz', 0, 0)  8.69 us
  transfers between devices with their start and end apart: 11, of which 8 were waited for; matrix products, arithmetic and copies ran while one was open for 3% of the time, Pallas kernels for 6%

profile of v1, /device:TPU:32, one launch (start us, length us, event | category | flops | bytes accessed | tf_op | source)
XLA Modules:
  0.0 172.9 jit_solution(18396081367354744690)
XLA Ops:
  0.0 1.1 slice_select_fusion
  1.1 3.3 %collective-permute-start = (bf16[4,264,128]{2,1,0:T(8,128)(2,1)S(1)}, bf16[4,264,128]{2,1,0:T(8,128)(2,1)S(1)}, u32[]{:S(2)}, u32[]{:S(2)}) collective-permute-start(bf16[4,264,128]{2,1,0:T(8,128)(2,1)S(1)} %slice_select_fusion), channel_id=1, source_target_pairs={{0,1},{1,0},{2,3},{3,2},{4,5},{5,4},{6,7},{7,6},{8,9},{9,8},{10,11... | collective-permute-start | bytes 811016 | tf_op jit(solution)/shard_map/ppermute | solution.py:491
  4.3 1.4 fusion.2
  8.8 0.8 eq.59
  9.6 0.9 select_reduce_fusion
  10.5 0.2 convert_reduce_fusion.rank
  10.7 0.7 reduce_max.9
  12.1 0.1 stack.35.p.place
  12.2 0.1 select_reduce_fusion.1
  12.3 0.0 collective-permute-done.refs_2_.refs_3_
  12.3 0.2 conditional.1
  12.3 0.2 broadcast.173
  12.5 0.0 copy-start.4
  12.5 2.7 %pack_images.3 = bf16[64,16,1152]{2,1,0:T(8,128)(2,1)S(1)} custom-call(s32[6]{0:T(128)S(1)} %stack.35.p.place, s32[2]{0:T(128)S(1)} %bitcast.10, bf16[4,264,1024]{2,1,0:T(8,128)(2,1)} %refs_1_.1, bf16[4,264,1024]{2,1,0:T(8,128)(2,1)} %refs_1_.1, bf16[4,264,128]{2,1,0:T(8,128)(2,1)S(1)} %collective-permute-done.refs_2_.refs_3_, ...), custom_call_target="tpu_custom_call" | custom-call | tf_op jit(solution)/shard_map/pack_images/pallas_call | solution.py:169
  15.2 0.0 copy-done.4
  15.2 0.0 copy-start
  15.2 1.4 copy-done
  16.6 0.0 copy-start.1
  16.6 8.7 %all-to-all-start.1 = ((bf16[64,16,1152]{2,1,0:T(8,128)(2,1)}), bf16[64,16,1152]{2,1,0:T(8,128)(2,1)S(1)}, u32[]{:S(2)}, u32[]{:S(2)}) async-start(bf16[64,16,1152]{2,1,0:T(8,128)(2,1)} %copy-done), calls=%async_computation.1 | async-start | bytes 4718592 | tf_op jit(solution)/shard_map/all_to_all | solution.py:545
  25.3 0.0 copy-done.1
  25.4 2.4 %collective-permute-start.1 = (f32[4,24,256]{2,1,0:T(8,128)S(1)}, f32[4,24,256]{2,1,0:T(8,128)S(1)}, u32[]{:S(2)}, u32[]{:S(2)}) collective-permute-start(f32[4,24,256]{2,1,0:T(8,128)S(1)} %slice_select_fusion.1), channel_id=1, source_target_pairs={{0,1},{1,0},{2,3},{3,2},{4,5},{5,4},{6,7},{7,6},{8,9},{9,8},{10,11... | collective-permute-start | bytes 294920 | tf_op jit(solution)/shard_map/ppermute | solution.py:491
  27.9 0.1 multiply_add_fusion
  27.9 0.1 add.63
  28.0 28.5 %collective-permute-done.1.edge = f32[4,24,256]{2,1,0:T(8,128)S(1)} collective-permute-done((f32[4,24,256]{2,1,0:T(8,128)S(1)}, f32[4,24,256]{2,1,0:T(8,128)S(1)}, u32[]{:S(2)}, u32[]{:S(2)}) %collective-permute-start.1) | collective-permute-done | bytes 98336 | tf_op jit(solution)/shard_map/ppermute | solution.py:491
  56.5 9.9 %split_project.1 = (f32[9,192,128]{2,1,0:T(8,128)S(1)}, f32[48,1152]{1,0:T(8,128)S(1)}, bf16[48,1152]{1,0:T(8,128)(2,1)S(1)}) custom-call(s32[6]{0:T(128)S(1)} %stack.35.p.place, s32[288]{0:T(512)S(1)} %get-tuple-element.35.steps, f32[288]{0:T(512)S(1)} %get-tuple-element.34.fractions, f32[4,24,2048]{2,1,0:T(8,128)S(1)} %copy-done.1, ...), custom_call_target="tpu_custom_call" | custom-call | tf_op jit(solution)/shard_map/split_project/pallas_call | solution.py:202
  66.5 0.0 copy-start.2
  66.5 0.9 copy-done.2
  67.4 6.1 %collective-permute-start.3 = (bf16[48,1152]{1,0:T(8,128)(2,1)S(1)}, bf16[48,1152]{1,0:T(8,128)(2,1)S(1)}, u32[]{:S(2)}, u32[]{:S(2)}) collective-permute-start(bf16[48,1152]{1,0:T(8,128)(2,1)S(1)} %get-tuple-element.28), channel_id=1, source_target_pairs={{2,0},{4,2},{6,4},{8,6},{10,8},{12,10},{14,12},{16,14},{18,16},{20... | collective-permute-start | bytes 331784 | tf_op jit(solution)/shard_map/ppermute | solution.py:487
  73.5 1.9 %collective-permute-start.2 = (bf16[48,1152]{1,0:T(8,128)(2,1)S(1)}, bf16[48,1152]{1,0:T(8,128)(2,1)S(1)}, u32[]{:S(2)}, u32[]{:S(2)}) collective-permute-start(bf16[48,1152]{1,0:T(8,128)(2,1)S(1)} %get-tuple-element.28), channel_id=1, source_target_pairs={{0,2},{2,4},{4,6},{6,8},{8,10},{10,12},{12,14},{14,16},{16,18},{18... | collective-permute-start | bytes 331784 | tf_op jit(solution)/shard_map/ppermute | solution.py:482
  75.4 0.4 collective-permute-done.3.refs_15_
  75.8 6.8 %collective-permute-done.2.refs_14_ = bf16[48,1152]{1,0:T(8,128)(2,1)S(1)} collective-permute-done((bf16[48,1152]{1,0:T(8,128)(2,1)S(1)}, bf16[48,1152]{1,0:T(8,128)(2,1)S(1)}, u32[]{:S(2)}, u32[]{:S(2)}) %collective-permute-start.2) | collective-permute-done | bytes 110624 | tf_op jit(solution)/shard_map/ppermute | solution.py:482
  82.6 0.0 all-to-all-done.1.refs_0_.refs_1_.refs_2_.refs_3_.refs_4_.refs_5_
  82.6 0.0 copy-start.3
  82.6 1.2 copy-done.3
  83.8 7.1 %residual_back.2.own = f32[4,9,2,24,128]{4,3,2,1,0:T(8,128)S(1)} custom-call(s32[6]{0:T(128)S(1)} %stack.35.p.place, s32[12]{0:T(128)S(1)} %get-tuple-element.33.owner, s32[12]{0:T(128)S(1)} %convert_reduce_fusion.rank, s32[288]{0:T(512)S(1)} %get-tuple-element.35.steps, f32[288]{0:T(512)S(1)} %get-tuple-element.34.fractions, ...), custom_call_target="tpu_custom_call" | custom-call | tf_op jit(solution)/shard_map/residual_back/pallas_call | solution.py:355
  90.9 0.0 copy-start.5
  90.9 2.1 %collective-permute-start.5 = (f32[4,9,2,24,128]{4,3,2,1,0:T(8,128)S(1)}, f32[4,9,2,24,128]{4,3,2,1,0:T(8,128)S(1)}, u32[]{:S(2)}, u32[]{:S(2)}) collective-permute-start(f32[4,9,2,24,128]{4,3,2,1,0:T(8,128)S(1)} %residual_back.2.own), channel_id=1, source_target_pairs={{2,0},{4,2},{6,4},{8,6},{10,8},{12,10},{14,12},{16,14},{18,16},{20... | collective-permute-start | bytes 2654216 | tf_op jit(solution)/shard_map/ppermute | solution.py:487
  93.0 2.4 %collective-permute-start.4 = (f32[4,9,2,24,128]{4,3,2,1,0:T(8,128)S(1)}, f32[4,9,2,24,128]{4,3,2,1,0:T(8,128)S(1)}, u32[]{:S(2)}, u32[]{:S(2)}) collective-permute-start(f32[4,9,2,24,128]{4,3,2,1,0:T(8,128)S(1)} %residual_back.2.own), channel_id=1, source_target_pairs={{0,2},{2,4},{4,6},{6,8},{8,10},{10,12},{12,14},{14,16},{16,18},{18... | collective-permute-start | bytes 2654216 | tf_op jit(solution)/shard_map/ppermute | solution.py:482
  95.4 8.1 %collective-permute-done.5.after = f32[4,9,2,24,128]{4,3,2,1,0:T(8,128)S(1)} collective-permute-done((f32[4,9,2,24,128]{4,3,2,1,0:T(8,128)S(1)}, f32[4,9,2,24,128]{4,3,2,1,0:T(8,128)S(1)}, u32[]{:S(2)}, u32[]{:S(2)}) %collective-permute-start.5) | collective-permute-done | bytes 884768 | tf_op jit(solution)/shard_map/ppermute | solution.py:487
  103.5 6.8 %collective-permute-done.4.before = f32[4,9,2,24,128]{4,3,2,1,0:T(8,128)S(1)} collective-permute-done((f32[4,9,2,24,128]{4,3,2,1,0:T(8,128)S(1)}, f32[4,9,2,24,128]{4,3,2,1,0:T(8,128)S(1)}, u32[]{:S(2)}, u32[]{:S(2)}) %collective-permute-start.4) | collective-permute-done | bytes 884768 | tf_op jit(solution)/shard_map/ppermute | solution.py:482
  110.3 16.0 %smooth_project.1 = (f32[9,192,128]{2,1,0:T(8,128)S(1)}, f32[48,1152]{1,0:T(8,128)S(1)}, bf16[48,1152]{1,0:T(8,128)(2,1)S(1)}) custom-call(s32[6]{0:T(128)S(1)} %stack.35.p.place, s32[288]{0:T(512)S(1)} %get-tuple-element.35.steps, f32[288]{0:T(512)S(1)} %get-tuple-element.34.fractions, f32[4,9,2,24,128]{4,3,2,1,0:T(8,128)S(1)} %residual_back.2.own, ...), custom_call_target="tpu_custom_call" | custom-call | tf_op jit(solution)/shard_map/smooth_project/pallas_call | solution.py:202
  126.3 1.9 %collective-permute-start.7 = (bf16[48,1152]{1,0:T(8,128)(2,1)S(1)}, bf16[48,1152]{1,0:T(8,128)(2,1)S(1)}, u32[]{:S(2)}, u32[]{:S(2)}) collective-permute-start(bf16[48,1152]{1,0:T(8,128)(2,1)S(1)} %get-tuple-element.31), channel_id=1, source_target_pairs={{2,0},{4,2},{6,4},{8,6},{10,8},{12,10},{14,12},{16,14},{18,16},{20... | collective-permute-start | bytes 331784 | tf_op jit(solution)/shard_map/ppermute | solution.py:487
  128.3 2.4 %collective-permute-start.6 = (bf16[48,1152]{1,0:T(8,128)(2,1)S(1)}, bf16[48,1152]{1,0:T(8,128)(2,1)S(1)}, u32[]{:S(2)}, u32[]{:S(2)}) collective-permute-start(bf16[48,1152]{1,0:T(8,128)(2,1)S(1)} %get-tuple-element.31), channel_id=1, source_target_pairs={{0,2},{2,4},{4,6},{6,8},{8,10},{10,12},{12,14},{14,16},{16,18},{18... | collective-permute-start | bytes 331784 | tf_op jit(solution)/shard_map/ppermute | solution.py:482
  130.7 0.0 collective-permute-done.7.refs_15_
  130.7 6.7 %collective-permute-done.6.refs_14_ = bf16[48,1152]{1,0:T(8,128)(2,1)S(1)} collective-permute-done((bf16[48,1152]{1,0:T(8,128)(2,1)S(1)}, bf16[48,1152]{1,0:T(8,128)(2,1)S(1)}, u32[]{:S(2)}, u32[]{:S(2)}) %collective-permute-start.6) | collective-permute-done | bytes 110624 | tf_op jit(solution)/shard_map/ppermute | solution.py:482
  137.3 0.0 copy-done.5
  137.3 6.3 %residual_back.3.own = f32[4,9,2,24,128]{4,3,2,1,0:T(8,128)S(1)} custom-call(s32[6]{0:T(128)S(1)} %stack.35.p.place, s32[12]{0:T(128)S(1)} %get-tuple-element.33.owner, s32[12]{0:T(128)S(1)} %convert_reduce_fusion.rank, s32[288]{0:T(512)S(1)} %get-tuple-element.35.steps, f32[288]{0:T(512)S(1)} %get-tuple-element.34.fractions, ...), custom_call_target="tpu_custom_call" | custom-call | tf_op jit(solution)/shard_map/residual_back/pallas_call | solution.py:355
  143.6 1.9 %collective-permute-start.9 = (f32[4,9,2,24,128]{4,3,2,1,0:T(8,128)S(1)}, f32[4,9,2,24,128]{4,3,2,1,0:T(8,128)S(1)}, u32[]{:S(2)}, u32[]{:S(2)}) collective-permute-start(f32[4,9,2,24,128]{4,3,2,1,0:T(8,128)S(1)} %residual_back.3.own), channel_id=1, source_target_pairs={{2,0},{4,2},{6,4},{8,6},{10,8},{12,10},{14,12},{16,14},{18,16},{20... | collective-permute-start | bytes 2654216 | tf_op jit(solution)/shard_map/ppermute | solution.py:487
  145.6 2.4 %collective-permute-start.8 = (f32[4,9,2,24,128]{4,3,2,1,0:T(8,128)S(1)}, f32[4,9,2,24,128]{4,3,2,1,0:T(8,128)S(1)}, u32[]{:S(2)}, u32[]{:S(2)}) collective-permute-start(f32[4,9,2,24,128]{4,3,2,1,0:T(8,128)S(1)} %residual_back.3.own), channel_id=1, source_target_pairs={{0,2},{2,4},{4,6},{6,8},{8,10},{10,12},{12,14},{14,16},{16,18},{18... | collective-permute-start | bytes 2654216 | tf_op jit(solution)/shard_map/ppermute | solution.py:482
  148.0 8.1 %collective-permute-done.9.after = f32[4,9,2,24,128]{4,3,2,1,0:T(8,128)S(1)} collective-permute-done((f32[4,9,2,24,128]{4,3,2,1,0:T(8,128)S(1)}, f32[4,9,2,24,128]{4,3,2,1,0:T(8,128)S(1)}, u32[]{:S(2)}, u32[]{:S(2)}) %collective-permute-start.9) | collective-permute-done | bytes 884768 | tf_op jit(solution)/shard_map/ppermute | solution.py:487
  156.1 6.8 %collective-permute-done.8.before = f32[4,9,2,24,128]{4,3,2,1,0:T(8,128)S(1)} collective-permute-done((f32[4,9,2,24,128]{4,3,2,1,0:T(8,128)S(1)}, f32[4,9,2,24,128]{4,3,2,1,0:T(8,128)S(1)}, u32[]{:S(2)}, u32[]{:S(2)}) %collective-permute-start.8) | collective-permute-done | bytes 884768 | tf_op jit(solution)/shard_map/ppermute | solution.py:482
  162.9 10.0 %smooth_join.1 = f32[4,24,2048]{2,1,0:T(8,128)} custom-call(s32[6]{0:T(128)S(1)} %stack.35.p.place, f32[4,9,2,24,128]{4,3,2,1,0:T(8,128)S(1)} %residual_back.3.own, f32[4,9,2,24,128]{4,3,2,1,0:T(8,128)S(1)} %collective-permute-done.8.before, f32[4,9,2,24,128]{4,3,2,1,0:T(8,128)S(1)} %collective-permute-done.9.after), custom_call_target="tpu_custom_call" | custom-call | tf_op jit(solution)/shard_map/smooth_join/pallas_call | solution.py:202
  (6 shorter events, 0.1 us)
Async XLA Ops:
  1.1 11.2 %collective-permute-start = (bf16[4,264,128]{2,1,0:T(8,128)(2,1)S(1)}, bf16[4,264,128]{2,1,0:T(8,128)(2,1)S(1)}, u32[]{:S(2)}, u32[]{:S(2)}) collective-permute-start(bf16[4,264,128]{2,1,0:T(8,128)(2,1)S(1)} %slice_select_fusion), channel_id=1, source_target_pairs={{0,1},{1,0},{2,3},{3,2},{4,5},{5,4},{6,7},{7,6},{8,9},{9,8},{10,11... | collective-permute-start | bytes 811016 | tf_op jit(solution)/shard_map/ppermute | solution.py:491
  12.5 2.7 %copy-start.4 = (bf16[64,16,1152]{2,1,0:T(8,128)(2,1)}, bf16[64,16,1152]{2,1,0:T(8,128)(2,1)S(1)}, u32[]{:S(2)}) copy-start(bf16[64,16,1152]{2,1,0:T(8,128)(2,1)S(1)} %get-tuple-element.41.refs_6_.refs_7_.refs_8_.refs_9_.refs_10_.refs_11_) | copy-start | bytes 7077892
  15.2 1.4 copy-start
  16.6 8.7 %copy-start.1 = (f32[4,24,2048]{2,1,0:T(8,128)S(1)}, f32[4,24,2048]{2,1,0:T(8,128)}, u32[]{:S(2)}) copy-start(f32[4,24,2048]{2,1,0:T(8,128)} %volume.1) | copy-start | bytes 2359300
  16.6 66.0 %all-to-all-start.1 = ((bf16[64,16,1152]{2,1,0:T(8,128)(2,1)}), bf16[64,16,1152]{2,1,0:T(8,128)(2,1)S(1)}, u32[]{:S(2)}, u32[]{:S(2)}) async-start(bf16[64,16,1152]{2,1,0:T(8,128)(2,1)} %copy-done), calls=%async_computation.1 | async-start | bytes 4718592 | tf_op jit(solution)/shard_map/all_to_all | solution.py:545
  25.4 31.2 %collective-permute-start.1 = (f32[4,24,256]{2,1,0:T(8,128)S(1)}, f32[4,24,256]{2,1,0:T(8,128)S(1)}, u32[]{:S(2)}, u32[]{:S(2)}) collective-permute-start(f32[4,24,256]{2,1,0:T(8,128)S(1)} %slice_select_fusion.1), channel_id=1, source_target_pairs={{0,1},{1,0},{2,3},{3,2},{4,5},{5,4},{6,7},{7,6},{8,9},{9,8},{10,11... | collective-permute-start | bytes 294920 | tf_op jit(solution)/shard_map/ppermute | solution.py:491
  66.5 1.0 copy-start.2
  67.4 8.4 %collective-permute-start.3 = (bf16[48,1152]{1,0:T(8,128)(2,1)S(1)}, bf16[48,1152]{1,0:T(8,128)(2,1)S(1)}, u32[]{:S(2)}, u32[]{:S(2)}) collective-permute-start(bf16[48,1152]{1,0:T(8,128)(2,1)S(1)} %get-tuple-element.28), channel_id=1, source_target_pairs={{2,0},{4,2},{6,4},{8,6},{10,8},{12,10},{14,12},{16,14},{18,16},{20... | collective-permute-start | bytes 331784 | tf_op jit(solution)/shard_map/ppermute | solution.py:487
  73.5 9.1 %collective-permute-start.2 = (bf16[48,1152]{1,0:T(8,128)(2,1)S(1)}, bf16[48,1152]{1,0:T(8,128)(2,1)S(1)}, u32[]{:S(2)}, u32[]{:S(2)}) collective-permute-start(bf16[48,1152]{1,0:T(8,128)(2,1)S(1)} %get-tuple-element.28), channel_id=1, source_target_pairs={{0,2},{2,4},{4,6},{6,8},{8,10},{10,12},{12,14},{14,16},{16,18},{18... | collective-permute-start | bytes 331784 | tf_op jit(solution)/shard_map/ppermute | solution.py:482
  82.6 1.2 copy-start.3
  90.9 46.5 %copy-start.5 = (bf16[64,16,1152]{2,1,0:T(8,128)(2,1)S(1)}, bf16[64,16,1152]{2,1,0:T(8,128)(2,1)}, u32[]{:S(2)}) copy-start(bf16[64,16,1152]{2,1,0:T(8,128)(2,1)} %copy-done.4) | copy-start | bytes 7077892
  90.9 12.6 %collective-permute-start.5 = (f32[4,9,2,24,128]{4,3,2,1,0:T(8,128)S(1)}, f32[4,9,2,24,128]{4,3,2,1,0:T(8,128)S(1)}, u32[]{:S(2)}, u32[]{:S(2)}) collective-permute-start(f32[4,9,2,24,128]{4,3,2,1,0:T(8,128)S(1)} %residual_back.2.own), channel_id=1, source_target_pairs={{2,0},{4,2},{6,4},{8,6},{10,8},{12,10},{14,12},{16,14},{18,16},{20... | collective-permute-start | bytes 2654216 | tf_op jit(solution)/shard_map/ppermute | solution.py:487
  93.0 17.4 %collective-permute-start.4 = (f32[4,9,2,24,128]{4,3,2,1,0:T(8,128)S(1)}, f32[4,9,2,24,128]{4,3,2,1,0:T(8,128)S(1)}, u32[]{:S(2)}, u32[]{:S(2)}) collective-permute-start(f32[4,9,2,24,128]{4,3,2,1,0:T(8,128)S(1)} %residual_back.2.own), channel_id=1, source_target_pairs={{0,2},{2,4},{4,6},{6,8},{8,10},{10,12},{12,14},{14,16},{16,18},{18... | collective-permute-start | bytes 2654216 | tf_op jit(solution)/shard_map/ppermute | solution.py:482
  126.3 4.3 %collective-permute-start.7 = (bf16[48,1152]{1,0:T(8,128)(2,1)S(1)}, bf16[48,1152]{1,0:T(8,128)(2,1)S(1)}, u32[]{:S(2)}, u32[]{:S(2)}) collective-permute-start(bf16[48,1152]{1,0:T(8,128)(2,1)S(1)} %get-tuple-element.31), channel_id=1, source_target_pairs={{2,0},{4,2},{6,4},{8,6},{10,8},{12,10},{14,12},{16,14},{18,16},{20... | collective-permute-start | bytes 331784 | tf_op jit(solution)/shard_map/ppermute | solution.py:487
  128.3 9.1 %collective-permute-start.6 = (bf16[48,1152]{1,0:T(8,128)(2,1)S(1)}, bf16[48,1152]{1,0:T(8,128)(2,1)S(1)}, u32[]{:S(2)}, u32[]{:S(2)}) collective-permute-start(bf16[48,1152]{1,0:T(8,128)(2,1)S(1)} %get-tuple-element.31), channel_id=1, source_target_pairs={{0,2},{2,4},{4,6},{6,8},{8,10},{10,12},{12,14},{14,16},{16,18},{18... | collective-permute-start | bytes 331784 | tf_op jit(solution)/shard_map/ppermute | solution.py:482
  143.6 12.5 %collective-permute-start.9 = (f32[4,9,2,24,128]{4,3,2,1,0:T(8,128)S(1)}, f32[4,9,2,24,128]{4,3,2,1,0:T(8,128)S(1)}, u32[]{:S(2)}, u32[]{:S(2)}) collective-permute-start(f32[4,9,2,24,128]{4,3,2,1,0:T(8,128)S(1)} %residual_back.3.own), channel_id=1, source_target_pairs={{2,0},{4,2},{6,4},{8,6},{10,8},{12,10},{14,12},{16,14},{18,16},{20... | collective-permute-start | bytes 2654216 | tf_op jit(solution)/shard_map/ppermute | solution.py:487
  145.6 17.4 %collective-permute-start.8 = (f32[4,9,2,24,128]{4,3,2,1,0:T(8,128)S(1)}, f32[4,9,2,24,128]{4,3,2,1,0:T(8,128)S(1)}, u32[]{:S(2)}, u32[]{:S(2)}) collective-permute-start(f32[4,9,2,24,128]{4,3,2,1,0:T(8,128)S(1)} %residual_back.3.own), channel_id=1, source_target_pairs={{0,2},{2,4},{4,6},{6,8},{8,10},{10,12},{12,14},{14,16},{16,18},{18... | collective-permute-start | bytes 2654216 | tf_op jit(solution)/shard_map/ppermute | solution.py:482

commit v2 on v1

--- a/solution.py
+++ b/solution.py
@@ -20,10 +20,13 @@
 XW = 24
 TILES = 9
 WIDE = TILES * 128
-WINDOW = 8
+USED = 6
+PACKED = 112
 HIGHEST = lax.Precision.HIGHEST
 PARAMS = pltpu.CompilerParams(vmem_limit_bytes=48 * 1024 * 1024)
 F32 = jnp.float32
+PROJECT_UNROLL = 24
+BACK_UNROLL = 8
 
 
 def view_geometry(view, xcount, margin, nviews):
@@ -89,7 +92,7 @@
                 for j in range(TILES + 1)
             )
 
-        sums = lax.fori_loop(0, XW, one_x, (zero,) * (3 * (TILES + 1)), unroll=2)
+        sums = lax.fori_loop(0, XW, one_x, (zero,) * (3 * (TILES + 1)), unroll=PROJECT_UNROLL)
         frame = []
         once = [zero] + [pltpu.roll(sums[TILES + 1 + j], 1, 1) for j in range(TILES + 1)]
         twice = [zero] + [pltpu.roll(sums[2 * TILES + 2 + j], 2, 1) for j in range(TILES + 1)]
@@ -118,61 +121,73 @@
                 )
 
 
-def pack_kernel(place, first, second, edge_first, edge_second, out, held):
-    column = place[0]
-    for slot, (image, edge) in enumerate(((first, edge_first), (second, edge_second))):
-
-        @pl.when(column == 0)
-        def _():
-            held[slot, :, :1024] = image[0].astype(F32)
-            held[slot, :, 1024:] = edge[0].astype(F32)
-
-        @pl.when(column == 1)
-        def _():
-            held[slot, :, 128:] = image[0].astype(F32)
-            held[slot, :, :128] = edge[0].astype(F32)
-
-    row = lax.broadcasted_iota(jnp.int32, (8, WIDE), 0)
-
-    def two_slabs(i, carry):
-        low, high = [], []
+def pack_kernel(first_slot, owners, subsets, offsets, images, edges, out, got, got_edge, held, sems):
+    slab, column = lax.axis_index("gz"), lax.axis_index("col")
+    stored = images.shape[0]
+    count = subsets.shape[0]
+    found = jnp.int32(0)
+    slots = [jnp.int32(0), jnp.int32(0)]
+    for i in range(stored):
+        view = owners[stored * slab + i]
+        hits = jnp.int32(0)
+        for k in range(count):
+            hits = hits + (subsets[k] == view).astype(jnp.int32)
         for slot in range(2):
-            a = held[slot, pl.ds(pl.multiple_of(8 * i, 8), 8), :]
-            b = held[slot, pl.ds(pl.multiple_of(8 * i + 8, 8), 8), :]
-            low.append(a)
-            high.append(jnp.where(row < 4, pltpu.roll(a, 4, 0), pltpu.roll(b, 4, 0)))
-        out[2 * i] = jnp.concatenate(low, axis=0).astype(jnp.bfloat16)
-        out[2 * i + 1] = jnp.concatenate(high, axis=0).astype(jnp.bfloat16)
+            slots[slot] = jnp.where((hits > 0) & (found == first_slot + slot), i, slots[slot])
+        found = found + hits
+    copies = []
+    for slot in range(2):
+        copies.append(pltpu.make_async_copy(images.at[slots[slot]], got.at[slot], sems.at[slot]))
+        copies.append(
+            pltpu.make_async_copy(edges.at[slots[slot]], got_edge.at[slot], sems.at[2 + slot])
+        )
+    for copy in copies:
+        copy.start()
+    for copy in copies:
+        copy.wait()
+    for slot in range(2):
+        for j in range(TILES - 1):
+            held[slot, j + column] = got[slot, :, 128 * j : 128 * j + 128].astype(F32)
+        held[slot, (TILES - 1) * (1 - column)] = got_edge[slot].astype(F32)
+
+    row = iota2(0)
+
+    def one_slab(i, carry):
+        window = pl.ds(offsets[i], 8)
+        parts = []
+        for j in range(TILES):
+            b = pltpu.roll(held[1, j, window, :], 6, 0)
+            a = jnp.where(row < USED, held[0, j, window, :], b)
+            if j % 2 == 0:
+                parts += [a, b]
+            else:
+                middle = pltpu.roll(a, 4, 0)
+                parts[-1] = jnp.where(row < 4, parts[-1], middle)
+                parts.append(jnp.where(row < 4, middle, pltpu.roll(b, 4, 0)))
+        out[i] = jnp.concatenate(parts, axis=0).astype(jnp.bfloat16)
         return carry
 
-    lax.fori_loop(0, out.shape[0] // 2, two_slabs, 0)
-
-
-def pack(place, slots, images, edges, slab_count):
+    lax.fori_loop(0, out.shape[0], one_slab, 0, unroll=2)
+
+
+def pack(first_slot, owners, subsets, offsets, images, edges):
     rows = images.shape[1]
-    spec = pltpu.PrefetchScalarGridSpec(
-        num_scalar_prefetch=2,
-        grid=(1,),
-        in_specs=[
-            pl.BlockSpec((1, rows, 1024), lambda i, p, s: (s[0], 0, 0)),
-            pl.BlockSpec((1, rows, 1024), lambda i, p, s: (s[1], 0, 0)),
-            pl.BlockSpec((1, rows, 128), lambda i, p, s: (s[0], 0, 0)),
-            pl.BlockSpec((1, rows, 128), lambda i, p, s: (s[1], 0, 0)),
+    smem = pl.BlockSpec(memory_space=pltpu.SMEM)
+    hbm = pl.BlockSpec(memory_space=pl.ANY)
+    return pl.pallas_call(
+        functools.partial(pack_kernel, first_slot),
+        in_specs=[smem] * 3 + [hbm] * 2,
+        out_specs=pl.BlockSpec(memory_space=pltpu.VMEM),
+        out_shape=jax.ShapeDtypeStruct((offsets.shape[0], PACKED, 128), jnp.bfloat16),
+        scratch_shapes=[
+            pltpu.VMEM((2, rows, 1024), jnp.bfloat16),
+            pltpu.VMEM((2, rows, 128), jnp.bfloat16),
+            pltpu.VMEM((2, TILES, rows, 128), F32),
+            pltpu.SemaphoreType.DMA((4,)),
         ],
-        out_specs=pl.BlockSpec((slab_count, 16, WIDE), lambda i, p, s: (0, 0, 0)),
-        scratch_shapes=[pltpu.VMEM((2, rows, WIDE), F32)],
-    )
-
-    def kernel(p, s, *refs):
-        pack_kernel(p, *refs)
-
-    return pl.pallas_call(
-        kernel,
-        grid_spec=spec,
-        out_shape=jax.ShapeDtypeStruct((slab_count, 16, WIDE), jnp.bfloat16),
         compiler_params=PARAMS,
         name="pack_images",
-    )(place, slots, images, images, edges, edges)
+    )(owners, subsets, offsets, images, edges)
 
 
 def start_kernel(place, steps, fractions, volume, edge, state, rows_ref, rows16_ref):
@@ -215,14 +230,17 @@
     jax.ShapeDtypeStruct((8 * SUBSET, WIDE), F32),
     jax.ShapeDtypeStruct((8 * SUBSET, WIDE), jnp.bfloat16),
 )
-SLAB = (ZS, TILES, 2, XW, 128)
+HALO = jax.ShapeDtypeStruct((ZS + 1, TILES, 2 * XW, 128), jnp.bfloat16)
+SLAB_OUT = (jax.ShapeDtypeStruct((ZS, TILES, 2, XW, 128), F32), HALO, HALO)
 
 
 def update_kernel(base, place, owner, rank, steps, fractions, *refs):
     images, extra = refs[:SUBSET], refs[SUBSET : 2 * SUBSET]
-    state, own, before, after, out, held, moved_state = refs[2 * SUBSET :]
+    state, own, before, after, out, out_before, out_after, held, moved_state, rows_of = refs[
+        2 * SUBSET :
+    ]
     column, to_before, to_after = place[0], place[1], place[2]
-    has_before, has_after, lift = place[3], place[4], place[5]
+    has_before, has_after = place[3], place[4]
     lane, sub = iota2(1), iota2(0)
     zero = jnp.zeros((8, 128), F32)
     totals = row_weights(0, False) + row_weights(1, False) + row_weights(2, False)
@@ -261,15 +279,13 @@
         edge_sum = lax.fori_loop(0, XW, one_x, zero, unroll=4)
         outer = jnp.maximum(row_total * edge_sum, 1.0)
         slot = rank[base + v]
-        take = 8 * lax.rem(slot, 2) + lift
-        later = (slot >= 2)
+        take = USED * lax.rem(slot, 2)
         turned = []
         if v % 2 == 0:
             pair_before = before[8 * v : 8 * v + 16, :].astype(F32)
             pair_after = after[8 * v : 8 * v + 16, :].astype(F32)
         low = 8 * (v % 2)
-        image = jnp.where(later, extra[v][0].astype(F32), images[v][0].astype(F32))
-        image = pltpu.roll(image, lax.rem(16 - take, 16), 0)[:8]
+        rows_of[v] = jnp.where(slot >= 2, extra[v][0].astype(F32), images[v][0].astype(F32))
         for j in range(TILES):
             cols = slice(128 * j, 128 * j + 128)
             predicted = (
@@ -280,7 +296,8 @@
             raysum = inner
             if j == 0 or j == TILES - 1:
                 raysum = jnp.where(edge_tile == j, outer, inner)
-            residual = (image[:, cols] - predicted) / raysum
+            image = rows_of[v, pl.ds(2 * USED * j + take, 8), :]
+            residual = (image - predicted) / raysum
             mixed = back_weights[0] * residual
             for shift in (1, 2):
                 mixed = mixed + back_weights[shift] * pltpu.roll(residual, 8 - shift, 0)
@@ -322,11 +339,19 @@
             moved_state[j, here, :] = state[j, here, :] + (relaxation / SUBSET) * totals_x[j]
         return carry
 
-    lax.fori_loop(0, XW, back_x, 0)
+    lax.fori_loop(0, XW, back_x, 0, unroll=BACK_UNROLL)
     for j in range(TILES):
         for z in range(ZS):
+            pair = [moved_state[j, pl.ds(4 * p + z, XW, stride=8), :] for p in range(2)]
             for p in range(2):
-                out[z, j, p] = moved_state[j, pl.ds(4 * p + z, XW, stride=8), :]
+                out[z, j, p] = pair[p]
+            both = jnp.concatenate(pair, axis=0)
+            high = both.astype(jnp.bfloat16)
+            out_before[z, j] = high
+            out_after[z, j] = high
+            if z in (0, ZS - 1):
+                rest = (both - high.astype(F32)).astype(jnp.bfloat16)
+                (out_before if z == 0 else out_after)[ZS, j] = rest
 
 
 def update(subset, place, owner, rank, steps, fractions, recv, extra, state, own, before, after):
@@ -334,7 +359,7 @@
 
     def of_view(v):
         return pl.BlockSpec(
-            (1, 16, WIDE), lambda i, place, owner, rank, steps, fr: (owner[base + v], 0, 0)
+            (1, PACKED, 128), lambda i, place, owner, rank, steps, fr: (owner[base + v], 0, 0)
         )
 
     def whole(array):
@@ -346,16 +371,17 @@
         grid=(1,),
         in_specs=[of_view(v) for v in range(SUBSET)] * 2
         + [whole(a) for a in (state, own, before, after)],
-        out_specs=pl.BlockSpec(SLAB, lambda i, *scalars: (0,) * 5),
+        out_specs=[whole(a) for a in SLAB_OUT],
         scratch_shapes=[
             pltpu.VMEM((SUBSET, 3, TILES + 1, 8, 128), F32),
             pltpu.VMEM((TILES, 8 * XW, 128), F32),
+            pltpu.VMEM((SUBSET, PACKED, 128), F32),
         ],
     )
     return pl.pallas_call(
         functools.partial(update_kernel, base),
         grid_spec=spec,
-        out_shape=jax.ShapeDtypeStruct(SLAB, F32),
+        out_shape=SLAB_OUT,
         compiler_params=PARAMS,
         name="residual_back",
     )(
@@ -365,7 +391,15 @@
 
 
 def smooth(own, before, after, buffers, along, in_before, in_after, store):
-    sources = (before, own, after)
+    def first(z, j):
+        if ZS <= z < 2 * ZS:
+            return [own[z - ZS, j, p] for p in range(2)]
+        side = before if z < ZS else after
+        both = side[z % ZS, j].astype(F32)
+        if z in (ZS - 1, 2 * ZS):
+            both = both + side[ZS, j].astype(F32)
+        return [both[:XW], both[XW:]]
+
     row24 = lax.broadcasted_iota(jnp.int32, (XW, 128), 0)
     lane24 = lax.broadcasted_iota(jnp.int32, (XW, 128), 1)
     zero = jnp.zeros((XW, 128), F32)
@@ -375,10 +409,10 @@
         target = buffers[index % 2]
         source = buffers[(index + 1) % 2]
 
-        def load(z, j, parity, index=index, source=source):
+        def load(z, j, index=index, source=source):
             if index == 0:
-                return sources[z // ZS][z % ZS, j, parity]
-            return source[z, j, parity]
+                return first(z, j)
+            return [source[z, j, p] for p in range(2)]
 
         for z in range(low, high + 1):
             along[z] = zero
@@ -386,11 +420,11 @@
         def one_tile(j, carry, low=low, high=high, last=last, target=target, load=load):
             following = jnp.minimum(j + 1, TILES - 1)
             has_following = j < TILES - 1
-            current = [load(low - 1, j, p) for p in range(2)]
+            current = load(low - 1, j)
             flux_before = None
             for z in range(low - 1, high + 1):
-                above = [load(z + 1, j, p) for p in range(2)]
-                beside = jnp.where(has_following, load(z, following, 0), 0.0)
+                above = load(z + 1, j)
+                beside = jnp.where(has_following, load(z, following)[0], 0.0)
                 next_even = pltpu.roll(
                     jnp.where(lane24 == 0, beside, current[0]), 127, 1
                 )
@@ -491,6 +525,10 @@
     return lax.ppermute(value, "col", [(0, 1), (1, 0)])
 
 
+def fetched(first_slot, *args):
+    return lax.all_to_all(pack(first_slot, *args), "gz", 0, 0)
+
+
 def body(volume, images, owners, subsets, offsets):
     slab_count = lax.axis_size("gz")
     slab = lax.axis_index("gz")
@@ -500,8 +538,10 @@
 
     edge = swap_halves(jnp.where(column == 0, volume[:, :, -256:], volume[:, :, :256]))
     image_edge = swap_halves(jnp.where(column == 0, images[:, :, -128:], images[:, :, :128]))
+    edge, image_edge = lax.optimization_barrier((edge, image_edge))
 
     views = subsets.reshape(-1)
+    recv = fetched(0, owners, views, offsets, images, image_edge)
     positions = jnp.sum(
         jnp.where(
             owners[None, :] == views[:, None], jnp.arange(nviews, dtype=jnp.int32)[None, :], 0
@@ -509,18 +549,10 @@
         axis=1,
     )
     owner = positions // stored
-    count = SUBSETS * SUBSET
-    order = jnp.arange(count)
     rank = jnp.sum(
-        ((owner[None, :] == owner[:, None]) & (order[None, :] < order[:, None])).astype(jnp.int32),
-        axis=1,
-    )
-    slots = jnp.sum(
-        jnp.where(
-            (owner[None, :] == slab) & (rank[None, :] == jnp.arange(4)[:, None]),
-            (positions % stored)[None, :],
-            0,
-        ),
+        (
+            (owner[None, :] == owner[:, None]) & (positions[None, :] < positions[:, None])
+        ).astype(jnp.int32),
         axis=1,
     )
     steps, fractions = view_geometry(views, XW, MARGIN, nviews)
@@ -536,30 +568,24 @@
             own_start - next_start,
             (slab > 0).astype(jnp.int32),
             (slab < slab_count - 1).astype(jnp.int32),
-            own_start - slab * ZS,
         ]
     ).astype(jnp.int32)
 
-    def fetched(two_slots):
-        packed = pack(place, two_slots, images, image_edge, slab_count)
-        return lax.all_to_all(packed, "gz", 0, 0)
-
-    recv = fetched(slots[:2])
+    state, rows, rows16 = scalar_call(
+        start_kernel, (place, steps, fractions), (volume, edge), ROWS_OUT, [], "split_project"
+    )
+    later_edge, recv = lax.optimization_barrier((image_edge, recv))
     extra = lax.cond(
         jnp.max(rank) >= 2,
-        lambda: fetched(slots[2:]),
-        lambda: jnp.zeros((slab_count, 16, WIDE), jnp.bfloat16),
-    )
-
-    state, rows, rows16 = scalar_call(
-        start_kernel, (place, steps, fractions), (volume, edge), ROWS_OUT, [], "split_project"
+        lambda: fetched(2, owners, views, offsets, images, later_edge),
+        lambda: jnp.zeros(recv.shape, recv.dtype),
     )
     for subset in range(SUBSETS):
-        fresh = update(
+        fresh, low_side, high_side = update(
             subset, place, owner, rank, steps, fractions, recv, extra,
             state, rows, to_next(rows16), to_before(rows16),
         )
-        around = (fresh, to_next(fresh), to_before(fresh))
+        around = (fresh, to_next(high_side), to_before(low_side))
         if subset < SUBSETS - 1:
             state, rows, rows16 = scalar_call(
                 smooth_project_kernel, (place, steps, fractions), around, ROWS_OUT,

time: 174 us -> 129 us (0.74)
  the two profiles are of different devices: /device:TPU:32 before, /device:TPU:15 now
where the time goes in v2:
time: 129 us
  waiting for transfers between devices  43.7 us (34%)
  Pallas kernels  38 us (29%)
  starting transfers between devices  34.8 us (27%)
  local copies, waits for them, and re-layouts  5.93 us (5%)
  other arithmetic  3.21 us (2%)
  between operations  3.2 us (2%)
    pallas_call x3, Pallas kernels, scalar_call(): pl.pallas_call(kernel, in_specs=[smem] * len(scalars) + [vmem] * len(arra...  25.2 us
    ppermute x4, waiting for transfers between devices, to_before(): return lax.ppermute(value, 'gz', [(i + 1, i) for i in range(count - 1)])  21.3 us
    ppermute x4, starting transfers between devices, to_next(): return lax.ppermute(value, 'gz', [(i, i + 1) for i in range(count - 1)])  11.8 us
    all_to_all x1, starting transfers between devices, fetched(): return lax.all_to_all(pack(first_slot, *args), 'gz', 0, 0)  11 us
    pallas_call x2, Pallas kernels, update(): pl.pallas_call(functools.partial(update_kernel, base), grid_spec=spec, ou...  10 us
    ppermute x4, starting transfers between devices, to_before(): return lax.ppermute(value, 'gz', [(i + 1, i) for i in range(count - 1)])  8.83 us
    ppermute x4, waiting for transfers between devices, to_next(): return lax.ppermute(value, 'gz', [(i, i + 1) for i in range(count - 1)])  8.48 us
    all_to_all x1, waiting for transfers between devices, fetched(): return lax.all_to_all(pack(first_slot, *args), 'gz', 0, 0)  7.71 us
  transfers between devices with their start and end apart: 11, of which 7 were waited for; matrix products, arithmetic and copies ran while one was open for 4% of the time, Pallas kernels for 4%

profile of v2, /device:TPU:15, one launch (start us, length us, event | category | flops | bytes accessed | tf_op | source)
XLA Modules:
  0.0 128.8 jit_solution(11902903123855622803)
XLA Ops:
  0.0 1.1 slice_select_fusion
  1.1 2.1 %collective-permute-start.1 = (bf16[4,264,128]{2,1,0:T(8,128)(2,1)S(1)}, bf16[4,264,128]{2,1,0:T(8,128)(2,1)S(1)}, u32[]{:S(2)}, u32[]{:S(2)}) collective-permute-start(bf16[4,264,128]{2,1,0:T(8,128)(2,1)S(1)} %slice_select_fusion), channel_id=1, source_target_pairs={{0,1},{1,0},{2,3},{3,2},{4,5},{5,4},{6,7},{7,6},{8,9},{9,8},{10,11... | collective-permute-start | bytes 811016 | tf_op jit(solution)/shard_map/ppermute | solution.py:525
  3.2 1.0 slice_select_fusion.1
  4.1 1.0 collective-permute-start
  5.2 0.8 eq.33.subsets
  5.9 6.2 %collective-permute-done.edge = f32[4,24,256]{2,1,0:T(8,128)S(1)} collective-permute-done((f32[4,24,256]{2,1,0:T(8,128)S(1)}, f32[4,24,256]{2,1,0:T(8,128)S(1)}, u32[]{:S(2)}, u32[]{:S(2)}) %collective-permute-start) | collective-permute-done | bytes 98336 | tf_op jit(solution)/shard_map/ppermute | solution.py:525
  12.1 0.0 copy-start.4
  12.1 0.0 collective-permute-done.1.edges
  12.1 0.0 copy-start.7
  12.1 2.7 %pack_images.3 = bf16[64,112,128]{2,1,0:T(8,128)(2,1)S(1)} custom-call(s32[256]{0:T(256)} %owners.1, s32[12]{0:T(128)S(1)} %eq.33.subsets, s32[64]{0:T(128)} %offsets.1, bf16[4,264,1024]{2,1,0:T(8,128)(2,1)} %images.1, bf16[4,264,128]{2,1,0:T(8,128)(2,1)S(1)} %collective-permute-done.1.edges), custom_call_target="tpu_custom_call" | custom-call | tf_op jit(solution)/shard_map/pack_images/pallas_call | solution.py:177
  14.9 0.0 copy-done.4
  14.9 0.0 copy-done.7
  14.9 0.0 copy-start
  14.9 1.3 copy-done
  16.2 0.0 copy-start.8
  16.2 0.0 copy-start.9
  16.2 0.0 copy-start.1
  16.2 11.0 %all-to-all-start.1 = ((bf16[64,112,128]{2,1,0:T(8,128)(2,1)}), bf16[64,112,128]{2,1,0:T(8,128)(2,1)S(1)}, u32[]{:S(2)}, u32[]{:S(2)}) async-start(bf16[64,112,128]{2,1,0:T(8,128)(2,1)} %copy-done), calls=%async_computation.1 | async-start | bytes 3670016 | tf_op jit(solution)/shard_map/all_to_all | solution.py:529
  27.2 0.0 copy-done.8
  27.2 0.6 fusion
  30.3 0.1 multiply_add_fusion
  30.4 0.1 add.50
  30.4 0.1 stack.25.place
  30.5 0.0 copy-done.9
  30.5 0.2 select_reduce_fusion
  30.7 0.0 copy-done.1
  30.8 0.0 copy-start.5
  30.8 0.9 copy-done.5
  31.7 4.6 %split_project.1 = (f32[9,192,128]{2,1,0:T(8,128)S(1)}, f32[48,1152]{1,0:T(8,128)S(1)}, bf16[48,1152]{1,0:T(8,128)(2,1)}) custom-call(s32[5]{0:T(128)S(1)} %stack.25.place, s32[288]{0:T(512)S(1)} %get-tuple-element.56.steps, f32[288]{0:T(512)S(1)} %get-tuple-element.55.fractions, f32[4,24,2048]{2,1,0:T(8,128)S(1)} %copy-done.1, f32[4,24,256]{2,1,0:T(8,128)S(1)} %copy-done.5), custom_call_target="tpu_custom_call" | custom-call | tf_op jit(solution)/shard_map/split_project/pallas_call | solution.py:217
  36.3 0.0 copy-start.2
  36.3 0.7 copy-done.2
  37.0 3.3 %collective-permute-start.2 = (bf16[48,1152]{1,0:T(8,128)(2,1)}, bf16[48,1152]{1,0:T(8,128)(2,1)S(1)}, u32[]{:S(2)}, u32[]{:S(2)}) collective-permute-start(bf16[48,1152]{1,0:T(8,128)(2,1)} %get-tuple-element.45), channel_id=1, source_target_pairs={{0,2},{2,4},{4,6},{6,8},{8,10},{10,12},{12,14},{14,16},{16,18},{18... | collective-permute-start | bytes 331784 | tf_op jit(solution)/shard_map/ppermute | solution.py:516
  40.3 1.9 %collective-permute-start.3 = (bf16[48,1152]{1,0:T(8,128)(2,1)}, bf16[48,1152]{1,0:T(8,128)(2,1)S(1)}, u32[]{:S(2)}, u32[]{:S(2)}) collective-permute-start(bf16[48,1152]{1,0:T(8,128)(2,1)} %get-tuple-element.45), channel_id=1, source_target_pairs={{2,0},{4,2},{6,4},{8,6},{10,8},{12,10},{14,12},{16,14},{18,16},{20... | collective-permute-start | bytes 331784 | tf_op jit(solution)/shard_map/ppermute | solution.py:521
  42.2 0.2 convert_reduce_fusion.rank
  42.4 0.7 reduce_max.9
  43.7 7.7 %all-to-all-done.1.refs_0_.refs_1_.refs_2_.refs_3_.refs_4_.refs_5_ = bf16[64,112,128]{2,1,0:T(8,128)(2,1)S(1)} async-done(((bf16[64,112,128]{2,1,0:T(8,128)(2,1)}), bf16[64,112,128]{2,1,0:T(8,128)(2,1)S(1)}, u32[]{:S(2)}, u32[]{:S(2)}) %all-to-all-start.1) | async-done | bytes 1835040 | tf_op jit(solution)/shard_map/all_to_all | solution.py:529
  51.4 0.0 copy-start.3
  51.4 1.5 %conditional.1 = (bf16[64,112,128]{2,1,0:T(8,128)(2,1)}) conditional(s32[]{:T(128)} %convert_element_type.25, () %tuple.15, (s32[256]{0:T(256)S(1)}, s32[12]{0:T(128)S(1)}, s32[64]{0:T(128)S(1)}, bf16[4,264,1024]{2,1,0:T(8,128)(2,1)}, bf16[4,264,128]{2,1,0:T(8,128)(2,1)}) %tuple.25), branch_computations={%region_3.4_spmd, %region_4.5_spmd} | conditional | bytes 3670024 | solution.py:578
  51.4 1.5 %broadcast.127 = bf16[64,112,128]{2,1,0:T(8,128)(2,1)} broadcast(bf16[]{:T(256)} %constant.18.clone), dimensions={} | broadcast | bytes 1835010 | tf_op jit(solution)/shard_map/broadcast.13
  52.9 0.0 collective-permute-done.2.refs_14_
  52.9 0.0 collective-permute-done.3.refs_15_
  52.9 0.0 copy-done.3
  52.9 5.4 %residual_back.2 = (f32[4,9,2,24,128]{4,3,2,1,0:T(8,128)S(1)}, bf16[5,9,48,128]{3,2,1,0:T(8,128)(2,1)S(1)}, bf16[5,9,48,128]{3,2,1,0:T(8,128)(2,1)S(1)}) custom-call(s32[5]{0:T(128)S(1)} %stack.25.place, s32[12]{0:T(128)S(1)} %and_select_fusion.owner, s32[12]{0:T(128)S(1)} %convert_reduce_fusion.rank, s32[288]{0:T(512)S(1)} %get-tuple-element.56.steps, ...), custom_call_target="tpu_custom_call" | custom-call | tf_op jit(solution)/shard_map/residual_back/pallas_call | solution.py:381
  58.4 0.0 copy-start.6
  58.4 4.6 %collective-permute-start.4 = (bf16[5,9,48,128]{3,2,1,0:T(8,128)(2,1)S(1)}, bf16[5,9,48,128]{3,2,1,0:T(8,128)(2,1)S(1)}, u32[]{:S(2)}, u32[]{:S(2)}) collective-permute-start(bf16[5,9,48,128]{3,2,1,0:T(8,128)(2,1)S(1)} %get-tuple-element.47), channel_id=1, source_target_pairs={{0,2},{2,4},{4,6},{6,8},{8,10},{10,12},{12,14},{14,16},{16,18},{18... | collective-permute-start | bytes 1658888 | tf_op jit(solution)/shard_map/ppermute | solution.py:516
  63.0 1.9 %collective-permute-start.5 = (bf16[5,9,48,128]{3,2,1,0:T(8,128)(2,1)S(1)}, bf16[5,9,48,128]{3,2,1,0:T(8,128)(2,1)S(1)}, u32[]{:S(2)}, u32[]{:S(2)}) collective-permute-start(bf16[5,9,48,128]{3,2,1,0:T(8,128)(2,1)S(1)} %get-tuple-element.48), channel_id=1, source_target_pairs={{2,0},{4,2},{6,4},{8,6},{10,8},{12,10},{14,12},{16,14},{18,16},{20... | collective-permute-start | bytes 1658888 | tf_op jit(solution)/shard_map/ppermute | solution.py:521
  64.9 4.5 %collective-permute-done.4.before = bf16[5,9,48,128]{3,2,1,0:T(8,128)(2,1)S(1)} collective-permute-done((bf16[5,9,48,128]{3,2,1,0:T(8,128)(2,1)S(1)}, bf16[5,9,48,128]{3,2,1,0:T(8,128)(2,1)S(1)}, u32[]{:S(2)}, u32[]{:S(2)}) %collective-permute-start.4) | collective-permute-done | bytes 552992 | tf_op jit(solution)/shard_map/ppermute | solution.py:516
  69.4 7.4 %collective-permute-done.5.after = bf16[5,9,48,128]{3,2,1,0:T(8,128)(2,1)S(1)} collective-permute-done((bf16[5,9,48,128]{3,2,1,0:T(8,128)(2,1)S(1)}, bf16[5,9,48,128]{3,2,1,0:T(8,128)(2,1)S(1)}, u32[]{:S(2)}, u32[]{:S(2)}) %collective-permute-start.5) | collective-permute-done | bytes 552992 | tf_op jit(solution)/shard_map/ppermute | solution.py:521
  76.8 10.5 %smooth_project.1 = (f32[9,192,128]{2,1,0:T(8,128)S(1)}, f32[48,1152]{1,0:T(8,128)S(1)}, bf16[48,1152]{1,0:T(8,128)(2,1)S(1)}) custom-call(s32[5]{0:T(128)S(1)} %stack.25.place, s32[288]{0:T(512)S(1)} %get-tuple-element.56.steps, f32[288]{0:T(512)S(1)} %get-tuple-element.55.fractions, f32[4,9,2,24,128]{4,3,2,1,0:T(8,128)S(1)} %get-tuple-element.46.own, ...), custom_call_target="tpu_custom_call" | custom-call | tf_op jit(solution)/shard_map/smooth_project/pallas_call | solution.py:217
  87.3 1.9 %collective-permute-start.6 = (bf16[48,1152]{1,0:T(8,128)(2,1)S(1)}, bf16[48,1152]{1,0:T(8,128)(2,1)S(1)}, u32[]{:S(2)}, u32[]{:S(2)}) collective-permute-start(bf16[48,1152]{1,0:T(8,128)(2,1)S(1)} %get-tuple-element.51), channel_id=1, source_target_pairs={{0,2},{2,4},{4,6},{6,8},{8,10},{10,12},{12,14},{14,16},{16,18},{18... | collective-permute-start | bytes 331784 | tf_op jit(solution)/shard_map/ppermute | solution.py:516
  89.3 2.6 %collective-permute-start.7 = (bf16[48,1152]{1,0:T(8,128)(2,1)S(1)}, bf16[48,1152]{1,0:T(8,128)(2,1)S(1)}, u32[]{:S(2)}, u32[]{:S(2)}) collective-permute-start(bf16[48,1152]{1,0:T(8,128)(2,1)S(1)} %get-tuple-element.51), channel_id=1, source_target_pairs={{2,0},{4,2},{6,4},{8,6},{10,8},{12,10},{14,12},{16,14},{18,16},{20... | collective-permute-start | bytes 331784 | tf_op jit(solution)/shard_map/ppermute | solution.py:521
  91.9 0.0 collective-permute-done.6.refs_14_
  91.9 6.5 %collective-permute-done.7.refs_15_ = bf16[48,1152]{1,0:T(8,128)(2,1)S(1)} collective-permute-done((bf16[48,1152]{1,0:T(8,128)(2,1)S(1)}, bf16[48,1152]{1,0:T(8,128)(2,1)S(1)}, u32[]{:S(2)}, u32[]{:S(2)}) %collective-permute-start.7) | collective-permute-done | bytes 110624 | tf_op jit(solution)/shard_map/ppermute | solution.py:521
  98.3 0.0 copy-done.6
  98.3 4.6 %residual_back.3 = (f32[4,9,2,24,128]{4,3,2,1,0:T(8,128)S(1)}, bf16[5,9,48,128]{3,2,1,0:T(8,128)(2,1)S(1)}, bf16[5,9,48,128]{3,2,1,0:T(8,128)(2,1)S(1)}) custom-call(s32[5]{0:T(128)S(1)} %stack.25.place, s32[12]{0:T(128)S(1)} %and_select_fusion.owner, s32[12]{0:T(128)S(1)} %convert_reduce_fusion.rank, s32[288]{0:T(512)S(1)} %get-tuple-element.56.steps, ...), custom_call_target="tpu_custom_call" | custom-call | tf_op jit(solution)/shard_map/residual_back/pallas_call | solution.py:381
  103.0 1.9 %collective-permute-start.8 = (bf16[5,9,48,128]{3,2,1,0:T(8,128)(2,1)S(1)}, bf16[5,9,48,128]{3,2,1,0:T(8,128)(2,1)S(1)}, u32[]{:S(2)}, u32[]{:S(2)}) collective-permute-start(bf16[5,9,48,128]{3,2,1,0:T(8,128)(2,1)S(1)} %get-tuple-element.53), channel_id=1, source_target_pairs={{0,2},{2,4},{4,6},{6,8},{8,10},{10,12},{12,14},{14,16},{16,18},{18... | collective-permute-start | bytes 1658888 | tf_op jit(solution)/shard_map/ppermute | solution.py:516
  104.9 2.4 %collective-permute-start.9 = (bf16[5,9,48,128]{3,2,1,0:T(8,128)(2,1)S(1)}, bf16[5,9,48,128]{3,2,1,0:T(8,128)(2,1)S(1)}, u32[]{:S(2)}, u32[]{:S(2)}) collective-permute-start(bf16[5,9,48,128]{3,2,1,0:T(8,128)(2,1)S(1)} %get-tuple-element.54), channel_id=1, source_target_pairs={{2,0},{4,2},{6,4},{8,6},{10,8},{12,10},{14,12},{16,14},{18,16},{20... | collective-permute-start | bytes 1658888 | tf_op jit(solution)/shard_map/ppermute | solution.py:521
  107.3 4.0 %collective-permute-done.8.before = bf16[5,9,48,128]{3,2,1,0:T(8,128)(2,1)S(1)} collective-permute-done((bf16[5,9,48,128]{3,2,1,0:T(8,128)(2,1)S(1)}, bf16[5,9,48,128]{3,2,1,0:T(8,128)(2,1)S(1)}, u32[]{:S(2)}, u32[]{:S(2)}) %collective-permute-start.8) | collective-permute-done | bytes 552992 | tf_op jit(solution)/shard_map/ppermute | solution.py:516
  111.3 7.4 %collective-permute-done.9.after = bf16[5,9,48,128]{3,2,1,0:T(8,128)(2,1)S(1)} collective-permute-done((bf16[5,9,48,128]{3,2,1,0:T(8,128)(2,1)S(1)}, bf16[5,9,48,128]{3,2,1,0:T(8,128)(2,1)S(1)}, u32[]{:S(2)}, u32[]{:S(2)}) %collective-permute-start.9) | collective-permute-done | bytes 552992 | tf_op jit(solution)/shard_map/ppermute | solution.py:521
  118.7 10.1 %smooth_join.1 = f32[4,24,2048]{2,1,0:T(8,128)} custom-call(s32[5]{0:T(128)S(1)} %stack.25.place, f32[4,9,2,24,128]{4,3,2,1,0:T(8,128)S(1)} %get-tuple-element.52.own, bf16[5,9,48,128]{3,2,1,0:T(8,128)(2,1)S(1)} %collective-permute-done.8.before, bf16[5,9,48,128]{3,2,1,0:T(8,128)(2,1)S(1)} %collective-permute-done.9.after), custom_call_target="tpu_custom_call" | custom-call | tf_op jit(solution)/shard_map/smooth_join/pallas_call | solution.py:217
  (4 shorter events, 0.1 us)
Async XLA Ops:
  1.1 11.0 %collective-permute-start.1 = (bf16[4,264,128]{2,1,0:T(8,128)(2,1)S(1)}, bf16[4,264,128]{2,1,0:T(8,128)(2,1)S(1)}, u32[]{:S(2)}, u32[]{:S(2)}) collective-permute-start(bf16[4,264,128]{2,1,0:T(8,128)(2,1)S(1)} %slice_select_fusion), channel_id=1, source_target_pairs={{0,1},{1,0},{2,3},{3,2},{4,5},{5,4},{6,7},{7,6},{8,9},{9,8},{10,11... | collective-permute-start | bytes 811016 | tf_op jit(solution)/shard_map/ppermute | solution.py:525
  4.1 8.0 %collective-permute-start = (f32[4,24,256]{2,1,0:T(8,128)S(1)}, f32[4,24,256]{2,1,0:T(8,128)S(1)}, u32[]{:S(2)}, u32[]{:S(2)}) collective-permute-start(f32[4,24,256]{2,1,0:T(8,128)S(1)} %slice_select_fusion.1), channel_id=1, source_target_pairs={{0,1},{1,0},{2,3},{3,2},{4,5},{5,4},{6,7},{7,6},{8,9},{9,8},{10,11... | collective-permute-start | bytes 294920 | tf_op jit(solution)/shard_map/ppermute | solution.py:525
  12.1 2.8 %copy-start.4 = (f32[4,24,256]{2,1,0:T(8,128)}, f32[4,24,256]{2,1,0:T(8,128)S(1)}, u32[]{:S(2)}) copy-start(f32[4,24,256]{2,1,0:T(8,128)S(1)} %collective-permute-done.edge) | copy-start | bytes 294916
  12.1 2.8 %copy-start.7 = (bf16[4,264,128]{2,1,0:T(8,128)(2,1)}, bf16[4,264,128]{2,1,0:T(8,128)(2,1)S(1)}, u32[]{:S(2)}) copy-start(bf16[4,264,128]{2,1,0:T(8,128)(2,1)S(1)} %collective-permute-done.1.edges) | copy-start | bytes 811012
  14.9 1.3 copy-start
  16.2 11.1 %copy-start.8 = (s32[64]{0:T(128)S(1)}, s32[64]{0:T(128)}, u32[]{:S(2)}) copy-start(s32[64]{0:T(128)} %offsets.1) | copy-start | bytes 772
  16.2 14.4 %copy-start.9 = (s32[256]{0:T(256)S(1)}, s32[256]{0:T(256)}, u32[]{:S(2)}) copy-start(s32[256]{0:T(256)} %owners.1) | copy-start | bytes 3076
  16.2 14.6 %copy-start.1 = (f32[4,24,2048]{2,1,0:T(8,128)S(1)}, f32[4,24,2048]{2,1,0:T(8,128)}, u32[]{:S(2)}) copy-start(f32[4,24,2048]{2,1,0:T(8,128)} %volume.1) | copy-start | bytes 2359300
  16.2 35.2 %all-to-all-start.1 = ((bf16[64,112,128]{2,1,0:T(8,128)(2,1)}), bf16[64,112,128]{2,1,0:T(8,128)(2,1)S(1)}, u32[]{:S(2)}, u32[]{:S(2)}) async-start(bf16[64,112,128]{2,1,0:T(8,128)(2,1)} %copy-done), calls=%async_computation.1 | async-start | bytes 3670016 | tf_op jit(solution)/shard_map/all_to_all | solution.py:529
  30.8 0.9 copy-start.5
  36.3 0.7 copy-start.2
  37.0 16.0 %collective-permute-start.2 = (bf16[48,1152]{1,0:T(8,128)(2,1)}, bf16[48,1152]{1,0:T(8,128)(2,1)S(1)}, u32[]{:S(2)}, u32[]{:S(2)}) collective-permute-start(bf16[48,1152]{1,0:T(8,128)(2,1)} %get-tuple-element.45), channel_id=1, source_target_pairs={{0,2},{2,4},{4,6},{6,8},{8,10},{10,12},{12,14},{14,16},{16,18},{18... | collective-permute-start | bytes 331784 | tf_op jit(solution)/shard_map/ppermute | solution.py:516
  40.3 12.6 %collective-permute-start.3 = (bf16[48,1152]{1,0:T(8,128)(2,1)}, bf16[48,1152]{1,0:T(8,128)(2,1)S(1)}, u32[]{:S(2)}, u32[]{:S(2)}) collective-permute-start(bf16[48,1152]{1,0:T(8,128)(2,1)} %get-tuple-element.45), channel_id=1, source_target_pairs={{2,0},{4,2},{6,4},{8,6},{10,8},{12,10},{14,12},{16,14},{18,16},{20... | collective-permute-start | bytes 331784 | tf_op jit(solution)/shard_map/ppermute | solution.py:521
  51.4 1.5 %copy-start.3 = (f32[48,1152]{1,0:T(8,128)S(1)}, f32[48,1152]{1,0:T(8,128)}, u32[]{:S(2)}) copy-start(f32[48,1152]{1,0:T(8,128)} %copy-done.2) | copy-start | bytes 663556
  58.4 40.0 %copy-start.6 = (bf16[64,112,128]{2,1,0:T(8,128)(2,1)S(1)}, bf16[64,112,128]{2,1,0:T(8,128)(2,1)}, u32[]{:S(2)}) copy-start(bf16[64,112,128]{2,1,0:T(8,128)(2,1)} %get-tuple-element.62.refs_6_.refs_7_.refs_8_.refs_9_.refs_10_.refs_11_) | copy-start | bytes 5505028
  58.4 11.0 %collective-permute-start.4 = (bf16[5,9,48,128]{3,2,1,0:T(8,128)(2,1)S(1)}, bf16[5,9,48,128]{3,2,1,0:T(8,128)(2,1)S(1)}, u32[]{:S(2)}, u32[]{:S(2)}) collective-permute-start(bf16[5,9,48,128]{3,2,1,0:T(8,128)(2,1)S(1)} %get-tuple-element.47), channel_id=1, source_target_pairs={{0,2},{2,4},{4,6},{6,8},{8,10},{10,12},{12,14},{14,16},{16,18},{18... | collective-permute-start | bytes 1658888 | tf_op jit(solution)/shard_map/ppermute | solution.py:516
  63.0 13.8 %collective-permute-start.5 = (bf16[5,9,48,128]{3,2,1,0:T(8,128)(2,1)S(1)}, bf16[5,9,48,128]{3,2,1,0:T(8,128)(2,1)S(1)}, u32[]{:S(2)}, u32[]{:S(2)}) collective-permute-start(bf16[5,9,48,128]{3,2,1,0:T(8,128)(2,1)S(1)} %get-tuple-element.48), channel_id=1, source_target_pairs={{2,0},{4,2},{6,4},{8,6},{10,8},{12,10},{14,12},{16,14},{18,16},{20... | collective-permute-start | bytes 1658888 | tf_op jit(solution)/shard_map/ppermute | solution.py:521
  87.3 4.5 %collective-permute-start.6 = (bf16[48,1152]{1,0:T(8,128)(2,1)S(1)}, bf16[48,1152]{1,0:T(8,128)(2,1)S(1)}, u32[]{:S(2)}, u32[]{:S(2)}) collective-permute-start(bf16[48,1152]{1,0:T(8,128)(2,1)S(1)} %get-tuple-element.51), channel_id=1, source_target_pairs={{0,2},{2,4},{4,6},{6,8},{8,10},{10,12},{12,14},{14,16},{16,18},{18... | collective-permute-start | bytes 331784 | tf_op jit(solution)/shard_map/ppermute | solution.py:516
  89.3 9.1 %collective-permute-start.7 = (bf16[48,1152]{1,0:T(8,128)(2,1)S(1)}, bf16[48,1152]{1,0:T(8,128)(2,1)S(1)}, u32[]{:S(2)}, u32[]{:S(2)}) collective-permute-start(bf16[48,1152]{1,0:T(8,128)(2,1)S(1)} %get-tuple-element.51), channel_id=1, source_target_pairs={{2,0},{4,2},{6,4},{8,6},{10,8},{12,10},{14,12},{16,14},{18,16},{20... | collective-permute-start | bytes 331784 | tf_op jit(solution)/shard_map/ppermute | solution.py:521
  103.0 8.3 %collective-permute-start.8 = (bf16[5,9,48,128]{3,2,1,0:T(8,128)(2,1)S(1)}, bf16[5,9,48,128]{3,2,1,0:T(8,128)(2,1)S(1)}, u32[]{:S(2)}, u32[]{:S(2)}) collective-permute-start(bf16[5,9,48,128]{3,2,1,0:T(8,128)(2,1)S(1)} %get-tuple-element.53), channel_id=1, source_target_pairs={{0,2},{2,4},{4,6},{6,8},{8,10},{10,12},{12,14},{14,16},{16,18},{18... | collective-permute-start | bytes 1658888 | tf_op jit(solution)/shard_map/ppermute | solution.py:516
  104.9 13.8 %collective-permute-start.9 = (bf16[5,9,48,128]{3,2,1,0:T(8,128)(2,1)S(1)}, bf16[5,9,48,128]{3,2,1,0:T(8,128)(2,1)S(1)}, u32[]{:S(2)}, u32[]{:S(2)}) collective-permute-start(bf16[5,9,48,128]{3,2,1,0:T(8,128)(2,1)S(1)} %get-tuple-element.54), channel_id=1, source_target_pairs={{2,0},{4,2},{6,4},{8,6},{10,8},{12,10},{14,12},{16,14},{18,16},{20... | collective-permute-start | bytes 1658888 | tf_op jit(solution)/shard_map/ppermute | solution.py:521

commit v3 on v2

--- a/solution.py
+++ b/solution.py
@@ -21,7 +21,9 @@
 TILES = 9
 WIDE = TILES * 128
 USED = 6
-PACKED = 112
+OWN = TILES - 1
+PACKED = 2 * USED * OWN
+CHUNKS = 4
 HIGHEST = lax.Precision.HIGHEST
 PARAMS = pltpu.CompilerParams(vmem_limit_bytes=48 * 1024 * 1024)
 F32 = jnp.float32
@@ -121,9 +123,10 @@
                 )
 
 
-def pack_kernel(first_slot, owners, subsets, offsets, images, edges, out, got, got_edge, held, sems):
-    slab, column = lax.axis_index("gz"), lax.axis_index("col")
+def pack_kernel(first_slot, owners, subsets, offsets, images, out, got, held, ready, sems, out_sems):
+    slab = lax.axis_index("gz")
     stored = images.shape[0]
+    slab_count = out.shape[0]
     count = subsets.shape[0]
     found = jnp.int32(0)
     slots = [jnp.int32(0), jnp.int32(0)]
@@ -135,27 +138,23 @@
         for slot in range(2):
             slots[slot] = jnp.where((hits > 0) & (found == first_slot + slot), i, slots[slot])
         found = found + hits
-    copies = []
-    for slot in range(2):
-        copies.append(pltpu.make_async_copy(images.at[slots[slot]], got.at[slot], sems.at[slot]))
-        copies.append(
-            pltpu.make_async_copy(edges.at[slots[slot]], got_edge.at[slot], sems.at[2 + slot])
-        )
+    copies = [
+        pltpu.make_async_copy(images.at[slots[slot]], got.at[slot], sems.at[slot])
+        for slot in range(2)
+    ]
     for copy in copies:
         copy.start()
-    for copy in copies:
+    for slot, copy in enumerate(copies):
         copy.wait()
-    for slot in range(2):
-        for j in range(TILES - 1):
-            held[slot, j + column] = got[slot, :, 128 * j : 128 * j + 128].astype(F32)
-        held[slot, (TILES - 1) * (1 - column)] = got_edge[slot].astype(F32)
+        for j in range(OWN):
+            held[slot, j] = got[slot, :, 128 * j : 128 * j + 128].astype(F32)
 
     row = iota2(0)
 
     def one_slab(i, carry):
         window = pl.ds(offsets[i], 8)
         parts = []
-        for j in range(TILES):
+        for j in range(OWN):
             b = pltpu.roll(held[1, j, window, :], 6, 0)
             a = jnp.where(row < USED, held[0, j, window, :], b)
             if j % 2 == 0:
@@ -164,30 +163,74 @@
                 middle = pltpu.roll(a, 4, 0)
                 parts[-1] = jnp.where(row < 4, parts[-1], middle)
                 parts.append(jnp.where(row < 4, middle, pltpu.roll(b, 4, 0)))
-        out[i] = jnp.concatenate(parts, axis=0).astype(jnp.bfloat16)
+        ready[i] = jnp.concatenate(parts, axis=0).astype(jnp.bfloat16)
         return carry
 
-    lax.fori_loop(0, out.shape[0], one_slab, 0, unroll=2)
-
-
-def pack(first_slot, owners, subsets, offsets, images, edges):
+    chunk = slab_count // CHUNKS
+    sent = []
+    for part in range(CHUNKS):
+        lax.fori_loop(part * chunk, part * chunk + chunk, one_slab, 0, unroll=2)
+        here = pl.ds(part * chunk, chunk)
+        sent.append(pltpu.make_async_copy(ready.at[here], out.at[here], out_sems.at[part]))
+        sent[-1].start()
+    for copy in sent:
+        copy.wait()
+
+
+def pack(first_slot, owners, subsets, offsets, images):
     rows = images.shape[1]
     smem = pl.BlockSpec(memory_space=pltpu.SMEM)
     hbm = pl.BlockSpec(memory_space=pl.ANY)
+    shape = (offsets.shape[0], PACKED, 128)
     return pl.pallas_call(
         functools.partial(pack_kernel, first_slot),
-        in_specs=[smem] * 3 + [hbm] * 2,
-        out_specs=pl.BlockSpec(memory_space=pltpu.VMEM),
-        out_shape=jax.ShapeDtypeStruct((offsets.shape[0], PACKED, 128), jnp.bfloat16),
+        in_specs=[smem] * 3 + [hbm],
+        out_specs=hbm,
+        out_shape=jax.ShapeDtypeStruct(shape, jnp.bfloat16),
         scratch_shapes=[
-            pltpu.VMEM((2, rows, 1024), jnp.bfloat16),
-            pltpu.VMEM((2, rows, 128), jnp.bfloat16),
-            pltpu.VMEM((2, TILES, rows, 128), F32),
-            pltpu.SemaphoreType.DMA((4,)),
+            pltpu.VMEM((2, rows, 128 * OWN), jnp.bfloat16),
+            pltpu.VMEM((2, OWN, rows, 128), F32),
+            pltpu.VMEM(shape, jnp.bfloat16),
+            pltpu.SemaphoreType.DMA((2,)),
+            pltpu.SemaphoreType.DMA((CHUNKS,)),
         ],
         compiler_params=PARAMS,
         name="pack_images",
-    )(owners, subsets, offsets, images, edges)
+    )(owners, subsets, offsets, images)
+
+
+def edge_kernel(place, owner, rank, *refs):
+    count = len(refs) // 2
+    out = refs[-1]
+    for v in range(count):
+        out[v] = jnp.where(rank[v] >= 2, refs[count + v][0].astype(F32), refs[v][0].astype(F32)).astype(
+            jnp.bfloat16
+        )
+
+
+def inner_edges(place, owner, rank, recv, extra):
+    count = owner.shape[0]
+    last = PACKED // 16 - 1
+
+    def of_view(v, direct):
+        def index(i, place, owner, rank):
+            return (v if direct else owner[v], last * (1 - place[0]), 0)
+
+        return pl.BlockSpec((1, 16, 128), index)
+
+    spec = pltpu.PrefetchScalarGridSpec(
+        num_scalar_prefetch=3,
+        grid=(1,),
+        in_specs=[of_view(v, False) for v in range(count)] + [of_view(v, True) for v in range(count)],
+        out_specs=pl.BlockSpec((count, 16, 128), lambda i, *scalars: (0, 0, 0)),
+    )
+    return pl.pallas_call(
+        edge_kernel,
+        grid_spec=spec,
+        out_shape=jax.ShapeDtypeStruct((count, 16, 128), jnp.bfloat16),
+        compiler_params=PARAMS,
+        name="inner_edges",
+    )(place, owner, rank, *([recv] * count), *([extra] * count))
 
 
 def start_kernel(place, steps, fractions, volume, edge, state, rows_ref, rows16_ref):
@@ -236,9 +279,8 @@
 
 def update_kernel(base, place, owner, rank, steps, fractions, *refs):
     images, extra = refs[:SUBSET], refs[SUBSET : 2 * SUBSET]
-    state, own, before, after, out, out_before, out_after, held, moved_state, rows_of = refs[
-        2 * SUBSET :
-    ]
+    state, own, before, after, edges, out, out_before, out_after = refs[2 * SUBSET :][:8]
+    held, moved_state, packed, packed_edge, rows_of = refs[2 * SUBSET :][8:]
     column, to_before, to_after = place[0], place[1], place[2]
     has_before, has_after = place[3], place[4]
     lane, sub = iota2(1), iota2(0)
@@ -285,7 +327,13 @@
             pair_before = before[8 * v : 8 * v + 16, :].astype(F32)
             pair_after = after[8 * v : 8 * v + 16, :].astype(F32)
         low = 8 * (v % 2)
-        rows_of[v] = jnp.where(slot >= 2, extra[v][0].astype(F32), images[v][0].astype(F32))
+        packed[v, :PACKED] = jnp.where(
+            slot >= 2, extra[v][0].astype(F32), images[v][0].astype(F32)
+        )
+        packed_edge[v, :16] = edges[base + v].astype(F32)
+        for j in range(OWN):
+            rows_of[v, j + column] = packed[v, pl.ds(2 * USED * j + take, 8), :]
+        rows_of[v, OWN * (1 - column)] = packed_edge[v, pl.ds(4 * column + take, 8), :]
         for j in range(TILES):
             cols = slice(128 * j, 128 * j + 128)
             predicted = (
@@ -296,8 +344,7 @@
             raysum = inner
             if j == 0 or j == TILES - 1:
                 raysum = jnp.where(edge_tile == j, outer, inner)
-            image = rows_of[v, pl.ds(2 * USED * j + take, 8), :]
-            residual = (image - predicted) / raysum
+            residual = jnp.where(sub < USED, (rows_of[v, j] - predicted) / raysum, 0.0)
             mixed = back_weights[0] * residual
             for shift in (1, 2):
                 mixed = mixed + back_weights[shift] * pltpu.roll(residual, 8 - shift, 0)
@@ -354,13 +401,14 @@
                 (out_before if z == 0 else out_after)[ZS, j] = rest
 
 
-def update(subset, place, owner, rank, steps, fractions, recv, extra, state, own, before, after):
+def update(subset, place, owner, rank, steps, fractions, recv, extra, state, own, before, after, edges):
     base = subset * SUBSET
 
-    def of_view(v):
-        return pl.BlockSpec(
-            (1, PACKED, 128), lambda i, place, owner, rank, steps, fr: (owner[base + v], 0, 0)
-        )
+    def of_view(v, direct):
+        def index(i, place, owner, rank, steps, fractions):
+            return (base + v if direct else owner[base + v], 0, 0)
+
+        return pl.BlockSpec((1, PACKED, 128), index)
 
     def whole(array):
         rank_of = array.ndim
@@ -369,13 +417,16 @@
     spec = pltpu.PrefetchScalarGridSpec(
         num_scalar_prefetch=5,
         grid=(1,),
-        in_specs=[of_view(v) for v in range(SUBSET)] * 2
-        + [whole(a) for a in (state, own, before, after)],
+        in_specs=[of_view(v, False) for v in range(SUBSET)]
+        + [of_view(v, True) for v in range(SUBSET)]
+        + [whole(a) for a in (state, own, before, after, edges)],
         out_specs=[whole(a) for a in SLAB_OUT],
         scratch_shapes=[
             pltpu.VMEM((SUBSET, 3, TILES + 1, 8, 128), F32),
             pltpu.VMEM((TILES, 8 * XW, 128), F32),
-            pltpu.VMEM((SUBSET, PACKED, 128), F32),
+            pltpu.VMEM((SUBSET, PACKED + 8, 128), F32),
+            pltpu.VMEM((SUBSET, 24, 128), F32),
+            pltpu.VMEM((SUBSET, TILES, 8, 128), F32),
         ],
     )
     return pl.pallas_call(
@@ -386,7 +437,7 @@
         name="residual_back",
     )(
         place, owner, rank, steps, fractions,
-        *([recv] * SUBSET), *([extra] * SUBSET), state, own, before, after,
+        *([recv] * SUBSET), *([extra] * SUBSET), state, own, before, after, edges,
     )
 
 
@@ -525,10 +576,6 @@
     return lax.ppermute(value, "col", [(0, 1), (1, 0)])
 
 
-def fetched(first_slot, *args):
-    return lax.all_to_all(pack(first_slot, *args), "gz", 0, 0)
-
-
 def body(volume, images, owners, subsets, offsets):
     slab_count = lax.axis_size("gz")
     slab = lax.axis_index("gz")
@@ -537,11 +584,11 @@
     nviews = owners.shape[0]
 
     edge = swap_halves(jnp.where(column == 0, volume[:, :, -256:], volume[:, :, :256]))
-    image_edge = swap_halves(jnp.where(column == 0, images[:, :, -128:], images[:, :, :128]))
-    edge, image_edge = lax.optimization_barrier((edge, image_edge))
-
     views = subsets.reshape(-1)
-    recv = fetched(0, owners, views, offsets, images, image_edge)
+    packed = pack(0, owners, views, offsets, images)
+    packed, edge = lax.optimization_barrier((packed, edge))
+    recv = lax.all_to_all(packed, "gz", 0, 0)
+
     positions = jnp.sum(
         jnp.where(
             owners[None, :] == views[:, None], jnp.arange(nviews, dtype=jnp.int32)[None, :], 0
@@ -574,16 +621,22 @@
     state, rows, rows16 = scalar_call(
         start_kernel, (place, steps, fractions), (volume, edge), ROWS_OUT, [], "split_project"
     )
-    later_edge, recv = lax.optimization_barrier((image_edge, recv))
+    later_images, recv = lax.optimization_barrier((images, recv))
+
+    def fetch_more():
+        more = lax.all_to_all(pack(2, owners, views, offsets, later_images), "gz", 0, 0)
+        return more[owner]
+
     extra = lax.cond(
         jnp.max(rank) >= 2,
-        lambda: fetched(2, owners, views, offsets, images, later_edge),
-        lambda: jnp.zeros(recv.shape, recv.dtype),
-    )
+        fetch_more,
+        lambda: jnp.zeros((views.shape[0],) + recv.shape[1:], recv.dtype),
+    )
+    edges = swap_halves(inner_edges(place, owner, rank, recv, extra))
     for subset in range(SUBSETS):
         fresh, low_side, high_side = update(
             subset, place, owner, rank, steps, fractions, recv, extra,
-            state, rows, to_next(rows16), to_before(rows16),
+            state, rows, to_next(rows16), to_before(rows16), edges,
         )
         around = (fresh, to_next(high_side), to_before(low_side))
         if subset < SUBSETS - 1:

time: 129 us -> 126 us (0.977)
  waiting for transfers between devices: 43.7 us -> 30 us
  starting transfers between devices: 34.8 us -> 48.3 us
  local copies, waits for them, and re-layouts: 5.93 us -> 3.18 us
    ppermute x4, starting transfers between devices: 11.8 us -> 26.2 us  [to_next(): return lax.ppermute(value, 'gz', [(i, i + 1) for i in range(count - 1)])]
    ppermute x4, waiting for transfers between devices: 21.3 us -> 15.1 us  [to_before(): return lax.ppermute(value, 'gz', [(i + 1, i) for i in range(count - 1)])]
    all_to_all x1, waiting for transfers between devices: 7.71 us -> 1.86 us  [body(): recv = lax.all_to_all(packed, 'gz', 0, 0)]
    ppermute x2, waiting for transfers between devices: 6.2 us -> 2.83 us  [swap_halves(): return lax.ppermute(value, 'col', [(0, 1), (1, 0)])]
    ppermute x4, waiting for transfers between devices: 8.48 us -> 10.2 us  [to_next(): return lax.ppermute(value, 'gz', [(i, i + 1) for i in range(count - 1)])]
    another operation x1, local copies, waits for them, and re-layouts: 1.51 us -> 0.04 us
    unnamed x20 -> x10, local copies, waits for them, and re-layouts: 2.86 us -> 1.54 us
  transfers between devices with their start and end apart: 11 -> 11, of which waited for: 7 -> 8; matrix products, arithmetic and copies ran while one was open for 4% -> 2% of each run, Pallas kernels for 4% -> 7%
where the time goes in v3:
time: 126 us
  starting transfers between devices  48.3 us (38%)
  Pallas kernels  38.6 us (31%)
  waiting for transfers between devices  30 us (24%)
  between operations  3.43 us (3%)
  local copies, waits for them, and re-layouts  3.18 us (3%)
  other arithmetic  2.17 us (2%)
    ppermute x4, starting transfers between devices, to_next(): return lax.ppermute(value, 'gz', [(i, i + 1) for i in range(count - 1)])  26.2 us
    pallas_call x3, Pallas kernels, scalar_call(): pl.pallas_call(kernel, in_specs=[smem] * len(scalars) + [vmem] * len(arra...  25.3 us
    ppermute x4, waiting for transfers between devices, to_before(): return lax.ppermute(value, 'gz', [(i + 1, i) for i in range(count - 1)])  15.1 us
    all_to_all x1, starting transfers between devices, body(): recv = lax.all_to_all(packed, 'gz', 0, 0)  10.3 us
    ppermute x4, waiting for transfers between devices, to_next(): return lax.ppermute(value, 'gz', [(i, i + 1) for i in range(count - 1)])  10.2 us
    pallas_call x2, Pallas kernels, update(): pl.pallas_call(functools.partial(update_kernel, base), grid_spec=spec, ou...  9.24 us
    ppermute x4, starting transfers between devices, to_before(): return lax.ppermute(value, 'gz', [(i + 1, i) for i in range(count - 1)])  8.02 us
    ppermute x2, starting transfers between devices, swap_halves(): return lax.ppermute(value, 'col', [(0, 1), (1, 0)])  3.79 us
  transfers between devices with their start and end apart: 11, of which 8 were waited for; matrix products, arithmetic and copies ran while one was open for 2% of the time, Pallas kernels for 7%

profile of v3, /device:TPU:15, one launch (start us, length us, event | category | flops | bytes accessed | tf_op | source)
XLA Modules:
  0.0 125.7 jit_solution(183314966768750347)
XLA Ops:
  0.0 1.0 slice_select_fusion
  1.0 2.1 %collective-permute-start = (f32[4,24,256]{2,1,0:T(8,128)S(1)}, f32[4,24,256]{2,1,0:T(8,128)S(1)}, u32[]{:S(2)}, u32[]{:S(2)}) collective-permute-start(f32[4,24,256]{2,1,0:T(8,128)S(1)} %slice_select_fusion), channel_id=1, source_target_pairs={{0,1},{1,0},{2,3},{3,2},{4,5},{5,4},{6,7},{7,6},{8,9},{9,8},{10,11... | collective-permute-start | bytes 294920 | tf_op jit(solution)/shard_map/ppermute | solution.py:576
  3.1 0.8 eq.32.subsets
  3.8 3.4 %pack_images.3 = bf16[64,96,128]{2,1,0:T(8,128)(2,1)} custom-call(s32[256]{0:T(256)} %owners.1, s32[12]{0:T(128)S(1)} %eq.32.subsets, s32[64]{0:T(128)} %offsets.1, bf16[4,264,1024]{2,1,0:T(8,128)(2,1)} %images.1), custom_call_target="tpu_custom_call" | custom-call | tf_op jit(solution)/shard_map/pack_images/pallas_call | solution.py:185
  7.2 0.0 copy-start.3
  7.2 0.0 copy-start.4
  7.3 0.0 copy-start
  7.3 0.0 collective-permute-done.edge
  7.3 0.0 copy-start.1
  7.3 0.6 copy-done.1
  7.9 10.3 %all-to-all-start.1 = ((bf16[64,96,128]{2,1,0:T(8,128)(2,1)}), bf16[64,96,128]{2,1,0:T(8,128)(2,1)S(1)}, u32[]{:S(2)}, u32[]{:S(2)}) async-start(bf16[64,96,128]{2,1,0:T(8,128)(2,1)} %pack_images.3), calls=%async_computation.1 | async-start | bytes 3145728 | tf_op jit(solution)/shard_map/all_to_all | solution.py:590
  18.2 0.0 copy-done.3
  18.3 0.7 fusion
  21.5 0.1 multiply_add_fusion
  21.6 0.1 add.53
  21.7 0.1 stack.25.place
  21.8 0.0 copy-done.4
  21.8 0.2 select_reduce_fusion
  22.0 0.0 copy-done
  22.0 0.0 copy-start.2
  22.0 0.9 copy-done.2
  22.9 4.7 %split_project.1 = (f32[9,192,128]{2,1,0:T(8,128)S(1)}, f32[48,1152]{1,0:T(8,128)S(1)}, bf16[48,1152]{1,0:T(8,128)(2,1)}) custom-call(s32[5]{0:T(128)S(1)} %stack.25.place, s32[288]{0:T(512)S(1)} %get-tuple-element.56.steps, f32[288]{0:T(512)S(1)} %get-tuple-element.55.fractions, f32[4,24,2048]{2,1,0:T(8,128)S(1)} %copy-done, f32[4,24,256]{2,1,0:T(8,128)S(1)} %copy-done.2), custom_call_target="tpu_custom_call" | custom-call | tf_op jit(solution)/shard_map/split_project/pallas_call | solution.py:260
  27.6 2.3 %collective-permute-start.2 = (bf16[48,1152]{1,0:T(8,128)(2,1)}, bf16[48,1152]{1,0:T(8,128)(2,1)S(1)}, u32[]{:S(2)}, u32[]{:S(2)}) collective-permute-start(bf16[48,1152]{1,0:T(8,128)(2,1)} %get-tuple-element.45), channel_id=1, source_target_pairs={{2,0},{4,2},{6,4},{8,6},{10,8},{12,10},{14,12},{16,14},{18,16},{20... | collective-permute-start | bytes 331784 | tf_op jit(solution)/shard_map/ppermute | solution.py:572
  29.9 6.3 %collective-permute-start.1 = (bf16[48,1152]{1,0:T(8,128)(2,1)}, bf16[48,1152]{1,0:T(8,128)(2,1)S(1)}, u32[]{:S(2)}, u32[]{:S(2)}) collective-permute-start(bf16[48,1152]{1,0:T(8,128)(2,1)} %get-tuple-element.45), channel_id=1, source_target_pairs={{0,2},{2,4},{4,6},{6,8},{8,10},{10,12},{12,14},{14,16},{16,18},{18... | collective-permute-start | bytes 331784 | tf_op jit(solution)/shard_map/ppermute | solution.py:567
  36.2 0.2 convert_reduce_fusion.rank
  36.4 0.7 reduce_max.9
  37.8 1.9 %all-to-all-done.1.refs_0_.refs_1_.refs_2_.refs_3_.refs_4_.refs_5_.refs_6_.refs_7_.refs_8_.refs_9_.refs_10_.refs_11_ = bf16[64,96,128]{2,1,0:T(8,128)(2,1)S(1)} async-done(((bf16[64,96,128]{2,1,0:T(8,128)(2,1)}), bf16[64,96,128]{2,1,0:T(8,128)(2,1)S(1)}, u32[]{:S(2)}, u32[]{:S(2)}) %all-to-all-start.1) | async-done | bytes 1572896 | tf_op jit(solution)/shard_map/all_to_all | solution.py:590
  39.7 0.6 inner_edges.1
  40.3 1.7 %collective-permute-start.3 = (bf16[12,16,128]{2,1,0:T(8,128)(2,1)S(1)}, bf16[12,16,128]{2,1,0:T(8,128)(2,1)S(1)}, u32[]{:S(2)}, u32[]{:S(2)}) collective-permute-start(bf16[12,16,128]{2,1,0:T(8,128)(2,1)S(1)} %inner_edges.1), channel_id=1, source_target_pairs={{0,1},{1,0},{2,3},{3,2},{4,5},{5,4},{6,7},{7,6},{8,9},{9,8},{10,11... | collective-permute-start | bytes 147464 | tf_op jit(solution)/shard_map/ppermute | solution.py:576
  42.0 0.0 collective-permute-done.2.refs_15_
  42.0 0.0 collective-permute-done.1.refs_14_
  42.0 2.8 %collective-permute-done.3.refs_16_ = bf16[12,16,128]{2,1,0:T(8,128)(2,1)S(1)} collective-permute-done((bf16[12,16,128]{2,1,0:T(8,128)(2,1)S(1)}, bf16[12,16,128]{2,1,0:T(8,128)(2,1)S(1)}, u32[]{:S(2)}, u32[]{:S(2)}) %collective-permute-start.3) | collective-permute-done | bytes 49184 | tf_op jit(solution)/shard_map/ppermute | solution.py:576
  44.8 4.6 %residual_back.2 = (f32[4,9,2,24,128]{4,3,2,1,0:T(8,128)S(1)}, bf16[5,9,48,128]{3,2,1,0:T(8,128)(2,1)S(1)}, bf16[5,9,48,128]{3,2,1,0:T(8,128)(2,1)S(1)}) custom-call(s32[5]{0:T(128)S(1)} %stack.25.place, s32[12]{0:T(128)S(1)} %and_select_fusion.owner, s32[12]{0:T(128)S(1)} %convert_reduce_fusion.rank, s32[288]{0:T(512)S(1)} %get-tuple-element.56.steps, ...), custom_call_target="tpu_custom_call" | custom-call | tf_op jit(solution)/shard_map/residual_back/pallas_call | solution.py:432
  49.5 5.7 %collective-permute-start.4 = (bf16[5,9,48,128]{3,2,1,0:T(8,128)(2,1)S(1)}, bf16[5,9,48,128]{3,2,1,0:T(8,128)(2,1)S(1)}, u32[]{:S(2)}, u32[]{:S(2)}) collective-permute-start(bf16[5,9,48,128]{3,2,1,0:T(8,128)(2,1)S(1)} %get-tuple-element.47), channel_id=1, source_target_pairs={{0,2},{2,4},{4,6},{6,8},{8,10},{10,12},{12,14},{14,16},{16,18},{18... | collective-permute-start | bytes 1658888 | tf_op jit(solution)/shard_map/ppermute | solution.py:567
  55.2 1.9 %collective-permute-start.5 = (bf16[5,9,48,128]{3,2,1,0:T(8,128)(2,1)S(1)}, bf16[5,9,48,128]{3,2,1,0:T(8,128)(2,1)S(1)}, u32[]{:S(2)}, u32[]{:S(2)}) collective-permute-start(bf16[5,9,48,128]{3,2,1,0:T(8,128)(2,1)S(1)} %get-tuple-element.48), channel_id=1, source_target_pairs={{2,0},{4,2},{6,4},{8,6},{10,8},{12,10},{14,12},{16,14},{18,16},{20... | collective-permute-start | bytes 1658888 | tf_op jit(solution)/shard_map/ppermute | solution.py:572
  57.1 4.5 %collective-permute-done.4.before = bf16[5,9,48,128]{3,2,1,0:T(8,128)(2,1)S(1)} collective-permute-done((bf16[5,9,48,128]{3,2,1,0:T(8,128)(2,1)S(1)}, bf16[5,9,48,128]{3,2,1,0:T(8,128)(2,1)S(1)}, u32[]{:S(2)}, u32[]{:S(2)}) %collective-permute-start.4) | collective-permute-done | bytes 552992 | tf_op jit(solution)/shard_map/ppermute | solution.py:567
  61.6 7.4 %collective-permute-done.5.after = bf16[5,9,48,128]{3,2,1,0:T(8,128)(2,1)S(1)} collective-permute-done((bf16[5,9,48,128]{3,2,1,0:T(8,128)(2,1)S(1)}, bf16[5,9,48,128]{3,2,1,0:T(8,128)(2,1)S(1)}, u32[]{:S(2)}, u32[]{:S(2)}) %collective-permute-start.5) | collective-permute-done | bytes 552992 | tf_op jit(solution)/shard_map/ppermute | solution.py:572
  69.0 10.5 %smooth_project.1 = (f32[9,192,128]{2,1,0:T(8,128)S(1)}, f32[48,1152]{1,0:T(8,128)S(1)}, bf16[48,1152]{1,0:T(8,128)(2,1)S(1)}) custom-call(s32[5]{0:T(128)S(1)} %stack.25.place, s32[288]{0:T(512)S(1)} %get-tuple-element.56.steps, f32[288]{0:T(512)S(1)} %get-tuple-element.55.fractions, f32[4,9,2,24,128]{4,3,2,1,0:T(8,128)S(1)} %get-tuple-element.46.own, ...), custom_call_target="tpu_custom_call" | custom-call | tf_op jit(solution)/shard_map/smooth_project/pallas_call | solution.py:260
  79.5 1.9 %collective-permute-start.7 = (bf16[48,1152]{1,0:T(8,128)(2,1)S(1)}, bf16[48,1152]{1,0:T(8,128)(2,1)S(1)}, u32[]{:S(2)}, u32[]{:S(2)}) collective-permute-start(bf16[48,1152]{1,0:T(8,128)(2,1)S(1)} %get-tuple-element.51), channel_id=1, source_target_pairs={{2,0},{4,2},{6,4},{8,6},{10,8},{12,10},{14,12},{16,14},{18,16},{20... | collective-permute-start | bytes 331784 | tf_op jit(solution)/shard_map/ppermute | solution.py:572
  81.5 6.8 %collective-permute-start.6 = (bf16[48,1152]{1,0:T(8,128)(2,1)S(1)}, bf16[48,1152]{1,0:T(8,128)(2,1)S(1)}, u32[]{:S(2)}, u32[]{:S(2)}) collective-permute-start(bf16[48,1152]{1,0:T(8,128)(2,1)S(1)} %get-tuple-element.51), channel_id=1, source_target_pairs={{0,2},{2,4},{4,6},{6,8},{8,10},{10,12},{12,14},{14,16},{16,18},{18... | collective-permute-start | bytes 331784 | tf_op jit(solution)/shard_map/ppermute | solution.py:567
  88.3 0.3 collective-permute-done.7.refs_15_
  88.6 1.2 collective-permute-done.6.refs_14_
  89.8 4.6 %residual_back.3 = (f32[4,9,2,24,128]{4,3,2,1,0:T(8,128)S(1)}, bf16[5,9,48,128]{3,2,1,0:T(8,128)(2,1)S(1)}, bf16[5,9,48,128]{3,2,1,0:T(8,128)(2,1)S(1)}) custom-call(s32[5]{0:T(128)S(1)} %stack.25.place, s32[12]{0:T(128)S(1)} %and_select_fusion.owner, s32[12]{0:T(128)S(1)} %convert_reduce_fusion.rank, s32[288]{0:T(512)S(1)} %get-tuple-element.56.steps, ...), custom_call_target="tpu_custom_call" | custom-call | tf_op jit(solution)/shard_map/residual_back/pallas_call | solution.py:432
  94.5 7.3 %collective-permute-start.8 = (bf16[5,9,48,128]{3,2,1,0:T(8,128)(2,1)S(1)}, bf16[5,9,48,128]{3,2,1,0:T(8,128)(2,1)S(1)}, u32[]{:S(2)}, u32[]{:S(2)}) collective-permute-start(bf16[5,9,48,128]{3,2,1,0:T(8,128)(2,1)S(1)} %get-tuple-element.53), channel_id=1, source_target_pairs={{0,2},{2,4},{4,6},{6,8},{8,10},{10,12},{12,14},{14,16},{16,18},{18... | collective-permute-start | bytes 1658888 | tf_op jit(solution)/shard_map/ppermute | solution.py:567
  101.8 1.9 %collective-permute-start.9 = (bf16[5,9,48,128]{3,2,1,0:T(8,128)(2,1)S(1)}, bf16[5,9,48,128]{3,2,1,0:T(8,128)(2,1)S(1)}, u32[]{:S(2)}, u32[]{:S(2)}) collective-permute-start(bf16[5,9,48,128]{3,2,1,0:T(8,128)(2,1)S(1)} %get-tuple-element.54), channel_id=1, source_target_pairs={{2,0},{4,2},{6,4},{8,6},{10,8},{12,10},{14,12},{16,14},{18,16},{20... | collective-permute-start | bytes 1658888 | tf_op jit(solution)/shard_map/ppermute | solution.py:572
  103.7 4.5 %collective-permute-done.8.before = bf16[5,9,48,128]{3,2,1,0:T(8,128)(2,1)S(1)} collective-permute-done((bf16[5,9,48,128]{3,2,1,0:T(8,128)(2,1)S(1)}, bf16[5,9,48,128]{3,2,1,0:T(8,128)(2,1)S(1)}, u32[]{:S(2)}, u32[]{:S(2)}) %collective-permute-start.8) | collective-permute-done | bytes 552992 | tf_op jit(solution)/shard_map/ppermute | solution.py:567
  108.2 7.4 %collective-permute-done.9.after = bf16[5,9,48,128]{3,2,1,0:T(8,128)(2,1)S(1)} collective-permute-done((bf16[5,9,48,128]{3,2,1,0:T(8,128)(2,1)S(1)}, bf16[5,9,48,128]{3,2,1,0:T(8,128)(2,1)S(1)}, u32[]{:S(2)}, u32[]{:S(2)}) %collective-permute-start.9) | collective-permute-done | bytes 552992 | tf_op jit(solution)/shard_map/ppermute | solution.py:572
  115.6 10.1 %smooth_join.1 = f32[4,24,2048]{2,1,0:T(8,128)} custom-call(s32[5]{0:T(128)S(1)} %stack.25.place, f32[4,9,2,24,128]{4,3,2,1,0:T(8,128)S(1)} %get-tuple-element.52.own, bf16[5,9,48,128]{3,2,1,0:T(8,128)(2,1)S(1)} %collective-permute-done.8.before, bf16[5,9,48,128]{3,2,1,0:T(8,128)(2,1)S(1)} %collective-permute-done.9.after), custom_call_target="tpu_custom_call" | custom-call | tf_op jit(solution)/shard_map/smooth_join/pallas_call | solution.py:260
  (6 shorter events, 0.2 us)
Async XLA Ops:
  1.0 6.3 %collective-permute-start = (f32[4,24,256]{2,1,0:T(8,128)S(1)}, f32[4,24,256]{2,1,0:T(8,128)S(1)}, u32[]{:S(2)}, u32[]{:S(2)}) collective-permute-start(f32[4,24,256]{2,1,0:T(8,128)S(1)} %slice_select_fusion), channel_id=1, source_target_pairs={{0,1},{1,0},{2,3},{3,2},{4,5},{5,4},{6,7},{7,6},{8,9},{9,8},{10,11... | collective-permute-start | bytes 294920 | tf_op jit(solution)/shard_map/ppermute | solution.py:576
  7.2 11.0 %copy-start.3 = (s32[64]{0:T(128)S(1)}, s32[64]{0:T(128)}, u32[]{:S(2)}) copy-start(s32[64]{0:T(128)} %offsets.1) | copy-start | bytes 772
  7.2 14.5 %copy-start.4 = (s32[256]{0:T(256)S(1)}, s32[256]{0:T(256)}, u32[]{:S(2)}) copy-start(s32[256]{0:T(256)} %owners.1) | copy-start | bytes 3076
  7.3 14.7 %copy-start = (f32[4,24,2048]{2,1,0:T(8,128)S(1)}, f32[4,24,2048]{2,1,0:T(8,128)}, u32[]{:S(2)}) copy-start(f32[4,24,2048]{2,1,0:T(8,128)} %volume.1) | copy-start | bytes 2359300
  7.3 0.6 copy-start.1
  7.9 31.7 %all-to-all-start.1 = ((bf16[64,96,128]{2,1,0:T(8,128)(2,1)}), bf16[64,96,128]{2,1,0:T(8,128)(2,1)S(1)}, u32[]{:S(2)}, u32[]{:S(2)}) async-start(bf16[64,96,128]{2,1,0:T(8,128)(2,1)} %pack_images.3), calls=%async_computation.1 | async-start | bytes 3145728 | tf_op jit(solution)/shard_map/all_to_all | solution.py:590
  22.0 0.9 copy-start.2
  27.6 14.4 %collective-permute-start.2 = (bf16[48,1152]{1,0:T(8,128)(2,1)}, bf16[48,1152]{1,0:T(8,128)(2,1)S(1)}, u32[]{:S(2)}, u32[]{:S(2)}) collective-permute-start(bf16[48,1152]{1,0:T(8,128)(2,1)} %get-tuple-element.45), channel_id=1, source_target_pairs={{2,0},{4,2},{6,4},{8,6},{10,8},{12,10},{14,12},{16,14},{18,16},{20... | collective-permute-start | bytes 331784 | tf_op jit(solution)/shard_map/ppermute | solution.py:572
  29.9 12.1 %collective-permute-start.1 = (bf16[48,1152]{1,0:T(8,128)(2,1)}, bf16[48,1152]{1,0:T(8,128)(2,1)S(1)}, u32[]{:S(2)}, u32[]{:S(2)}) collective-permute-start(bf16[48,1152]{1,0:T(8,128)(2,1)} %get-tuple-element.45), channel_id=1, source_target_pairs={{0,2},{2,4},{4,6},{6,8},{8,10},{10,12},{12,14},{14,16},{16,18},{18... | collective-permute-start | bytes 331784 | tf_op jit(solution)/shard_map/ppermute | solution.py:567
  40.3 4.5 %collective-permute-start.3 = (bf16[12,16,128]{2,1,0:T(8,128)(2,1)S(1)}, bf16[12,16,128]{2,1,0:T(8,128)(2,1)S(1)}, u32[]{:S(2)}, u32[]{:S(2)}) collective-permute-start(bf16[12,16,128]{2,1,0:T(8,128)(2,1)S(1)} %inner_edges.1), channel_id=1, source_target_pairs={{0,1},{1,0},{2,3},{3,2},{4,5},{5,4},{6,7},{7,6},{8,9},{9,8},{10,11... | collective-permute-start | bytes 147464 | tf_op jit(solution)/shard_map/ppermute | solution.py:576
  49.5 12.1 %collective-permute-start.4 = (bf16[5,9,48,128]{3,2,1,0:T(8,128)(2,1)S(1)}, bf16[5,9,48,128]{3,2,1,0:T(8,128)(2,1)S(1)}, u32[]{:S(2)}, u32[]{:S(2)}) collective-permute-start(bf16[5,9,48,128]{3,2,1,0:T(8,128)(2,1)S(1)} %get-tuple-element.47), channel_id=1, source_target_pairs={{0,2},{2,4},{4,6},{6,8},{8,10},{10,12},{12,14},{14,16},{16,18},{18... | collective-permute-start | bytes 1658888 | tf_op jit(solution)/shard_map/ppermute | solution.py:567
  55.2 13.8 %collective-permute-start.5 = (bf16[5,9,48,128]{3,2,1,0:T(8,128)(2,1)S(1)}, bf16[5,9,48,128]{3,2,1,0:T(8,128)(2,1)S(1)}, u32[]{:S(2)}, u32[]{:S(2)}) collective-permute-start(bf16[5,9,48,128]{3,2,1,0:T(8,128)(2,1)S(1)} %get-tuple-element.48), channel_id=1, source_target_pairs={{2,0},{4,2},{6,4},{8,6},{10,8},{12,10},{14,12},{16,14},{18,16},{20... | collective-permute-start | bytes 1658888 | tf_op jit(solution)/shard_map/ppermute | solution.py:572
  79.5 9.1 %collective-permute-start.7 = (bf16[48,1152]{1,0:T(8,128)(2,1)S(1)}, bf16[48,1152]{1,0:T(8,128)(2,1)S(1)}, u32[]{:S(2)}, u32[]{:S(2)}) collective-permute-start(bf16[48,1152]{1,0:T(8,128)(2,1)S(1)} %get-tuple-element.51), channel_id=1, source_target_pairs={{2,0},{4,2},{6,4},{8,6},{10,8},{12,10},{14,12},{16,14},{18,16},{20... | collective-permute-start | bytes 331784 | tf_op jit(solution)/shard_map/ppermute | solution.py:572
  81.5 8.4 %collective-permute-start.6 = (bf16[48,1152]{1,0:T(8,128)(2,1)S(1)}, bf16[48,1152]{1,0:T(8,128)(2,1)S(1)}, u32[]{:S(2)}, u32[]{:S(2)}) collective-permute-start(bf16[48,1152]{1,0:T(8,128)(2,1)S(1)} %get-tuple-element.51), channel_id=1, source_target_pairs={{0,2},{2,4},{4,6},{6,8},{8,10},{10,12},{12,14},{14,16},{16,18},{18... | collective-permute-start | bytes 331784 | tf_op jit(solution)/shard_map/ppermute | solution.py:567
  94.5 13.8 %collective-permute-start.8 = (bf16[5,9,48,128]{3,2,1,0:T(8,128)(2,1)S(1)}, bf16[5,9,48,128]{3,2,1,0:T(8,128)(2,1)S(1)}, u32[]{:S(2)}, u32[]{:S(2)}) collective-permute-start(bf16[5,9,48,128]{3,2,1,0:T(8,128)(2,1)S(1)} %get-tuple-element.53), channel_id=1, source_target_pairs={{0,2},{2,4},{4,6},{6,8},{8,10},{10,12},{12,14},{14,16},{16,18},{18... | collective-permute-start | bytes 1658888 | tf_op jit(solution)/shard_map/ppermute | solution.py:567
  101.8 13.8 %collective-permute-start.9 = (bf16[5,9,48,128]{3,2,1,0:T(8,128)(2,1)S(1)}, bf16[5,9,48,128]{3,2,1,0:T(8,128)(2,1)S(1)}, u32[]{:S(2)}, u32[]{:S(2)}) collective-permute-start(bf16[5,9,48,128]{3,2,1,0:T(8,128)(2,1)S(1)} %get-tuple-element.54), channel_id=1, source_target_pairs={{2,0},{4,2},{6,4},{8,6},{10,8},{12,10},{14,12},{16,14},{18,16},{20... | collective-permute-start | bytes 1658888 | tf_op jit(solution)/shard_map/ppermute | solution.py:572

commit v4 on v3

--- a/solution.py
+++ b/solution.py
@@ -15,6 +15,7 @@
 relaxation = 0.8
 smooth_step = 0.05
 smooth_floor = 0.1
+SCALE = 20.0
 
 ZS = 4
 XW = 24
@@ -127,14 +128,14 @@
     slab = lax.axis_index("gz")
     stored = images.shape[0]
     slab_count = out.shape[0]
-    count = subsets.shape[0]
+    count = SUBSETS * SUBSET
     found = jnp.int32(0)
     slots = [jnp.int32(0), jnp.int32(0)]
     for i in range(stored):
         view = owners[stored * slab + i]
         hits = jnp.int32(0)
         for k in range(count):
-            hits = hits + (subsets[k] == view).astype(jnp.int32)
+            hits = hits + (subsets[k // SUBSET, k % SUBSET] == view).astype(jnp.int32)
         for slot in range(2):
             slots[slot] = jnp.where((hits > 0) & (found == first_slot + slot), i, slots[slot])
         found = found + hits
@@ -169,7 +170,7 @@
     chunk = slab_count // CHUNKS
     sent = []
     for part in range(CHUNKS):
-        lax.fori_loop(part * chunk, part * chunk + chunk, one_slab, 0, unroll=2)
+        lax.fori_loop(part * chunk, part * chunk + chunk, one_slab, 0, unroll=4)
         here = pl.ds(part * chunk, chunk)
         sent.append(pltpu.make_async_copy(ready.at[here], out.at[here], out_sems.at[part]))
         sent[-1].start()
@@ -353,17 +354,20 @@
         frame = [
             jnp.where(lane < 64, a, b) for a, b in zip([zero] + turned, turned + [zero])
         ]
-        for shift in range(3):
-            if shift == 0:
-                rows = frame
-            else:
-                back = [pltpu.roll(tile, 128 - shift, 1) for tile in frame] + [zero]
-                rows = [
+        moved = [frame]
+        for shift in (1, 2):
+            back = [pltpu.roll(tile, 128 - shift, 1) for tile in frame] + [zero]
+            moved.append(
+                [
                     jnp.where(lane < 128 - shift, back[j], back[j + 1])
                     for j in range(TILES + 1)
                 ]
-            for j in range(TILES + 1):
-                held[v, shift, j] = rows[j]
+            )
+        for j in range(TILES + 1):
+            held[v, 0, j] = moved[0][j]
+            held[v, 1, j] = moved[1][j]
+            held[v, 2, j] = jnp.where(sub < ZS, moved[0][j], moved[1][j])
+            held[v, 3, j] = jnp.where(sub < ZS, moved[1][j], moved[2][j])
 
     def back_x(x, carry):
         here = pl.ds(pl.multiple_of(8 * x, 8), 8)
@@ -371,19 +375,22 @@
         for v in range(SUBSET):
             at = (base + v) * XW + x
             step = steps[at]
-            coef = taps(fractions[at])
+            fraction = fractions[at]
+            late = (fraction >= 0.5).astype(jnp.int32)
+            near = 1.0 - fraction + jnp.where(sub >= ZS, late.astype(F32) - 0.5, 0.0)
+            far = 1.0 - near
             turned = []
             for j in range(TILES + 1):
-                mix = (
-                    coef[0] * held[v, 0, j] + coef[1] * held[v, 1, j] + coef[2] * held[v, 2, j]
-                )
+                mix = near * held[v, 2 * late, j] + far * held[v, 2 * late + 1, j]
                 turned.append(pltpu.roll(mix, 128 - step, 1))
             mask = lane < 128 - step
             totals_x = [
                 totals_x[j] + jnp.where(mask, turned[j], turned[j + 1]) for j in range(TILES)
             ]
         for j in range(TILES):
-            moved_state[j, here, :] = state[j, here, :] + (relaxation / SUBSET) * totals_x[j]
+            moved_state[j, here, :] = (
+                SCALE * state[j, here, :] + (SCALE * relaxation / SUBSET) * totals_x[j]
+            )
         return carry
 
     lax.fori_loop(0, XW, back_x, 0, unroll=BACK_UNROLL)
@@ -422,7 +429,7 @@
         + [whole(a) for a in (state, own, before, after, edges)],
         out_specs=[whole(a) for a in SLAB_OUT],
         scratch_shapes=[
-            pltpu.VMEM((SUBSET, 3, TILES + 1, 8, 128), F32),
+            pltpu.VMEM((SUBSET, 4, TILES + 1, 8, 128), F32),
             pltpu.VMEM((TILES, 8 * XW, 128), F32),
             pltpu.VMEM((SUBSET, PACKED + 8, 128), F32),
             pltpu.VMEM((SUBSET, 24, 128), F32),
@@ -442,18 +449,22 @@
 
 
 def smooth(own, before, after, buffers, along, in_before, in_after, store):
+    sub, lane = iota2(0), iota2(1)
+    zero = jnp.zeros((8, 128), F32)
+    blocks = range(XW // 8)
+    first_lane, not_last, not_first = lane == 0, sub < 7, sub > 0
+
     def first(z, j):
         if ZS <= z < 2 * ZS:
-            return [own[z - ZS, j, p] for p in range(2)]
-        side = before if z < ZS else after
-        both = side[z % ZS, j].astype(F32)
-        if z in (ZS - 1, 2 * ZS):
-            both = both + side[ZS, j].astype(F32)
-        return [both[:XW], both[XW:]]
-
-    row24 = lax.broadcasted_iota(jnp.int32, (XW, 128), 0)
-    lane24 = lax.broadcasted_iota(jnp.int32, (XW, 128), 1)
-    zero = jnp.zeros((XW, 128), F32)
+            both = [own[z - ZS, j, p] for p in range(2)]
+        else:
+            side = before if z < ZS else after
+            joined = side[z % ZS, j].astype(F32)
+            if z in (ZS - 1, 2 * ZS):
+                joined = joined + side[ZS, j].astype(F32)
+            both = [joined[:XW], joined[XW:]]
+        return [[both[p][8 * i : 8 * i + 8] for i in blocks] for p in range(2)]
+
     for index in range(PASSES):
         low, high = 1 + index, 10 - index
         last = index == PASSES - 1
@@ -463,66 +474,93 @@
         def load(z, j, index=index, source=source):
             if index == 0:
                 return first(z, j)
-            return [source[z, j, p] for p in range(2)]
+            return [[source[z, j, p, 8 * i : 8 * i + 8] for i in blocks] for p in range(2)]
+
+        def next_row(z, j, p, values, index=index, source=source):
+            if index == 0:
+                turned = [pltpu.roll(value, 7, 0) for value in values] + [zero]
+                return [jnp.where(not_last, turned[i], turned[i + 1]) for i in blocks]
+            moved = [source[z, j, p, 8 * i + 1 : 8 * i + 9] for i in blocks]
+            moved[-1] = jnp.where(not_last, moved[-1], 0.0)
+            return moved
 
         for z in range(low, high + 1):
-            along[z] = zero
-
-        def one_tile(j, carry, low=low, high=high, last=last, target=target, load=load):
+            along[z] = jnp.zeros((XW, 128), F32)
+
+        def one_tile(
+            j, carry, low=low, high=high, last=last, target=target, load=load, next_row=next_row
+        ):
             following = jnp.minimum(j + 1, TILES - 1)
-            has_following = j < TILES - 1
+            has_following = (j < TILES - 1).astype(F32)
             current = load(low - 1, j)
             flux_before = None
             for z in range(low - 1, high + 1):
                 above = load(z + 1, j)
-                beside = jnp.where(has_following, load(z, following)[0], 0.0)
-                next_even = pltpu.roll(
-                    jnp.where(lane24 == 0, beside, current[0]), 127, 1
-                )
+                beside = load(z, following)[0]
+                next_even = [
+                    pltpu.roll(
+                        jnp.where(first_lane, beside[i] * has_following, current[0][i]), 127, 1
+                    )
+                    for i in blocks
+                ]
                 ahead = [current[1], next_even]
-                fluxes = []
+                flux_z, flux_x, flux_y = [], [], []
                 for p in range(2):
                     c = current[p]
-                    dz = above[p] - c
-                    dx = jnp.where(row24 < XW - 1, pltpu.roll(c, XW - 1, 0), 0.0) - c
-                    dy = ahead[p] - c
-                    scale = lax.rsqrt(dz * dz + dx * dx + dy * dy + smooth_floor)
-                    fluxes.append((dz * scale, dx * scale, dy * scale))
-                flux_z = [fluxes[p][0] for p in range(2)]
+                    row_next = next_row(z, j, p, c)
+                    for i in blocks:
+                        dz = above[p][i] - c[i]
+                        dx = row_next[i] - c[i]
+                        dy = ahead[p][i] - c[i]
+                        scale = lax.rsqrt(
+                            dz * dz + dx * dx + dy * dy + smooth_floor * SCALE * SCALE
+                        )
+                        flux_z.append(dz * scale)
+                        flux_x.append(dx * scale)
+                        flux_y.append(dy * scale)
+                count = len(blocks)
+                if z >= low:
+                    turned = [pltpu.roll(flux_y[count + i], 1, 1) for i in blocks]
+                    behind = [
+                        jnp.where(first_lane, along[z, 8 * i : 8 * i + 8], turned[i])
+                        for i in blocks
+                    ] + flux_y[:count]
+                    for i in blocks:
+                        along[z, 8 * i : 8 * i + 8] = turned[i]
+                    for p in range(2):
+                        rolled = [
+                            pltpu.roll(flux_x[count * p + i], 1, 0) for i in blocks
+                        ]
+                        rolled = [zero] + rolled
+                        for i in blocks:
+                            k = count * p + i
+                            row_before = jnp.where(not_first, rolled[i + 1], rolled[i])
+                            fresh = (
+                                current[p][i]
+                                + (flux_z[k] - flux_before[k])
+                                + (flux_x[k] - row_before)
+                                + (flux_y[k] - behind[k])
+                            )
+                            if z < ZS:
+                                fresh = fresh * in_before
+                            if z >= 2 * ZS:
+                                fresh = fresh * in_after
+                            if last:
+                                store(z - ZS, j, p, i, fresh * smooth_step)
+                            else:
+                                target[z, j, p, 8 * i : 8 * i + 8] = fresh
                 if z < ZS:
                     flux_z = [f * in_before for f in flux_z]
-                if z >= low:
-                    turned = pltpu.roll(fluxes[1][2], 1, 1)
-                    behind_even = jnp.where(lane24 == 0, along[z], turned)
-                    along[z] = turned
-                    behind = [behind_even, fluxes[0][2]]
-                    for p in range(2):
-                        flux_x = fluxes[p][1]
-                        back_x = jnp.where(row24 > 0, pltpu.roll(flux_x, 1, 0), 0.0)
-                        gradient = (
-                            (flux_before[p] - fluxes[p][0])
-                            + (back_x - flux_x)
-                            + (behind[p] - fluxes[p][2])
-                        )
-                        fresh = current[p] - smooth_step * gradient
-                        if z < ZS:
-                            fresh = fresh * in_before
-                        if z >= 2 * ZS:
-                            fresh = fresh * in_after
-                        if last:
-                            store(z - ZS, j, p, fresh)
-                        else:
-                            target[z, j, p] = fresh
                 flux_before = flux_z
                 current = above
             return carry
 
-        lax.fori_loop(0, TILES, one_tile, 0)
+        lax.fori_loop(0, TILES, one_tile, 0, unroll=3)
 
 
 SMOOTH_SCRATCH = [
-    pltpu.VMEM((3 * ZS, TILES, 2, XW, 128), F32),
-    pltpu.VMEM((3 * ZS, TILES, 2, XW, 128), F32),
+    pltpu.VMEM((3 * ZS, TILES, 2, XW + 8, 128), F32),
+    pltpu.VMEM((3 * ZS, TILES, 2, XW + 8, 128), F32),
     pltpu.VMEM((3 * ZS, XW, 128), F32),
 ]
 
@@ -530,8 +568,8 @@
 def smooth_project_kernel(
     place, steps, fractions, own, before, after, state, rows_ref, rows16_ref, one, two, along
 ):
-    def store(z, j, p, value):
-        state[j, pl.ds(4 * p + z, XW, stride=8), :] = value
+    def store(z, j, p, i, value):
+        state[j, pl.ds(64 * i + 4 * p + z, 8, stride=8), :] = value
 
     smooth(
         own, before, after, (one, two), along,
@@ -541,8 +579,8 @@
 
 
 def smooth_end_kernel(place, own, before, after, out, one, two, along):
-    def store(z, j, p, value):
-        two[z, j, p] = value
+    def store(z, j, p, i, value):
+        two[z, j, p, 8 * i : 8 * i + 8] = value
 
     smooth(
         own, before, after, (one, two), along,
@@ -553,7 +591,7 @@
     for j in range(TILES - 1):
         pixels = jnp.concatenate(
             [
-                jnp.concatenate([two[z, j + column, 0], two[z, j + column, 1]], axis=1)
+                jnp.concatenate([two[z, j + column, p, :XW] for p in range(2)], axis=1)
                 for z in range(ZS)
             ],
             axis=0,
@@ -585,7 +623,7 @@
 
     edge = swap_halves(jnp.where(column == 0, volume[:, :, -256:], volume[:, :, :256]))
     views = subsets.reshape(-1)
-    packed = pack(0, owners, views, offsets, images)
+    packed = pack(0, owners, subsets, offsets, images)
     packed, edge = lax.optimization_barrier((packed, edge))
     recv = lax.all_to_all(packed, "gz", 0, 0)
 
@@ -624,7 +662,7 @@
     later_images, recv = lax.optimization_barrier((images, recv))
 
     def fetch_more():
-        more = lax.all_to_all(pack(2, owners, views, offsets, later_images), "gz", 0, 0)
+        more = lax.all_to_all(pack(2, owners, subsets, offsets, later_images), "gz", 0, 0)
         return more[owner]
 
     extra = lax.cond(

time: 126 us -> 123 us (0.976)
  Pallas kernels: 38.6 us -> 35.7 us
    pallas_call x3, Pallas kernels: 25.3 us -> 22.5 us  [scalar_call(): pl.pallas_call(kernel, in_specs=[smem] * len(scalars) + [vmem] * len(arra...]
where the time goes in v4:
time: 123 us; the launch traced here: 122 us
  starting transfers between devices  49.1 us (40%)
  Pallas kernels  35.7 us (29%)
  waiting for transfers between devices  29.8 us (24%)
  between operations  3.27 us (3%)
  local copies, waits for them, and re-layouts  2.49 us (2%)
  other arithmetic  2.07 us (2%)
    ppermute x4, starting transfers between devices, to_next(): return lax.ppermute(value, 'gz', [(i, i + 1) for i in range(count - 1)])  26 us
    pallas_call x3, Pallas kernels, scalar_call(): pl.pallas_call(kernel, in_specs=[smem] * len(scalars) + [vmem] * len(arra...  22.5 us
    ppermute x4, waiting for transfers between devices, to_before(): return lax.ppermute(value, 'gz', [(i + 1, i) for i in range(count - 1)])  15.3 us
    all_to_all x1, starting transfers between devices, body(): recv = lax.all_to_all(packed, 'gz', 0, 0)  10.7 us
    ppermute x4, waiting for transfers between devices, to_next(): return lax.ppermute(value, 'gz', [(i, i + 1) for i in range(count - 1)])  10 us
    pallas_call x2, Pallas kernels, update(): pl.pallas_call(functools.partial(update_kernel, base), grid_spec=spec, ou...  9.19 us
    ppermute x4, starting transfers between devices, to_before(): return lax.ppermute(value, 'gz', [(i + 1, i) for i in range(count - 1)])  8.2 us
    ppermute x2, starting transfers between devices, swap_halves(): return lax.ppermute(value, 'col', [(0, 1), (1, 0)])  4.19 us
  transfers between devices with their start and end apart: 11, of which 8 were waited for; matrix products, arithmetic and copies ran while one was open for 2% of the time, Pallas kernels for 7%

profile of v4, /device:TPU:15, one launch (start us, length us, event | category | flops | bytes accessed | tf_op | source)
XLA Modules:
  0.0 122.4 jit_solution(7789959598088016339)
XLA Ops:
  0.0 1.0 slice_select_fusion
  1.0 2.1 %collective-permute-start = (f32[4,24,256]{2,1,0:T(8,128)S(1)}, f32[4,24,256]{2,1,0:T(8,128)S(1)}, u32[]{:S(2)}, u32[]{:S(2)}) collective-permute-start(f32[4,24,256]{2,1,0:T(8,128)S(1)} %slice_select_fusion), channel_id=1, source_target_pairs={{0,1},{1,0},{2,3},{3,2},{4,5},{5,4},{6,7},{7,6},{8,9},{9,8},{10,11... | collective-permute-start | bytes 294920 | tf_op jit(solution)/shard_map/ppermute | solution.py:614
  3.1 3.4 %pack_images.3 = bf16[64,96,128]{2,1,0:T(8,128)(2,1)} custom-call(s32[256]{0:T(256)} %owners.1, s32[2,6]{1,0:T(2,128)} %subsets.1, s32[64]{0:T(128)} %offsets.1, bf16[4,264,1024]{2,1,0:T(8,128)(2,1)} %images.1), custom_call_target="tpu_custom_call" | custom-call | tf_op jit(solution)/shard_map/pack_images/pallas_call | solution.py:186
  6.4 0.0 copy-start.5
  6.5 0.0 copy-start.3
  6.5 0.0 copy-start.4
  6.5 0.0 copy-start
  6.5 0.0 collective-permute-done.edge
  6.5 0.0 copy-start.1
  6.5 0.6 copy-done.1
  7.2 10.7 %all-to-all-start.1 = ((bf16[64,96,128]{2,1,0:T(8,128)(2,1)}), bf16[64,96,128]{2,1,0:T(8,128)(2,1)S(1)}, u32[]{:S(2)}, u32[]{:S(2)}) async-start(bf16[64,96,128]{2,1,0:T(8,128)(2,1)} %pack_images.3), calls=%async_computation.1 | async-start | bytes 3145728 | tf_op jit(solution)/shard_map/all_to_all | solution.py:628
  17.8 0.0 copy-done.5
  17.9 0.1 eq.32
  17.9 0.0 copy-done.3
  17.9 0.6 fusion
  21.1 0.1 multiply_add_fusion
  21.2 0.1 add.53
  21.3 0.1 stack.25.place
  21.4 0.0 copy-done.4
  21.4 0.2 select_reduce_fusion
  21.6 0.0 copy-done
  21.6 0.0 copy-start.2
  21.6 0.9 copy-done.2
  22.5 4.7 %split_project.1 = (f32[9,192,128]{2,1,0:T(8,128)S(1)}, f32[48,1152]{1,0:T(8,128)S(1)}, bf16[48,1152]{1,0:T(8,128)(2,1)}) custom-call(s32[5]{0:T(128)S(1)} %stack.25.place, s32[288]{0:T(512)S(1)} %get-tuple-element.56.steps, f32[288]{0:T(512)S(1)} %get-tuple-element.55.fractions, f32[4,24,2048]{2,1,0:T(8,128)S(1)} %copy-done, f32[4,24,256]{2,1,0:T(8,128)S(1)} %copy-done.2), custom_call_target="tpu_custom_call" | custom-call | tf_op jit(solution)/shard_map/split_project/pallas_call | solution.py:261
  27.2 2.3 %collective-permute-start.2 = (bf16[48,1152]{1,0:T(8,128)(2,1)}, bf16[48,1152]{1,0:T(8,128)(2,1)S(1)}, u32[]{:S(2)}, u32[]{:S(2)}) collective-permute-start(bf16[48,1152]{1,0:T(8,128)(2,1)} %get-tuple-element.45), channel_id=1, source_target_pairs={{2,0},{4,2},{6,4},{8,6},{10,8},{12,10},{14,12},{16,14},{18,16},{20... | collective-permute-start | bytes 331784 | tf_op jit(solution)/shard_map/ppermute | solution.py:610
  29.5 6.3 %collective-permute-start.1 = (bf16[48,1152]{1,0:T(8,128)(2,1)}, bf16[48,1152]{1,0:T(8,128)(2,1)S(1)}, u32[]{:S(2)}, u32[]{:S(2)}) collective-permute-start(bf16[48,1152]{1,0:T(8,128)(2,1)} %get-tuple-element.45), channel_id=1, source_target_pairs={{0,2},{2,4},{4,6},{6,8},{8,10},{10,12},{12,14},{14,16},{16,18},{18... | collective-permute-start | bytes 331784 | tf_op jit(solution)/shard_map/ppermute | solution.py:605
  35.8 0.2 convert_reduce_fusion.rank
  36.0 0.6 reduce_max.9
  37.1 2.1 %all-to-all-done.1.refs_0_.refs_1_.refs_2_.refs_3_.refs_4_.refs_5_.refs_6_.refs_7_.refs_8_.refs_9_.refs_10_.refs_11_ = bf16[64,96,128]{2,1,0:T(8,128)(2,1)S(1)} async-done(((bf16[64,96,128]{2,1,0:T(8,128)(2,1)}), bf16[64,96,128]{2,1,0:T(8,128)(2,1)S(1)}, u32[]{:S(2)}, u32[]{:S(2)}) %all-to-all-start.1) | async-done | bytes 1572896 | tf_op jit(solution)/shard_map/all_to_all | solution.py:628
  39.3 0.6 inner_edges.1
  39.9 2.1 %collective-permute-start.3 = (bf16[12,16,128]{2,1,0:T(8,128)(2,1)S(1)}, bf16[12,16,128]{2,1,0:T(8,128)(2,1)S(1)}, u32[]{:S(2)}, u32[]{:S(2)}) collective-permute-start(bf16[12,16,128]{2,1,0:T(8,128)(2,1)S(1)} %inner_edges.1), channel_id=1, source_target_pairs={{0,1},{1,0},{2,3},{3,2},{4,5},{5,4},{6,7},{7,6},{8,9},{9,8},{10,11... | collective-permute-start | bytes 147464 | tf_op jit(solution)/shard_map/ppermute | solution.py:614
  42.0 0.0 collective-permute-done.2.refs_15_
  42.0 0.0 collective-permute-done.1.refs_14_
  42.0 2.4 %collective-permute-done.3.refs_16_ = bf16[12,16,128]{2,1,0:T(8,128)(2,1)S(1)} collective-permute-done((bf16[12,16,128]{2,1,0:T(8,128)(2,1)S(1)}, bf16[12,16,128]{2,1,0:T(8,128)(2,1)S(1)}, u32[]{:S(2)}, u32[]{:S(2)}) %collective-permute-start.3) | collective-permute-done | bytes 49184 | tf_op jit(solution)/shard_map/ppermute | solution.py:614
  44.4 4.6 %residual_back.2 = (f32[4,9,2,24,128]{4,3,2,1,0:T(8,128)S(1)}, bf16[5,9,48,128]{3,2,1,0:T(8,128)(2,1)S(1)}, bf16[5,9,48,128]{3,2,1,0:T(8,128)(2,1)S(1)}) custom-call(s32[5]{0:T(128)S(1)} %stack.25.place, s32[12]{0:T(128)S(1)} %and_select_fusion.owner, s32[12]{0:T(128)S(1)} %convert_reduce_fusion.rank, s32[288]{0:T(512)S(1)} %get-tuple-element.56.steps, ...), custom_call_target="tpu_custom_call" | custom-call | tf_op jit(solution)/shard_map/residual_back/pallas_call | solution.py:439
  49.0 5.7 %collective-permute-start.4 = (bf16[5,9,48,128]{3,2,1,0:T(8,128)(2,1)S(1)}, bf16[5,9,48,128]{3,2,1,0:T(8,128)(2,1)S(1)}, u32[]{:S(2)}, u32[]{:S(2)}) collective-permute-start(bf16[5,9,48,128]{3,2,1,0:T(8,128)(2,1)S(1)} %get-tuple-element.47), channel_id=1, source_target_pairs={{0,2},{2,4},{4,6},{6,8},{8,10},{10,12},{12,14},{14,16},{16,18},{18... | collective-permute-start | bytes 1658888 | tf_op jit(solution)/shard_map/ppermute | solution.py:605
  54.7 2.1 %collective-permute-start.5 = (bf16[5,9,48,128]{3,2,1,0:T(8,128)(2,1)S(1)}, bf16[5,9,48,128]{3,2,1,0:T(8,128)(2,1)S(1)}, u32[]{:S(2)}, u32[]{:S(2)}) collective-permute-start(bf16[5,9,48,128]{3,2,1,0:T(8,128)(2,1)S(1)} %get-tuple-element.48), channel_id=1, source_target_pairs={{2,0},{4,2},{6,4},{8,6},{10,8},{12,10},{14,12},{16,14},{18,16},{20... | collective-permute-start | bytes 1658888 | tf_op jit(solution)/shard_map/ppermute | solution.py:610
  56.8 4.3 %collective-permute-done.4.before = bf16[5,9,48,128]{3,2,1,0:T(8,128)(2,1)S(1)} collective-permute-done((bf16[5,9,48,128]{3,2,1,0:T(8,128)(2,1)S(1)}, bf16[5,9,48,128]{3,2,1,0:T(8,128)(2,1)S(1)}, u32[]{:S(2)}, u32[]{:S(2)}) %collective-permute-start.4) | collective-permute-done | bytes 552992 | tf_op jit(solution)/shard_map/ppermute | solution.py:605
  61.1 7.4 %collective-permute-done.5.after = bf16[5,9,48,128]{3,2,1,0:T(8,128)(2,1)S(1)} collective-permute-done((bf16[5,9,48,128]{3,2,1,0:T(8,128)(2,1)S(1)}, bf16[5,9,48,128]{3,2,1,0:T(8,128)(2,1)S(1)}, u32[]{:S(2)}, u32[]{:S(2)}) %collective-permute-start.5) | collective-permute-done | bytes 552992 | tf_op jit(solution)/shard_map/ppermute | solution.py:610
  68.6 9.2 %smooth_project.1 = (f32[9,192,128]{2,1,0:T(8,128)S(1)}, f32[48,1152]{1,0:T(8,128)S(1)}, bf16[48,1152]{1,0:T(8,128)(2,1)S(1)}) custom-call(s32[5]{0:T(128)S(1)} %stack.25.place, s32[288]{0:T(512)S(1)} %get-tuple-element.56.steps, f32[288]{0:T(512)S(1)} %get-tuple-element.55.fractions, f32[4,9,2,24,128]{4,3,2,1,0:T(8,128)S(1)} %get-tuple-element.46.own, ...), custom_call_target="tpu_custom_call" | custom-call | tf_op jit(solution)/shard_map/smooth_project/pallas_call | solution.py:261
  77.7 1.9 %collective-permute-start.7 = (bf16[48,1152]{1,0:T(8,128)(2,1)S(1)}, bf16[48,1152]{1,0:T(8,128)(2,1)S(1)}, u32[]{:S(2)}, u32[]{:S(2)}) collective-permute-start(bf16[48,1152]{1,0:T(8,128)(2,1)S(1)} %get-tuple-element.51), channel_id=1, source_target_pairs={{2,0},{4,2},{6,4},{8,6},{10,8},{12,10},{14,12},{16,14},{18,16},{20... | collective-permute-start | bytes 331784 | tf_op jit(solution)/shard_map/ppermute | solution.py:610
  79.7 6.7 %collective-permute-start.6 = (bf16[48,1152]{1,0:T(8,128)(2,1)S(1)}, bf16[48,1152]{1,0:T(8,128)(2,1)S(1)}, u32[]{:S(2)}, u32[]{:S(2)}) collective-permute-start(bf16[48,1152]{1,0:T(8,128)(2,1)S(1)} %get-tuple-element.51), channel_id=1, source_target_pairs={{0,2},{2,4},{4,6},{6,8},{8,10},{10,12},{12,14},{14,16},{16,18},{18... | collective-permute-start | bytes 331784 | tf_op jit(solution)/shard_map/ppermute | solution.py:605
  86.3 0.5 collective-permute-done.7.refs_15_
  86.8 1.2 %collective-permute-done.6.refs_14_ = bf16[48,1152]{1,0:T(8,128)(2,1)S(1)} collective-permute-done((bf16[48,1152]{1,0:T(8,128)(2,1)S(1)}, bf16[48,1152]{1,0:T(8,128)(2,1)S(1)}, u32[]{:S(2)}, u32[]{:S(2)}) %collective-permute-start.6) | collective-permute-done | bytes 110624 | tf_op jit(solution)/shard_map/ppermute | solution.py:605
  88.0 4.6 %residual_back.3 = (f32[4,9,2,24,128]{4,3,2,1,0:T(8,128)S(1)}, bf16[5,9,48,128]{3,2,1,0:T(8,128)(2,1)S(1)}, bf16[5,9,48,128]{3,2,1,0:T(8,128)(2,1)S(1)}) custom-call(s32[5]{0:T(128)S(1)} %stack.25.place, s32[12]{0:T(128)S(1)} %and_select_fusion.owner, s32[12]{0:T(128)S(1)} %convert_reduce_fusion.rank, s32[288]{0:T(512)S(1)} %get-tuple-element.56.steps, ...), custom_call_target="tpu_custom_call" | custom-call | tf_op jit(solution)/shard_map/residual_back/pallas_call | solution.py:439
  92.6 7.3 %collective-permute-start.8 = (bf16[5,9,48,128]{3,2,1,0:T(8,128)(2,1)S(1)}, bf16[5,9,48,128]{3,2,1,0:T(8,128)(2,1)S(1)}, u32[]{:S(2)}, u32[]{:S(2)}) collective-permute-start(bf16[5,9,48,128]{3,2,1,0:T(8,128)(2,1)S(1)} %get-tuple-element.53), channel_id=1, source_target_pairs={{0,2},{2,4},{4,6},{6,8},{8,10},{10,12},{12,14},{14,16},{16,18},{18... | collective-permute-start | bytes 1658888 | tf_op jit(solution)/shard_map/ppermute | solution.py:605
  100.0 1.9 %collective-permute-start.9 = (bf16[5,9,48,128]{3,2,1,0:T(8,128)(2,1)S(1)}, bf16[5,9,48,128]{3,2,1,0:T(8,128)(2,1)S(1)}, u32[]{:S(2)}, u32[]{:S(2)}) collective-permute-start(bf16[5,9,48,128]{3,2,1,0:T(8,128)(2,1)S(1)} %get-tuple-element.54), channel_id=1, source_target_pairs={{2,0},{4,2},{6,4},{8,6},{10,8},{12,10},{14,12},{16,14},{18,16},{20... | collective-permute-start | bytes 1658888 | tf_op jit(solution)/shard_map/ppermute | solution.py:610
  101.9 4.5 %collective-permute-done.8.before = bf16[5,9,48,128]{3,2,1,0:T(8,128)(2,1)S(1)} collective-permute-done((bf16[5,9,48,128]{3,2,1,0:T(8,128)(2,1)S(1)}, bf16[5,9,48,128]{3,2,1,0:T(8,128)(2,1)S(1)}, u32[]{:S(2)}, u32[]{:S(2)}) %collective-permute-start.8) | collective-permute-done | bytes 552992 | tf_op jit(solution)/shard_map/ppermute | solution.py:605
  106.4 7.4 %collective-permute-done.9.after = bf16[5,9,48,128]{3,2,1,0:T(8,128)(2,1)S(1)} collective-permute-done((bf16[5,9,48,128]{3,2,1,0:T(8,128)(2,1)S(1)}, bf16[5,9,48,128]{3,2,1,0:T(8,128)(2,1)S(1)}, u32[]{:S(2)}, u32[]{:S(2)}) %collective-permute-start.9) | collective-permute-done | bytes 552992 | tf_op jit(solution)/shard_map/ppermute | solution.py:610
  113.8 8.6 %smooth_join.1 = f32[4,24,2048]{2,1,0:T(8,128)} custom-call(s32[5]{0:T(128)S(1)} %stack.25.place, f32[4,9,2,24,128]{4,3,2,1,0:T(8,128)S(1)} %get-tuple-element.52.own, bf16[5,9,48,128]{3,2,1,0:T(8,128)(2,1)S(1)} %collective-permute-done.8.before, bf16[5,9,48,128]{3,2,1,0:T(8,128)(2,1)S(1)} %collective-permute-done.9.after), custom_call_target="tpu_custom_call" | custom-call | tf_op jit(solution)/shard_map/smooth_join/pallas_call | solution.py:261
  (6 shorter events, 0.2 us)
Async XLA Ops:
  1.0 5.5 %collective-permute-start = (f32[4,24,256]{2,1,0:T(8,128)S(1)}, f32[4,24,256]{2,1,0:T(8,128)S(1)}, u32[]{:S(2)}, u32[]{:S(2)}) collective-permute-start(f32[4,24,256]{2,1,0:T(8,128)S(1)} %slice_select_fusion), channel_id=1, source_target_pairs={{0,1},{1,0},{2,3},{3,2},{4,5},{5,4},{6,7},{7,6},{8,9},{9,8},{10,11... | collective-permute-start | bytes 294920 | tf_op jit(solution)/shard_map/ppermute | solution.py:614
  6.4 11.4 %copy-start.5 = (s32[2,6]{1,0:T(2,128)S(1)}, s32[2,6]{1,0:T(2,128)}, u32[]{:S(2)}) copy-start(s32[2,6]{1,0:T(2,128)} %subsets.1) | copy-start | bytes 148
  6.5 11.5 %copy-start.3 = (s32[64]{0:T(128)S(1)}, s32[64]{0:T(128)}, u32[]{:S(2)}) copy-start(s32[64]{0:T(128)} %offsets.1) | copy-start | bytes 772
  6.5 14.9 %copy-start.4 = (s32[256]{0:T(256)S(1)}, s32[256]{0:T(256)}, u32[]{:S(2)}) copy-start(s32[256]{0:T(256)} %owners.1) | copy-start | bytes 3076
  6.5 15.1 %copy-start = (f32[4,24,2048]{2,1,0:T(8,128)S(1)}, f32[4,24,2048]{2,1,0:T(8,128)}, u32[]{:S(2)}) copy-start(f32[4,24,2048]{2,1,0:T(8,128)} %volume.1) | copy-start | bytes 2359300
  6.5 0.6 copy-start.1
  7.2 32.1 %all-to-all-start.1 = ((bf16[64,96,128]{2,1,0:T(8,128)(2,1)}), bf16[64,96,128]{2,1,0:T(8,128)(2,1)S(1)}, u32[]{:S(2)}, u32[]{:S(2)}) async-start(bf16[64,96,128]{2,1,0:T(8,128)(2,1)} %pack_images.3), calls=%async_computation.1 | async-start | bytes 3145728 | tf_op jit(solution)/shard_map/all_to_all | solution.py:628
  21.6 0.9 copy-start.2
  27.2 14.8 %collective-permute-start.2 = (bf16[48,1152]{1,0:T(8,128)(2,1)}, bf16[48,1152]{1,0:T(8,128)(2,1)S(1)}, u32[]{:S(2)}, u32[]{:S(2)}) collective-permute-start(bf16[48,1152]{1,0:T(8,128)(2,1)} %get-tuple-element.45), channel_id=1, source_target_pairs={{2,0},{4,2},{6,4},{8,6},{10,8},{12,10},{14,12},{16,14},{18,16},{20... | collective-permute-start | bytes 331784 | tf_op jit(solution)/shard_map/ppermute | solution.py:610
  29.5 12.5 %collective-permute-start.1 = (bf16[48,1152]{1,0:T(8,128)(2,1)}, bf16[48,1152]{1,0:T(8,128)(2,1)S(1)}, u32[]{:S(2)}, u32[]{:S(2)}) collective-permute-start(bf16[48,1152]{1,0:T(8,128)(2,1)} %get-tuple-element.45), channel_id=1, source_target_pairs={{0,2},{2,4},{4,6},{6,8},{8,10},{10,12},{12,14},{14,16},{16,18},{18... | collective-permute-start | bytes 331784 | tf_op jit(solution)/shard_map/ppermute | solution.py:605
  39.9 4.5 %collective-permute-start.3 = (bf16[12,16,128]{2,1,0:T(8,128)(2,1)S(1)}, bf16[12,16,128]{2,1,0:T(8,128)(2,1)S(1)}, u32[]{:S(2)}, u32[]{:S(2)}) collective-permute-start(bf16[12,16,128]{2,1,0:T(8,128)(2,1)S(1)} %inner_edges.1), channel_id=1, source_target_pairs={{0,1},{1,0},{2,3},{3,2},{4,5},{5,4},{6,7},{7,6},{8,9},{9,8},{10,11... | collective-permute-start | bytes 147464 | tf_op jit(solution)/shard_map/ppermute | solution.py:614
  49.0 12.1 %collective-permute-start.4 = (bf16[5,9,48,128]{3,2,1,0:T(8,128)(2,1)S(1)}, bf16[5,9,48,128]{3,2,1,0:T(8,128)(2,1)S(1)}, u32[]{:S(2)}, u32[]{:S(2)}) collective-permute-start(bf16[5,9,48,128]{3,2,1,0:T(8,128)(2,1)S(1)} %get-tuple-element.47), channel_id=1, source_target_pairs={{0,2},{2,4},{4,6},{6,8},{8,10},{10,12},{12,14},{14,16},{16,18},{18... | collective-permute-start | bytes 1658888 | tf_op jit(solution)/shard_map/ppermute | solution.py:605
  54.7 13.8 %collective-permute-start.5 = (bf16[5,9,48,128]{3,2,1,0:T(8,128)(2,1)S(1)}, bf16[5,9,48,128]{3,2,1,0:T(8,128)(2,1)S(1)}, u32[]{:S(2)}, u32[]{:S(2)}) collective-permute-start(bf16[5,9,48,128]{3,2,1,0:T(8,128)(2,1)S(1)} %get-tuple-element.48), channel_id=1, source_target_pairs={{2,0},{4,2},{6,4},{8,6},{10,8},{12,10},{14,12},{16,14},{18,16},{20... | collective-permute-start | bytes 1658888 | tf_op jit(solution)/shard_map/ppermute | solution.py:610
  77.7 9.1 %collective-permute-start.7 = (bf16[48,1152]{1,0:T(8,128)(2,1)S(1)}, bf16[48,1152]{1,0:T(8,128)(2,1)S(1)}, u32[]{:S(2)}, u32[]{:S(2)}) collective-permute-start(bf16[48,1152]{1,0:T(8,128)(2,1)S(1)} %get-tuple-element.51), channel_id=1, source_target_pairs={{2,0},{4,2},{6,4},{8,6},{10,8},{12,10},{14,12},{16,14},{18,16},{20... | collective-permute-start | bytes 331784 | tf_op jit(solution)/shard_map/ppermute | solution.py:610
  79.7 8.4 %collective-permute-start.6 = (bf16[48,1152]{1,0:T(8,128)(2,1)S(1)}, bf16[48,1152]{1,0:T(8,128)(2,1)S(1)}, u32[]{:S(2)}, u32[]{:S(2)}) collective-permute-start(bf16[48,1152]{1,0:T(8,128)(2,1)S(1)} %get-tuple-element.51), channel_id=1, source_target_pairs={{0,2},{2,4},{4,6},{6,8},{8,10},{10,12},{12,14},{14,16},{16,18},{18... | collective-permute-start | bytes 331784 | tf_op jit(solution)/shard_map/ppermute | solution.py:605
  92.6 13.8 %collective-permute-start.8 = (bf16[5,9,48,128]{3,2,1,0:T(8,128)(2,1)S(1)}, bf16[5,9,48,128]{3,2,1,0:T(8,128)(2,1)S(1)}, u32[]{:S(2)}, u32[]{:S(2)}) collective-permute-start(bf16[5,9,48,128]{3,2,1,0:T(8,128)(2,1)S(1)} %get-tuple-element.53), channel_id=1, source_target_pairs={{0,2},{2,4},{4,6},{6,8},{8,10},{10,12},{12,14},{14,16},{16,18},{18... | collective-permute-start | bytes 1658888 | tf_op jit(solution)/shard_map/ppermute | solution.py:605
  100.0 13.8 %collective-permute-start.9 = (bf16[5,9,48,128]{3,2,1,0:T(8,128)(2,1)S(1)}, bf16[5,9,48,128]{3,2,1,0:T(8,128)(2,1)S(1)}, u32[]{:S(2)}, u32[]{:S(2)}) collective-permute-start(bf16[5,9,48,128]{3,2,1,0:T(8,128)(2,1)S(1)} %get-tuple-element.54), channel_id=1, source_target_pairs={{2,0},{4,2},{6,4},{8,6},{10,8},{12,10},{14,12},{16,14},{18,16},{20... | collective-permute-start | bytes 1658888 | tf_op jit(solution)/shard_map/ppermute | solution.py:610
